TPU v7x, 32 devices: a whole 2x2x4 slice. The times are simulated.
32 devices in a mesh: ctx: 4 (over y, x), exp: 8 (over z, core).
Axes of the slice: x: 2, y: 2, z: 4, core: 2. Of those that a mesh axis runs over, the one named last changes fastest.
Arguments:
- queries: bfloat16 [8, 512, 4096], P('exp', 'ctx'), may hold values from -6 to 6
- keys: bfloat16 [8, 512, 512], P('exp', 'ctx'), may hold values from -6 to 6
- values: bfloat16 [8, 512, 512], P('exp', 'ctx'), may hold values from -8 to 8
- resid: bfloat16 [8, 512, 2048], P('exp', 'ctx'), may hold values from -40 to 40
- out_weight: bfloat16 [4096, 2048], P('ctx', 'exp'), may hold values from -0.5 to 0.5
- norm_gain: float32 [2048], replicated, may hold values from 0.5 to 2
- expert_gate: bfloat16 [16, 2048, 768], P('exp'), may hold values from -0.125 to 0.125
- expert_up: bfloat16 [16, 2048, 768], P('exp'), may hold values from -0.125 to 0.125
- expert_down: bfloat16 [16, 768, 2048], P('exp'), may hold values from -0.4375 to 0.4375
- route_ids: int32 [8, 512, 8], P('exp', 'ctx'), may hold values from 0 to 15, as said below
- route_gates: float32 [8, 512, 8], P('exp', 'ctx'), may hold values from 0.1 to 1
Outputs:
- attn_resid: bfloat16 [8, 512, 2048], P('exp', 'ctx')
- layer_out: bfloat16 [8, 512, 2048], P('exp', 'ctx')
Inputs may be any that keep to these rules, and one draw needn't show every extreme that they name: `route_ids`: each row names 8 different experts. In every block of 128 consecutive positions of a sequence (the tokens of one device) each expert is named by at most 64 rows, and one expert, the same in all blocks of a draw, by exactly 64 rows.
All inputs are finite; a program needn't handle non-finite values.
Results may differ from a plain program's by a relative error of at most 0.017.
Values may be sent and summed in bfloat16 or wider, within the bound.
No kernel may reach another device: no remote copies, remote signals or barrier semaphores. Data moves between devices by JAX's collectives and lax.ppermute only.
A program may use at most 128 MiB of HBM per device.

v0:
```python
import jax
import jax.numpy as jnp
from jax import lax
from jax.sharding import PartitionSpec as P

QUERY_HEAD_COUNT = 32
KEY_VALUE_HEADS = 4
HEAD_SIZE = 128
TOPK = 8
CAP = 64


norm_eps = 1e-06
mask_fill_value = -1e30


def from_behind(shard, axis, by):
    devices = lax.axis_size(axis)
    pairs = [(i, i + by) for i in range(devices) if 0 <= i + by < devices]
    return lax.ppermute(shard, axis, pairs)


def attend_block(state_now, key_value_portion, begin_row, query_head_rows, query_place):
    row_top, row_total, accum = state_now
    key_total = key_value_portion.shape[1]
    key_head_rows = key_value_portion[0].reshape(key_total, KEY_VALUE_HEADS, HEAD_SIZE)
    value_head_rows = key_value_portion[1].reshape(key_total, KEY_VALUE_HEADS, HEAD_SIZE)
    raw_scores = jnp.einsum(
        "tngd,und->ngtu", query_head_rows, key_head_rows, preferred_element_type=jnp.float32
    ) * HEAD_SIZE ** (-0.5)
    key_place = begin_row + jnp.arange(key_total, dtype=jnp.int32)
    allowed = query_place[:, None] >= key_place[None, :]
    raw_scores = jnp.where(allowed, raw_scores, mask_fill_value)
    new_top = jnp.maximum(row_top, jnp.max(raw_scores, axis=-1))
    factor = jnp.exp(row_top - new_top)
    exp_scores = jnp.where(allowed, jnp.exp(raw_scores - new_top[..., None]), 0.0)
    row_total = row_total * factor + jnp.sum(exp_scores, axis=-1)
    weights = exp_scores.astype(jnp.bfloat16)
    accum = accum * factor[..., None] + jnp.einsum(
        "ngtu,und->ngtd", weights, value_head_rows, preferred_element_type=jnp.float32
    )
    return (new_top, row_total, accum)


def experts_apply(arrived, gate_local, up_local, down_local):
    gate_part = jnp.einsum(
        "secd,edf->secf", arrived, gate_local, preferred_element_type=jnp.float32
    )
    up_part = jnp.einsum("secd,edf->secf", arrived, up_local, preferred_element_type=jnp.float32)
    activated = (jax.nn.silu(gate_part) * up_part).astype(jnp.bfloat16)
    return jnp.einsum(
        "secf,efd->secd", activated, down_local, preferred_element_type=jnp.float32
    ).astype(jnp.bfloat16)


def local(
    queries,
    keys,
    values,
    resid,
    out_weight,
    norm_gain,
    expert_gate,
    expert_up,
    expert_down,
    route_ids,
    route_gates,
):
    token_rows = queries.shape[1]
    ctx_count = lax.axis_size("ctx")
    exp_count = lax.axis_size("exp")
    my_block = lax.axis_index("ctx")
    query_group = QUERY_HEAD_COUNT // KEY_VALUE_HEADS
    query_head_rows = queries[0].reshape(token_rows, KEY_VALUE_HEADS, query_group, HEAD_SIZE)
    query_place = my_block * token_rows + jnp.arange(token_rows, dtype=jnp.int32)
    kv_local = jnp.stack([keys[0], values[0]])
    state_first = (
        jnp.full((KEY_VALUE_HEADS, query_group, token_rows), mask_fill_value, jnp.float32),
        jnp.zeros((KEY_VALUE_HEADS, query_group, token_rows), jnp.float32),
        jnp.zeros((KEY_VALUE_HEADS, query_group, token_rows, HEAD_SIZE), jnp.float32),
    )
    state_now = attend_block(
        state_first, kv_local, my_block * token_rows, query_head_rows, query_place
    )

    def circle_step(step_num, carried):
        state_in, key_value_portion = carried
        key_value_portion = from_behind(key_value_portion, "ctx", 1)
        source = my_block - step_num
        state_out = lax.cond(
            source >= 0,
            lambda held: attend_block(
                held, key_value_portion, source * token_rows, query_head_rows, query_place
            ),
            lambda held: held,
            state_in,
        )
        return (state_out, key_value_portion)

    state_now, kv_last = lax.fori_loop(1, ctx_count, circle_step, (state_now, kv_local))
    row_top, row_total, accum = state_now
    attention = (
        (accum / row_total[..., None])
        .transpose(2, 0, 1, 3)
        .reshape(token_rows, QUERY_HEAD_COUNT * HEAD_SIZE)
        .astype(jnp.bfloat16)
    )
    all_rows = lax.all_gather(out_weight, "ctx", axis=0, tiled=True)
    projected = jnp.dot(
        attention,
        lax.all_gather(all_rows, "exp", axis=1, tiled=True),
        preferred_element_type=jnp.float32,
    )
    attn_resid = (resid[0].astype(jnp.float32) + projected).astype(jnp.bfloat16)
    resid_wide = attn_resid.astype(jnp.float32)
    scale_row = lax.rsqrt(jnp.mean(resid_wide * resid_wide, axis=-1, keepdims=True) + norm_eps)
    normed = (resid_wide * scale_row * norm_gain).astype(jnp.bfloat16)
    route_list = route_ids[0]
    local_experts = expert_gate.shape[0]
    expert_total = local_experts * exp_count
    expert_range = jnp.arange(expert_total, dtype=jnp.int32)
    expert_hits = jnp.sum(
        (route_list[:, :, None] == expert_range[None, None, :]).astype(jnp.int32), axis=1
    )
    earlier_hits = jnp.cumsum(expert_hits, axis=0) - expert_hits
    slot_index = jnp.take_along_axis(earlier_hits, route_list, axis=1)
    flat_index = route_list * CAP + slot_index
    token_range = jnp.arange(token_rows, dtype=jnp.int32)
    slot_token = jnp.full((expert_total * CAP,), token_rows, jnp.int32)
    slot_token = slot_token.at[flat_index.reshape(-1)].set(jnp.repeat(token_range, TOPK))
    normed_padded = jnp.concatenate([normed, jnp.zeros((1, normed.shape[1]), jnp.bfloat16)], axis=0)
    outgoing = normed_padded[slot_token].reshape(exp_count, local_experts, CAP, normed.shape[1])
    finished = experts_apply(
        lax.all_to_all(outgoing, "exp", split_axis=0, concat_axis=0, tiled=True),
        expert_gate,
        expert_up,
        expert_down,
    )
    returned_rows = lax.all_to_all(finished, "exp", split_axis=0, concat_axis=0, tiled=True)
    flat_out = returned_rows.reshape(expert_total * CAP, normed.shape[1])
    gate_rows = route_gates[0]
    shares = gate_rows / jnp.sum(gate_rows, axis=-1, keepdims=True)
    combined = resid_wide
    for column in range(TOPK):
        combined = combined + shares[:, column : column + 1] * flat_out[
            flat_index[:, column]
        ].astype(jnp.float32)
    layer_out = combined.astype(jnp.bfloat16)
    return (attn_resid[None], layer_out[None])


def solution(mesh):
    in_specs = (
        P("exp", "ctx", None),
        P("exp", "ctx", None),
        P("exp", "ctx", None),
        P("exp", "ctx", None),
        P("ctx", "exp"),
        P(),
        P("exp", None, None),
        P("exp", None, None),
        P("exp", None, None),
        P("exp", "ctx", None),
        P("exp", "ctx", None),
    )
    out_specs = (P("exp", "ctx", None), P("exp", "ctx", None))
    return jax.shard_map(local, mesh=mesh, in_specs=in_specs, out_specs=out_specs, check_vma=False)
```

profile of v0, /device:TPU:0, one launch (start us, length us, event | category | flops | bytes accessed | tf_op | source)
XLA Modules:
  0.0 473.8 jit_solution(1381583549810535851)
XLA Ops:
  8.0 39.9 %all-gather.3.cloned.1.call-done = bf16[4096,256]{1,0:T(8,128)(2,1)} async-done(((bf16[1024,256]{1,0:T(8,128)(2,1)}), bf16[4096,256]{1,0:T(8,128)(2,1)}) %all-gather.3.cloned.1.call-update) | async-done | bytes 2097168 | tf_op jit(solution)/shard_map/all_gather | solution.py:108
  52.7 31.8 %while.20 = (s32[]{:T(128)}, f32[4,8,128]{2,1,0:T(8,128)S(1)}, f32[4,8,128]{2,1,0:T(8,128)S(1)}, f32[4,8,128,128]{3,2,1,0:T(8,128)S(1)}, bf16[2,128,512]{1,2,0:T...) while((s32[]{:T(128)}, f32[4,8,128]{2,1,0:T(8,128)S(1)}, ...), condition=%wide.region_7.8_spmd.clone, body=%wide.region_2.7_spmd.clone.sunk | while | flops 276324608 | bytes 14224691 | solution.py:100
  56.1 5.8 %collective-permute-done = bf16[2,128,512]{1,2,0:T(8,128)(2,1)S(1)} collective-permute-done((bf16[2,128,512]{1,2,0:T(8,128)(2,1)}, bf16[2,128,512]{1,2,0:T(8,128)(2,1)S(1)}, u32[]{:S(2)}, u32[]{:S(2)}) %collective-permute-start) | collective-permute-done | bytes 262176 | tf_op jit(solution)/shard_map/while/body/eval_jaxpr/ppermute | solution.py:20
  62.7 7.0 %collective-permute-start = (bf16[2,128,512]{1,2,0:T(8,128)(2,1)}, bf16[2,128,512]{1,2,0:T(8,128)(2,1)S(1)}, u32[]{:S(2)}, u32[]{:S(2)}) collective-permute-start(bf16[2,128,512]{1,2,0:T(8,128)(2,1)} %get-tuple-element.366), channel_id=1, source_target_pairs={{0,8},{8,16},{16,24},{1,9},{9,17},{17,25},{2,10},{10,18},{18,26},{... | collective-permute-start | bytes 786440 | tf_op jit(solution)/shard_map/while/body/eval_jaxpr/ppermute | solution.py:20
  69.7 5.0 %collective-permute-done = bf16[2,128,512]{1,2,0:T(8,128)(2,1)S(1)} collective-permute-done((bf16[2,128,512]{1,2,0:T(8,128)(2,1)}, bf16[2,128,512]{1,2,0:T(8,128)(2,1)S(1)}, u32[]{:S(2)}, u32[]{:S(2)}) %collective-permute-start) | collective-permute-done | bytes 262176 | tf_op jit(solution)/shard_map/while/body/eval_jaxpr/ppermute | solution.py:20
  75.3 4.3 collective-permute-start
  79.6 4.2 collective-permute-done
  87.2 7.1 %gather_fusion.9 = s32[1024]{0:T(1024)S(1)} fusion(s32[128,16]{1,0:T(8,128)S(1)} %sub.39, s32[1024]{0:T(1024)S(1)} %reshape.236), kind=kCustom, calls=%fused_computation.9 | custom fusion | bytes 16384 | tf_op jit(solution)/shard_map/jit(take_along_axis)/gather | solution.py:126
  94.3 4.3 scatter_custom_fusion
  98.9 102.5 %all-gather.5.cloned.1.call-done = bf16[4096,2048]{1,0:T(8,128)(2,1)} async-done(((bf16[4096,256]{1,0:T(8,128)(2,1)}), bf16[4096,2048]{1,0:T(8,128)(2,1)}) %all-gather.5.cloned.1.call-update) | async-done | bytes 16777232 | tf_op jit(solution)/shard_map/all_gather | solution.py:111
  201.4 8.3 %fusion.37 = (f32[128]{0:T(128)S(1)}, bf16[128,2048]{1,0:T(8,128)(2,1)S(1)}) fusion(bf16[128,4096]{0,1:T(8,128)(2,1)S(1)} %bitcast.128, bf16[4096,2048]{1,0:T(8,128)(2,1)} %all-gather.5.cloned.1.call-done, bf16[1,128,2048]{2,1,0:T(8,128)(2,1)} %param.18), kind=kOutput, calls=%fused_computation.59 | convolution fusion | flops 2149056512 | bytes 18874880 | tf_op jit(solution)/shard_map/dot_general | solution.py:109
  209.9 6.0 %gather_fusion = bf16[1024,2048]{1,0:T(8,128)(2,1)} fusion(bf16[129,2048]{1,0:T(8,128)(2,1)S(1)} %concatenate.3, s32[1024]{0:T(1024)S(1)} %fusion.69), kind=kCustom, calls=%fused_computation | custom fusion | bytes 8392704 | tf_op jit(solution)/shard_map/gather | solution.py:132
  215.9 97.9 %all_to_all.10 = bf16[8,2,64,2048]{3,2,1,0:T(8,128)(2,1)S(1)} all-to-all(bf16[8,2,64,2048]{3,2,1,0:T(8,128)(2,1)} %bitcast.123), channel_id=1, replica_groups=mesh['ctx'=4,'exp'=8] {'exp'}, dimensions={0} | all-to-all | bytes 8388608 | tf_op jit(solution)/shard_map/all_to_all | solution.py:134
  313.8 5.7 %fusion.16 = f32[2,8,64,768]{3,2,1,0:T(8,128)S(1)} fusion(bf16[2,2048,768]{2,1,0:T(8,128)(2,1)} %param.22, bf16[8,2,64,2048]{3,2,1,0:T(8,128)(2,1)S(1)} %all_to_all.10), kind=kOutput, calls=%fused_computation.33 | convolution fusion | flops 3221225472 | bytes 13631488 | tf_op jit(solution)/shard_map/secd,edf->secf/dot_general | solution.py:49
  329.4 4.7 all-to-all-start.1
  334.7 93.4 %all-to-all-done.1 = bf16[8,2,64,2048]{3,2,1,0:T(8,128)(2,1)} async-done(((bf16[8,2,64,2048]{3,2,1,0:T(8,128)(2,1)}), bf16[8,2,64,2048]{3,2,1,0:T(8,128)(2,1)}, u32[]{:S(2)}, u32[]{:S(2)}) %all-to-all-start.1) | async-done | bytes 4194336 | tf_op jit(solution)/shard_map/all_to_all | solution.py:139
  428.1 4.2 gather_fusion.1
  432.3 4.2 gather_fusion.2
  436.4 4.2 gather_fusion.3
  440.6 4.2 gather_fusion.4
  444.8 4.2 gather_fusion.5
  449.0 5.0 %gather_fusion.6 = bf16[128,2048]{1,0:T(8,128)(2,1)} fusion(bf16[1024,2048]{1,0:T(8,128)(2,1)} %bitcast.30, s32[1024]{0:T(1024)S(1)} %get-tuple-element.285), kind=kCustom, calls=%fused_computation.6 | custom fusion | bytes 1049088 | tf_op jit(solution)/shard_map/gather | solution.py:145
  454.0 5.0 %gather_fusion.7 = bf16[128,2048]{1,0:T(8,128)(2,1)} fusion(bf16[1024,2048]{1,0:T(8,128)(2,1)} %bitcast.30, s32[1024]{0:T(1024)S(1)} %get-tuple-element.284), kind=kCustom, calls=%fused_computation.7 | custom fusion | bytes 1049088 | tf_op jit(solution)/shard_map/gather | solution.py:145
  458.9 5.0 %gather_fusion.8 = bf16[128,2048]{1,0:T(8,128)(2,1)} fusion(bf16[1024,2048]{1,0:T(8,128)(2,1)} %bitcast.30, s32[1024]{0:T(1024)S(1)} %get-tuple-element.283), kind=kCustom, calls=%fused_computation.8 | custom fusion | bytes 1049088 | tf_op jit(solution)/shard_map/gather | solution.py:145
  (86 shorter events, 27.5 us)
Async XLA Ops:
  7.2 40.8 %copy-start.3 = (bf16[1,128,512]{2,1,0:T(8,128)(2,1)S(1)}, bf16[1,128,512]{2,1,0:T(8,128)(2,1)}, u32[]{:S(2)}) copy-start(bf16[1,128,512]{2,1,0:T(8,128)(2,1)} %param.16) | copy-start | bytes 393220
  7.2 40.9 %copy-start.4 = (bf16[1,128,512]{2,1,0:T(8,128)(2,1)S(1)}, bf16[1,128,512]{2,1,0:T(8,128)(2,1)}, u32[]{:S(2)}) copy-start(bf16[1,128,512]{2,1,0:T(8,128)(2,1)} %param.17) | copy-start | bytes 393220
  7.2 41.1 %copy-start.2 = (bf16[1,128,4096]{2,1,0:T(8,128)(2,1)S(1)}, bf16[1,128,4096]{2,1,0:T(8,128)(2,1)}, u32[]{:S(2)}) copy-start(bf16[1,128,4096]{2,1,0:T(8,128)(2,1)} %param.15) | copy-start | bytes 3145732
  7.2 40.7 %all-gather.3.cloned.1.call-start = ((), (), s32[]{:S(2)}) async-start(), calls=%async_computation.2 | async-start | bytes 2621440 | tf_op jit(solution)/shard_map/all_gather | solution.py:108
  7.9 193.4 %all-gather.5.cloned.1.call-start = ((), (), s32[]{:S(2)}) async-start(), calls=%async_computation.3 | async-start | bytes 18874368 | tf_op jit(solution)/shard_map/all_gather | solution.py:111
  52.7 9.2 %collective-permute-start = (bf16[2,128,512]{1,2,0:T(8,128)(2,1)}, bf16[2,128,512]{1,2,0:T(8,128)(2,1)S(1)}, u32[]{:S(2)}, u32[]{:S(2)}) collective-permute-start(bf16[2,128,512]{1,2,0:T(8,128)(2,1)} %get-tuple-element.366), channel_id=1, source_target_pairs={{0,8},{8,16},{16,24},{1,9},{9,17},{17,25},{2,10},{10,18},{18,26},{... | collective-permute-start | bytes 786440 | tf_op jit(solution)/shard_map/while/body/eval_jaxpr/ppermute | solution.py:20
  62.7 12.0 %collective-permute-start = (bf16[2,128,512]{1,2,0:T(8,128)(2,1)}, bf16[2,128,512]{1,2,0:T(8,128)(2,1)S(1)}, u32[]{:S(2)}, u32[]{:S(2)}) collective-permute-start(bf16[2,128,512]{1,2,0:T(8,128)(2,1)} %get-tuple-element.366), channel_id=1, source_target_pairs={{0,8},{8,16},{16,24},{1,9},{9,17},{17,25},{2,10},{10,18},{18,26},{... | collective-permute-start | bytes 786440 | tf_op jit(solution)/shard_map/while/body/eval_jaxpr/ppermute | solution.py:20
  75.3 8.5 %collective-permute-start = (bf16[2,128,512]{1,2,0:T(8,128)(2,1)}, bf16[2,128,512]{1,2,0:T(8,128)(2,1)S(1)}, u32[]{:S(2)}, u32[]{:S(2)}) collective-permute-start(bf16[2,128,512]{1,2,0:T(8,128)(2,1)} %get-tuple-element.366), channel_id=1, source_target_pairs={{0,8},{8,16},{16,24},{1,9},{9,17},{17,25},{2,10},{10,18},{18,26},{... | collective-permute-start | bytes 786440 | tf_op jit(solution)/shard_map/while/body/eval_jaxpr/ppermute | solution.py:20
  84.5 1.8 copy-start.5
  87.2 11.4 %copy-start = (f32[4,8,128,128]{2,3,1,0:T(8,128)S(1)}, f32[4,8,128,128]{2,3,1,0:T(8,128)}, u32[]{:S(2)}) copy-start(f32[4,8,128,128]{2,3,1,0:T(8,128)} %copy.81) | copy-start | bytes 6291460
  201.4 8.3 %copy-start.7 = (f32[2048]{0:T(1024)S(1)}, f32[2048]{0:T(1024)}, u32[]{:S(2)}) copy-start(f32[2048]{0:T(1024)} %param.20) | copy-start | bytes 24580
  209.6 254.2 %copy-start.1 = (bf16[128,2048]{1,0:T(8,128)(2,1)}, bf16[128,2048]{1,0:T(8,128)(2,1)S(1)}, u32[]{:S(2)}) copy-start(bf16[128,2048]{1,0:T(8,128)(2,1)S(1)} %get-tuple-element.282) | copy-start | bytes 1572868
  215.9 103.6 %slice-start = ((s8[6291456]{0:T(1024)(128)(4,1)}), s8[4194304]{0:T(1024)(128)(4,1)S(1)}, s32[]{:S(2)}) async-start(s8[6291456]{0:T(1024)(128)(4,1)} %bitcast.135), calls=%async_computation.4 | async-start | bytes 8388608
  313.8 5.7 %slice-start.1 = ((s8[6291456]{0:T(1024)(128)(4,1)}), s8[2097152]{0:T(1024)(128)(4,1)S(1)}, s32[]{:S(2)}) async-start(s8[6291456]{0:T(1024)(128)(4,1)} %bitcast.135), calls=%async_computation.5 | async-start | bytes 4194304
  313.8 9.6 %slice-start.2 = ((s8[6291456]{0:T(1024)(128)(4,1)}), s8[4194304]{0:T(1024)(128)(4,1)S(1)}, s32[]{:S(2)}) async-start(s8[6291456]{0:T(1024)(128)(4,1)} %bitcast.137), calls=%async_computation.6 | async-start | bytes 8388608
  319.6 3.9 slice-start.3
  329.4 4.8 %copy-start.6 = (f32[1,128,8]{1,2,0:T(8,128)S(1)}, f32[1,128,8]{1,2,0:T(8,128)}, u32[]{:S(2)}) copy-start(f32[1,128,8]{1,2,0:T(8,128)} %param.25) | copy-start | bytes 12292
  329.4 98.7 %all-to-all-start.1 = ((bf16[8,2,64,2048]{3,2,1,0:T(8,128)(2,1)}), bf16[8,2,64,2048]{3,2,1,0:T(8,128)(2,1)}, u32[]{:S(2)}, u32[]{:S(2)}) async-start(bf16[8,2,64,2048]{3,2,1,0:T(8,128)(2,1)} %copy.90), calls=%async_computation.1 | async-start | bytes 8388608 | tf_op jit(solution)/shard_map/all_to_all | solution.py:139
Sparse Core Ops, SparseCore 0:
  9.9 38.0 all-gather.2
  49.5 151.8 all-gather.4
where the time goes:
time: 474 us
  waiting for transfers between devices  252 us (53%)
  blocking collectives  97.9 us (21%)
  local copies, waits for them, and re-layouts  61.8 us (13%)
  matrix products  23.1 us (5%)
  starting transfers between devices  19.4 us (4%)
  between operations  14.5 us (3%)
  other arithmetic  5.62 us (1%)
    all_gather x1, waiting for transfers between devices, local(): lax.all_gather(all_rows, 'exp', axis=1, tiled=True)  102 us
    all_to_all x1, blocking collectives, local(): lax.all_to_all(outgoing, 'exp', split_axis=0, concat_axis=0, tiled=True)  97.9 us
    all_to_all x1, waiting for transfers between devices, local(): lax.all_to_all(finished, 'exp', split_axis=0, concat_axis=0, tiled=True)  93.4 us
    all_gather x1, waiting for transfers between devices, local(): all_rows = lax.all_gather(out_weight, 'ctx', axis=0, tiled=True)  39.9 us
    gather x8, local copies, waits for them, and re-layouts, local(): flat_out[flat_index[:, column]].astype(jnp.float32)  35.7 us
    ppermute x3, waiting for transfers between devices, from_behind(): return lax.ppermute(shard, axis, pairs)  15 us
    ppermute x3, starting transfers between devices, from_behind(): return lax.ppermute(shard, axis, pairs)  14.7 us
  transfers between devices with their start and end apart: 6, of which 6 were waited for; matrix products, arithmetic and copies ran while one was open for 5% of the time, Pallas kernels for 0%

commit v1 on v0

v1 whole, which is shorter than its diff:
```python
import functools

import jax
import jax.numpy as jnp
from jax import lax
from jax.experimental import pallas as pl
from jax.experimental.pallas import tpu as pltpu
from jax.sharding import PartitionSpec as P

QUERY_HEAD_COUNT = 32
KEY_VALUE_HEADS = 4
HEAD_SIZE = 128
TOPK = 8
CAP = 64

norm_eps = 1e-06
mask_fill_value = -1e30
MIB = 1024 * 1024


def swap(shard, axis, by):
    devices = lax.axis_size(axis)
    return lax.ppermute(shard, axis, [(i, i ^ by) for i in range(devices)])


def dot(a, b):
    return jnp.dot(a, b, preferred_element_type=jnp.float32)


def attention_kernel(blocks, heads, kv_heads, me_ref, *refs):
    ins, out_ref, seq = refs[:blocks], refs[blocks], refs[blocks + 1]
    rows = ins[0].shape[0]
    me = me_ref[0]
    wide = heads * HEAD_SIZE
    for j in range(blocks):
        seq[pl.ds(pl.multiple_of((me ^ j) * rows, rows), rows), :] = ins[j][...]
    row = lax.broadcasted_iota(jnp.int32, (rows, rows), 0)
    col = lax.broadcasted_iota(jnp.int32, (rows, rows), 1)
    allowed = row >= col
    for h in range(heads):
        g = h // (heads // kv_heads)
        key_at = wide + g * HEAD_SIZE
        value_at = wide + (kv_heads + g) * HEAD_SIZE
        for i in range(blocks):
            q = seq[i * rows : (i + 1) * rows, h * HEAD_SIZE : (h + 1) * HEAD_SIZE]
            k = seq[: (i + 1) * rows, key_at : key_at + HEAD_SIZE]
            v = seq[: (i + 1) * rows, value_at : value_at + HEAD_SIZE]
            s = lax.dot_general(
                q, k, (((1,), (1,)), ((), ())), preferred_element_type=jnp.float32
            ) * HEAD_SIZE ** (-0.5)
            last = jnp.where(allowed, s[:, i * rows :], mask_fill_value)
            s = last if i == 0 else jnp.concatenate([s[:, : i * rows], last], axis=1)
            p = jnp.exp(s - jnp.max(s, axis=1, keepdims=True))
            total = jnp.sum(p, axis=1, keepdims=True)
            o = dot(p.astype(jnp.bfloat16), v) / total
            out_ref[
                pl.ds(pl.multiple_of((me ^ i) * rows, rows), rows),
                h * HEAD_SIZE : (h + 1) * HEAD_SIZE,
            ] = o.astype(jnp.bfloat16)


def attention_call(me, ins, heads, kv_heads):
    blocks = len(ins)
    rows, wide_in = ins[0].shape
    length, wide = blocks * rows, heads * HEAD_SIZE
    return pl.pallas_call(
        functools.partial(attention_kernel, blocks, heads, kv_heads),
        out_shape=jax.ShapeDtypeStruct((length, wide), jnp.bfloat16),
        in_specs=[pl.BlockSpec(memory_space=pltpu.SMEM)]
        + [pl.BlockSpec(memory_space=pltpu.VMEM)] * blocks,
        out_specs=pl.BlockSpec(memory_space=pltpu.VMEM),
        scratch_shapes=[pltpu.VMEM((length, wide_in), jnp.bfloat16)],
        compiler_params=pltpu.CompilerParams(vmem_limit_bytes=16 * MIB),
        cost_estimate=pl.CostEstimate(
            flops=4 * length * length * wide,
            bytes_accessed=4 * length * wide_in,
            transcendentals=length * length * heads,
        ),
        name="attention",
    )(me, *ins)


def projection_kernel(pieces, depth, att_ref, *refs):
    ins, outs = refs[:pieces], refs[pieces:]
    rows = outs[0].shape[0]
    piece = ins[0].shape[1]
    for k in range(pieces):
        y = dot(att_ref[...], ins[k][:depth, :]).astype(jnp.bfloat16)
        for j, out in enumerate(outs):
            out[:, k * piece : (k + 1) * piece] = y[j * rows : (j + 1) * rows]


def projection_call(att, packs, blocks):
    length, depth = att.shape
    piece = packs[0].shape[1]
    rows, wide = length // blocks, piece * len(packs)
    return pl.pallas_call(
        functools.partial(projection_kernel, len(packs), depth),
        out_shape=[jax.ShapeDtypeStruct((rows, wide), jnp.bfloat16)] * blocks,
        in_specs=[pl.BlockSpec(memory_space=pltpu.VMEM)] * (1 + len(packs)),
        out_specs=[pl.BlockSpec(memory_space=pltpu.VMEM)] * blocks,
        compiler_params=pltpu.CompilerParams(vmem_limit_bytes=16 * MIB),
        cost_estimate=pl.CostEstimate(
            flops=2 * length * depth * wide,
            bytes_accessed=2 * (length * depth + depth * wide + length * wide),
            transcendentals=0,
        ),
        name="projection",
    )(att, *packs)


def norm_kernel(chunks, blocks, me_ref, resid_ref, gain_ref, *refs):
    parts, (attn_ref, normed_ref) = refs[: chunks * blocks], refs[chunks * blocks :]
    me = me_ref[0]
    width = resid_ref.shape[1]
    wide = parts[0].shape[1]
    pieces = me_ref.shape[0] - 1
    piece = width // pieces
    per = wide // piece
    total = None
    for n in range(chunks):
        for k in range(per):
            at = pl.ds(pl.multiple_of((me ^ (n * per + k)) * piece, piece), piece)
            acc = resid_ref[:, at].astype(jnp.float32)
            for j in range(blocks):
                acc = acc + parts[n * blocks + j][:, k * piece : (k + 1) * piece].astype(
                    jnp.float32
                )
            acc = acc.astype(jnp.bfloat16)
            attn_ref[:, at] = acc
            acc = acc.astype(jnp.float32)
            squares = jnp.sum(acc * acc, axis=1, keepdims=True)
            total = squares if total is None else total + squares
    scale = lax.rsqrt(total / width + norm_eps)
    normed_ref[...] = (attn_ref[...].astype(jnp.float32) * scale * gain_ref[...]).astype(
        jnp.bfloat16
    )


def norm_call(me, resid, gain, parts, blocks, pieces):
    rows, width = resid.shape
    marks = jnp.full((pieces + 1,), me, jnp.int32)
    return pl.pallas_call(
        functools.partial(norm_kernel, len(parts) // blocks, blocks),
        out_shape=[jax.ShapeDtypeStruct((rows, width), jnp.bfloat16)] * 2,
        in_specs=[pl.BlockSpec(memory_space=pltpu.SMEM)]
        + [pl.BlockSpec(memory_space=pltpu.VMEM)] * (2 + len(parts)),
        out_specs=[pl.BlockSpec(memory_space=pltpu.VMEM)] * 2,
        compiler_params=pltpu.CompilerParams(vmem_limit_bytes=16 * MIB),
        cost_estimate=pl.CostEstimate(
            flops=10 * rows * width, bytes_accessed=2 * rows * width * 8, transcendentals=rows
        ),
        name="resid_norm",
    )(marks, resid, gain.reshape(1, width), *parts)


def experts_kernel(sources, local_experts, share_ref, *refs):
    ins = refs[:sources]
    gate_ref, up_ref, down_ref = refs[sources : sources + 3]
    outs = refs[sources + 3 : 2 * sources + 3]
    picked, slot_map, slot_share, acc = refs[2 * sources + 3 :]
    rows = ins[0].shape[0]
    e, f = pl.program_id(0), pl.program_id(1)
    f_last = pl.num_programs(1) - 1

    @pl.when((e == 0) & (f == 0))
    def _():
        before = (
            lax.broadcasted_iota(jnp.int32, (rows, rows), 0)
            < lax.broadcasted_iota(jnp.int32, (rows, rows), 1)
        ).astype(jnp.bfloat16)
        slot = lax.broadcasted_iota(jnp.int32, (CAP, rows), 0).astype(jnp.float32)
        for s in range(sources):
            share = share_ref[s]
            hit = (share > 0.0).astype(jnp.bfloat16)
            rank = dot(hit, before)
            rank = jnp.where(share > 0.0, rank, -1.0)
            for n in range(local_experts):
                taken = slot == rank[n : n + 1, :]
                slot_map[s, n * CAP : (n + 1) * CAP, :] = taken.astype(jnp.bfloat16)
                slot_share[n, s * CAP : (s + 1) * CAP, :] = jnp.sum(
                    jnp.where(taken, share[n : n + 1, :], 0.0), axis=1, keepdims=True
                )
            rows_picked = dot(slot_map[s], ins[s][...]).astype(jnp.bfloat16)
            for n in range(local_experts):
                picked[n, s * CAP : (s + 1) * CAP, :] = rows_picked[n * CAP : (n + 1) * CAP]

    x = picked[e]
    gate_part = dot(x, gate_ref[0])
    up_part = dot(x, up_ref[0])
    activated = gate_part / (1.0 + jnp.exp(-gate_part)) * up_part * slot_share[e]
    y = dot(activated.astype(jnp.bfloat16), down_ref[0])

    @pl.when(f == 0)
    def _():
        acc[e] = y

    @pl.when(f > 0)
    def _():
        acc[e] += y

    @pl.when((e == local_experts - 1) & (f == f_last))
    def _():
        for s in range(sources):
            y_all = jnp.concatenate(
                [acc[n, s * CAP : (s + 1) * CAP, :] for n in range(local_experts)], axis=0
            ).astype(jnp.bfloat16)
            outs[s][...] = lax.dot_general(
                slot_map[s], y_all, (((0,), (0,)), ((), ())), preferred_element_type=jnp.float32
            ).astype(jnp.bfloat16)


def experts_call(share, tokens, gate, up, down, step=256):
    sources = len(tokens)
    rows, width = tokens[0].shape
    local_experts, _, hidden = gate.shape
    slots = sources * CAP
    whole = pl.BlockSpec((rows, width), lambda e, f: (0, 0))
    return pl.pallas_call(
        functools.partial(experts_kernel, sources, local_experts),
        grid=(local_experts, hidden // step),
        out_shape=[jax.ShapeDtypeStruct((rows, width), jnp.bfloat16)] * sources,
        in_specs=[pl.BlockSpec(share.shape, lambda e, f: (0, 0, 0))]
        + [whole] * sources
        + [
            pl.BlockSpec((1, width, step), lambda e, f: (e, 0, f)),
            pl.BlockSpec((1, width, step), lambda e, f: (e, 0, f)),
            pl.BlockSpec((1, step, width), lambda e, f: (e, f, 0)),
        ],
        out_specs=[whole] * sources,
        scratch_shapes=[
            pltpu.VMEM((local_experts, slots, width), jnp.bfloat16),
            pltpu.VMEM((sources, local_experts * CAP, rows), jnp.bfloat16),
            pltpu.VMEM((local_experts, slots, 1), jnp.float32),
            pltpu.VMEM((local_experts, slots, width), jnp.float32),
        ],
        compiler_params=pltpu.CompilerParams(
            vmem_limit_bytes=40 * MIB, dimension_semantics=("arbitrary", "arbitrary")
        ),
        cost_estimate=pl.CostEstimate(
            flops=6 * local_experts * slots * width * hidden,
            bytes_accessed=2 * (3 * local_experts * width * hidden + 2 * sources * rows * width),
            transcendentals=local_experts * slots * hidden,
        ),
        name="experts",
    )(share, *tokens, gate, up, down)


def gather_chips(own, chips):
    same = [own] + [swap(own, "exp", 2 * k) for k in range(1, chips)]
    return [piece for s in same for piece in (s, swap(s, "exp", 1))]


def local(
    queries,
    keys,
    values,
    resid,
    out_weight,
    norm_gain,
    expert_gate,
    expert_up,
    expert_down,
    route_ids,
    route_gates,
):
    rows = queries.shape[1]
    ctx_count = lax.axis_size("ctx")
    exp_count = lax.axis_size("exp")
    chips = exp_count // 2
    ctx_me, exp_me = lax.axis_index("ctx"), lax.axis_index("exp")
    local_experts = expert_gate.shape[0]
    expert_total = local_experts * exp_count
    heads = QUERY_HEAD_COUNT // ctx_count
    group = QUERY_HEAD_COUNT // KEY_VALUE_HEADS
    kv_heads = max(1, heads // group)

    def block_for(who):
        kv_at = who * heads // group * HEAD_SIZE
        return jnp.concatenate(
            [
                lax.dynamic_slice_in_dim(
                    queries[0], who * heads * HEAD_SIZE, heads * HEAD_SIZE, axis=1
                ),
                lax.dynamic_slice_in_dim(keys[0], kv_at, kv_heads * HEAD_SIZE, axis=1),
                lax.dynamic_slice_in_dim(values[0], kv_at, kv_heads * HEAD_SIZE, axis=1),
            ],
            axis=1,
        )

    blocks_in = [block_for(ctx_me)] + [
        swap(block_for(ctx_me ^ j), "ctx", j) for j in range(1, ctx_count)
    ]

    gate_rows = route_gates[0]
    shares = gate_rows / jnp.sum(gate_rows, axis=-1, keepdims=True)
    expert_range = jnp.arange(expert_total, dtype=jnp.int32)
    share_rows = jnp.sum(
        jnp.where(route_ids[0].T[None] == expert_range[:, None, None], shares.T[None], 0.0), axis=1
    )
    share_high = lax.reduce_precision(share_rows, 8, 7)
    share_parts = [share_high.astype(jnp.bfloat16), (share_rows - share_high).astype(jnp.bfloat16)]
    depth, piece = out_weight.shape
    side = 1 if piece >= 2 * rows else 0
    extra = jnp.concatenate(share_parts, axis=side)
    extra = jnp.pad(extra, ((0, 0), (0, piece - extra.shape[1])))
    packs = gather_chips(jnp.concatenate([out_weight, extra], axis=0), chips)

    def share_of(pack):
        both = pack[depth:].astype(jnp.float32)
        if side:
            both = both[:, :rows] + both[:, rows : 2 * rows]
        else:
            both = both[:expert_total, :rows] + both[expert_total:, :rows]
        mine = lax.dynamic_slice_in_dim(both, exp_me * local_experts, local_experts, axis=0)
        return jnp.pad(mine, ((0, 8 - local_experts), (0, 0)))

    share_mine = [share_of(pack) for pack in packs]

    att = attention_call(jnp.full((1,), ctx_me, jnp.int32), blocks_in, heads, kv_heads)

    parts = []
    half = len(packs) // 2
    for some in (packs[:half], packs[half:]):
        mine = projection_call(att, some, ctx_count)
        parts += [mine[0]] + [swap(mine[j], "ctx", j) for j in range(1, ctx_count)]
    attn_resid, normed = norm_call(exp_me, resid[0], norm_gain, parts, ctx_count, exp_count)

    tokens = gather_chips(normed, chips)
    sums = []
    for at in (0, half):
        partial = experts_call(
            jnp.stack(share_mine[at : at + half]),
            tokens[at : at + half],
            expert_gate,
            expert_up,
            expert_down,
        )
        for k in range(0, half, 2):
            both = partial[k].astype(jnp.float32) + swap(partial[k + 1], "exp", 1).astype(
                jnp.float32
            )
            if at + k:
                both = swap(both.astype(jnp.bfloat16), "exp", at + k).astype(jnp.float32)
            sums.append(both)
    layer_out = attn_resid.astype(jnp.float32)
    for s in sums:
        layer_out = layer_out + s
    return (attn_resid[None], layer_out.astype(jnp.bfloat16)[None])


def solution(mesh):
    in_specs = (
        P("exp", "ctx", None),
        P("exp", "ctx", None),
        P("exp", "ctx", None),
        P("exp", "ctx", None),
        P("ctx", "exp"),
        P(),
        P("exp", None, None),
        P("exp", None, None),
        P("exp", None, None),
        P("exp", "ctx", None),
        P("exp", "ctx", None),
    )
    out_specs = (P("exp", "ctx", None), P("exp", "ctx", None))
    return jax.shard_map(local, mesh=mesh, in_specs=in_specs, out_specs=out_specs, check_vma=False)
```

time: 474 us -> 206 us (0.43)
  the two profiles are of different devices: /device:TPU:0 before, /device:TPU:17 now
where the time goes in v1:
time: 206 us
  waiting for transfers between devices  125 us (61%)
  starting transfers between devices  36.8 us (18%)
  Pallas kernels  35.4 us (17%)
  other arithmetic  6.58 us (3%)
    ppermute x30, waiting for transfers between devices, swap(): return lax.ppermute(shard, axis, [(i, i ^ by) for i in range(devices)])  125 us
    ppermute x30, starting transfers between devices, swap(): return lax.ppermute(shard, axis, [(i, i ^ by) for i in range(devices)])  36.8 us
    pallas_call x2, Pallas kernels, experts_call(): pl.pallas_call(functools.partial(experts_kernel, sources, local_experts),...  24.3 us
    pallas_call x1, Pallas kernels, attention_call(): pl.pallas_call(functools.partial(attention_kernel, blocks, heads, kv_head...  6.81 us
  transfers between devices with their start and end apart: 30, of which 15 were waited for; matrix products, arithmetic and copies ran while one was open for 1% of the time, Pallas kernels for 16%

profile of v1, /device:TPU:17, one launch (start us, length us, event | category | flops | bytes accessed | tf_op | source)
XLA Modules:
  0.0 205.7 jit_solution(17487372164077788876)
XLA Ops:
  10.4 5.2 %collective-permute-done.1.refs_2_ = bf16[128,1280]{1,0:T(8,128)(2,1)S(1)} collective-permute-done((bf16[128,1280]{1,0:T(8,128)(2,1)S(1)}, bf16[128,1280]{1,0:T(8,128)(2,1)S(1)}, u32[]{:S(2)}, u32[]{:S(2)}) %collective-permute-start.1) | collective-permute-done | bytes 327712 | tf_op jit(solution)/shard_map/ppermute | solution.py:23
  15.6 3.2 %collective-permute-start.9 = (bf16[1040,256]{1,0:T(8,128)(2,1)S(1)}, bf16[1040,256]{1,0:T(8,128)(2,1)S(1)}, u32[]{:S(2)}, u32[]{:S(2)}) collective-permute-start(bf16[1040,256]{1,0:T(8,128)(2,1)S(1)} %maximum_maximum_fusion.refs_0_), channel_id=1, source_target_pairs={{0,4},{1,5},{2,6},{3,7},{4,0},{5,1},{6,2},{7,3},{8,12},{9,13},{10,... | collective-permute-start | bytes 1597448 | tf_op jit(solution)/shard_map/ppermute | solution.py:23
  18.8 5.6 %collective-permute-done.2.refs_3_ = bf16[128,1280]{1,0:T(8,128)(2,1)S(1)} collective-permute-done((bf16[128,1280]{1,0:T(8,128)(2,1)}, bf16[128,1280]{1,0:T(8,128)(2,1)S(1)}, u32[]{:S(2)}, u32[]{:S(2)}) %collective-permute-start.2) | collective-permute-done | bytes 327712 | tf_op jit(solution)/shard_map/ppermute | solution.py:23
  24.4 6.8 %attention.1.att_ref = bf16[512,1024]{1,0:T(8,128)(2,1)S(1)} custom-call(s32[1]{0:T(128)} %bitcast.2.me_ref, bf16[128,1280]{1,0:T(8,128)(2,1)S(1)} %pad_maximum_fusion.refs_0_, bf16[128,1280]{1,0:T(8,128)(2,1)S(1)} %collective-permute-done.refs_1_, bf16[128,1280]{1,0:T(8,128)(2,1)S(1)} %collective-permute-done.1.refs_2_, ...), custom_call_target="tpu_custom_call" | custom-call | flops 1073741824 | bytes 2621440 | tf_op jit(solution)/shard_map/attention/pallas_call | solution.py:66
  31.3 8.5 %collective-permute-done.11.refs_2_ = bf16[1040,256]{1,0:T(8,128)(2,1)S(1)} collective-permute-done((bf16[1040,256]{1,0:T(8,128)(2,1)S(1)}, bf16[1040,256]{1,0:T(8,128)(2,1)S(1)}, u32[]{:S(2)}, u32[]{:S(2)}) %collective-permute-start.11) | collective-permute-done | bytes 532512 | tf_op jit(solution)/shard_map/ppermute | solution.py:23
  39.8 2.7 %collective-permute-start.12 = (bf16[1040,256]{1,0:T(8,128)(2,1)S(1)}, bf16[1040,256]{1,0:T(8,128)(2,1)S(1)}, u32[]{:S(2)}, u32[]{:S(2)}) collective-permute-start(bf16[1040,256]{1,0:T(8,128)(2,1)S(1)} %collective-permute-done.11.refs_2_), channel_id=1, source_target_pairs={{0,1},{1,0},{2,3},{3,2},{4,5},{5,4},{6,7},{7,6},{8,9},{9,8},{10,11... | collective-permute-start | bytes 1597448 | tf_op jit(solution)/shard_map/ppermute | solution.py:23
  42.5 6.8 %collective-permute-done.9.refs_0_ = bf16[1040,256]{1,0:T(8,128)(2,1)S(1)} collective-permute-done((bf16[1040,256]{1,0:T(8,128)(2,1)S(1)}, bf16[1040,256]{1,0:T(8,128)(2,1)S(1)}, u32[]{:S(2)}, u32[]{:S(2)}) %collective-permute-start.9) | collective-permute-done | bytes 532512 | tf_op jit(solution)/shard_map/ppermute | solution.py:23
  49.4 1.4 collective-permute-start.10
  50.9 1.4 collective-permute-done.10.refs_1_
  61.1 2.2 %collective-permute-start.8 = (bf16[128,1024]{1,0:T(8,128)(2,1)S(1)}, bf16[128,1024]{1,0:T(8,128)(2,1)S(1)}, u32[]{:S(2)}, u32[]{:S(2)}) collective-permute-start(bf16[128,1024]{1,0:T(8,128)(2,1)S(1)} %get-tuple-element.23), channel_id=1, source_target_pairs={{0,24},{8,16},{16,8},{24,0},{1,25},{9,17},{17,9},{25,1},{2,26},{10... | collective-permute-start | bytes 786440 | tf_op jit(solution)/shard_map/ppermute | solution.py:23
  63.3 4.4 %collective-permute-done.15.refs_7_ = bf16[128,1024]{1,0:T(8,128)(2,1)S(1)} collective-permute-done((bf16[128,1024]{1,0:T(8,128)(2,1)S(1)}, bf16[128,1024]{1,0:T(8,128)(2,1)S(1)}, u32[]{:S(2)}, u32[]{:S(2)}) %collective-permute-start.15) | collective-permute-done | bytes 262176 | tf_op jit(solution)/shard_map/ppermute | solution.py:23
  67.7 4.7 %collective-permute-done.6.refs_1_ = bf16[128,1024]{1,0:T(8,128)(2,1)S(1)} collective-permute-done((bf16[128,1024]{1,0:T(8,128)(2,1)S(1)}, bf16[128,1024]{1,0:T(8,128)(2,1)S(1)}, u32[]{:S(2)}, u32[]{:S(2)}) %collective-permute-start.6) | collective-permute-done | bytes 262176 | tf_op jit(solution)/shard_map/ppermute | solution.py:23
  73.2 5.8 %collective-permute-done.8.refs_3_ = bf16[128,1024]{1,0:T(8,128)(2,1)S(1)} collective-permute-done((bf16[128,1024]{1,0:T(8,128)(2,1)S(1)}, bf16[128,1024]{1,0:T(8,128)(2,1)S(1)}, u32[]{:S(2)}, u32[]{:S(2)}) %collective-permute-start.8) | collective-permute-done | bytes 262176 | tf_op jit(solution)/shard_map/ppermute | solution.py:23
  79.0 1.8 resid_norm.1
  82.1 4.0 %collective-permute-start.22 = (bf16[128,2048]{1,0:T(8,128)(2,1)S(1)}, bf16[128,2048]{1,0:T(8,128)(2,1)S(1)}, u32[]{:S(2)}, u32[]{:S(2)}) collective-permute-start(bf16[128,2048]{1,0:T(8,128)(2,1)S(1)} %get-tuple-element.29.refs_0_), channel_id=1, source_target_pairs={{0,4},{1,5},{2,6},{3,7},{4,0},{5,1},{6,2},{7,3},{8,12},{9,13},{10,... | collective-permute-start | bytes 1572872 | tf_op jit(solution)/shard_map/ppermute | solution.py:23
  86.2 29.1 %collective-permute-done.24.refs_2_ = bf16[128,2048]{1,0:T(8,128)(2,1)S(1)} collective-permute-done((bf16[128,2048]{1,0:T(8,128)(2,1)S(1)}, bf16[128,2048]{1,0:T(8,128)(2,1)S(1)}, u32[]{:S(2)}, u32[]{:S(2)}) %collective-permute-start.24) | collective-permute-done | bytes 524320 | tf_op jit(solution)/shard_map/ppermute | solution.py:23
  115.3 4.3 %collective-permute-start.25 = (bf16[128,2048]{1,0:T(8,128)(2,1)S(1)}, bf16[128,2048]{1,0:T(8,128)(2,1)S(1)}, u32[]{:S(2)}, u32[]{:S(2)}) collective-permute-start(bf16[128,2048]{1,0:T(8,128)(2,1)S(1)} %collective-permute-done.24.refs_2_), channel_id=1, source_target_pairs={{0,1},{1,0},{2,3},{3,2},{4,5},{5,4},{6,7},{7,6},{8,9},{9,8},{10,11... | collective-permute-start | bytes 1572872 | tf_op jit(solution)/shard_map/ppermute | solution.py:23
  119.5 6.1 %collective-permute-done.22.refs_0_ = bf16[128,2048]{1,0:T(8,128)(2,1)S(1)} collective-permute-done((bf16[128,2048]{1,0:T(8,128)(2,1)S(1)}, bf16[128,2048]{1,0:T(8,128)(2,1)S(1)}, u32[]{:S(2)}, u32[]{:S(2)}) %collective-permute-start.22) | collective-permute-done | bytes 524320 | tf_op jit(solution)/shard_map/ppermute | solution.py:23
  125.6 2.3 %collective-permute-start.23 = (bf16[128,2048]{1,0:T(8,128)(2,1)S(1)}, bf16[128,2048]{1,0:T(8,128)(2,1)S(1)}, u32[]{:S(2)}, u32[]{:S(2)}) collective-permute-start(bf16[128,2048]{1,0:T(8,128)(2,1)S(1)} %collective-permute-done.22.refs_0_), channel_id=1, source_target_pairs={{0,1},{1,0},{2,3},{3,2},{4,5},{5,4},{6,7},{7,6},{8,9},{9,8},{10,11... | collective-permute-start | bytes 1572872 | tf_op jit(solution)/shard_map/ppermute | solution.py:23
  129.5 12.2 %experts.3 = (bf16[128,2048]{1,0:T(8,128)(2,1)S(1)}, bf16[128,2048]{1,0:T(8,128)(2,1)S(1)}, bf16[128,2048]{1,0:T(8,128)(2,1)S(1)}, bf16[128,2048]{1,0:T(8,128)(2,1)S(1)}) custom-call(f32[4,8,128]{2,1,0:T(8,128)S(1)} %pad_maximum_fusion.5.share_ref, bf16[128,2048]{1,0:T(8,128)(2,1)S(1)} %collective-permute-done.22.refs_0_, ...), custom_call_target="tpu_custom_call" | custom-call | flops 4831838208 | bytes 23068672 | tf_op jit(solution)/shard_map/experts/pallas_call | solution.py:219
  142.3 12.0 %experts.2 = (bf16[128,2048]{1,0:T(8,128)(2,1)S(1)}, bf16[128,2048]{1,0:T(8,128)(2,1)S(1)}, bf16[128,2048]{1,0:T(8,128)(2,1)S(1)}, bf16[128,2048]{1,0:T(8,128)(2,1)S(1)}) custom-call(f32[4,8,128]{2,1,0:T(8,128)S(1)} %pad_maximum_fusion.4.share_ref, bf16[128,2048]{1,0:T(8,128)(2,1)S(1)} %get-tuple-element.29.refs_0_, ...), custom_call_target="tpu_custom_call" | custom-call | flops 4831838208 | bytes 23068672 | tf_op jit(solution)/shard_map/experts/pallas_call | solution.py:219
  155.0 3.2 %collective-permute-start.27 = (bf16[128,2048]{1,0:T(8,128)(2,1)S(1)}, bf16[128,2048]{1,0:T(8,128)(2,1)S(1)}, u32[]{:S(2)}, u32[]{:S(2)}) collective-permute-start(bf16[128,2048]{1,0:T(8,128)(2,1)S(1)} %add_convert_fusion.2), channel_id=1, source_target_pairs={{0,4},{1,5},{2,6},{3,7},{4,0},{5,1},{6,2},{7,3},{8,12},{9,13},{10,... | collective-permute-start | bytes 1572872 | tf_op jit(solution)/shard_map/ppermute | solution.py:23
  159.8 31.3 %collective-permute-done.27 = bf16[128,2048]{1,0:T(8,128)(2,1)S(1)} collective-permute-done((bf16[128,2048]{1,0:T(8,128)(2,1)S(1)}, bf16[128,2048]{1,0:T(8,128)(2,1)S(1)}, u32[]{:S(2)}, u32[]{:S(2)}) %collective-permute-start.27) | collective-permute-done | bytes 524320 | tf_op jit(solution)/shard_map/ppermute | solution.py:23
  191.1 13.3 %collective-permute-done.29 = bf16[128,2048]{1,0:T(8,128)(2,1)S(1)} collective-permute-done((bf16[128,2048]{1,0:T(8,128)(2,1)S(1)}, bf16[128,2048]{1,0:T(8,128)(2,1)S(1)}, u32[]{:S(2)}, u32[]{:S(2)}) %collective-permute-start.29) | collective-permute-done | bytes 524320 | tf_op jit(solution)/shard_map/ppermute | solution.py:23
  (105 shorter events, 26.6 us)
Async XLA Ops:
  3.9 35.9 %collective-permute-start.11 = (bf16[1040,256]{1,0:T(8,128)(2,1)S(1)}, bf16[1040,256]{1,0:T(8,128)(2,1)S(1)}, u32[]{:S(2)}, u32[]{:S(2)}) collective-permute-start(bf16[1040,256]{1,0:T(8,128)(2,1)S(1)} %maximum_maximum_fusion.refs_0_), channel_id=1, source_target_pairs={{0,6},{1,7},{2,4},{3,5},{4,2},{5,3},{6,0},{7,1},{8,14},{9,15},{10,... | collective-permute-start | bytes 1597448 | tf_op jit(solution)/shard_map/ppermute | solution.py:23
  4.2 27.1 %collective-permute-start.3 = (bf16[1040,256]{1,0:T(8,128)(2,1)S(1)}, bf16[1040,256]{1,0:T(8,128)(2,1)S(1)}, u32[]{:S(2)}, u32[]{:S(2)}) collective-permute-start(bf16[1040,256]{1,0:T(8,128)(2,1)S(1)} %maximum_maximum_fusion.refs_0_), channel_id=1, source_target_pairs={{0,1},{1,0},{2,3},{3,2},{4,5},{5,4},{6,7},{7,6},{8,9},{9,8},{10,11... | collective-permute-start | bytes 1597448 | tf_op jit(solution)/shard_map/ppermute | solution.py:23
  6.2 9.4 %collective-permute-start.1 = (bf16[128,1280]{1,0:T(8,128)(2,1)S(1)}, bf16[128,1280]{1,0:T(8,128)(2,1)S(1)}, u32[]{:S(2)}, u32[]{:S(2)}) collective-permute-start(bf16[128,1280]{1,0:T(8,128)(2,1)S(1)} %pad_maximum_fusion.2), channel_id=1, source_target_pairs={{0,16},{8,24},{16,0},{24,8},{1,17},{9,25},{17,1},{25,9},{2,18},{10... | collective-permute-start | bytes 983048 | tf_op jit(solution)/shard_map/ppermute | solution.py:23
  8.2 10.6 %collective-permute-start = (bf16[128,1280]{1,0:T(8,128)(2,1)}, bf16[128,1280]{1,0:T(8,128)(2,1)S(1)}, u32[]{:S(2)}, u32[]{:S(2)}) collective-permute-start(bf16[128,1280]{1,0:T(8,128)(2,1)} %pad_maximum_fusion.1), channel_id=1, source_target_pairs={{0,8},{8,0},{16,24},{24,16},{1,9},{9,1},{17,25},{25,17},{2,10},{10... | collective-permute-start | bytes 983048 | tf_op jit(solution)/shard_map/ppermute | solution.py:23
  10.2 14.2 %collective-permute-start.2 = (bf16[128,1280]{1,0:T(8,128)(2,1)}, bf16[128,1280]{1,0:T(8,128)(2,1)S(1)}, u32[]{:S(2)}, u32[]{:S(2)}) collective-permute-start(bf16[128,1280]{1,0:T(8,128)(2,1)} %pad_maximum_fusion.3), channel_id=1, source_target_pairs={{0,24},{8,16},{16,8},{24,0},{1,25},{9,17},{17,9},{25,1},{2,26},{10... | collective-permute-start | bytes 983048 | tf_op jit(solution)/shard_map/ppermute | solution.py:23
  15.6 33.8 %collective-permute-start.9 = (bf16[1040,256]{1,0:T(8,128)(2,1)S(1)}, bf16[1040,256]{1,0:T(8,128)(2,1)S(1)}, u32[]{:S(2)}, u32[]{:S(2)}) collective-permute-start(bf16[1040,256]{1,0:T(8,128)(2,1)S(1)} %maximum_maximum_fusion.refs_0_), channel_id=1, source_target_pairs={{0,4},{1,5},{2,6},{3,7},{4,0},{5,1},{6,2},{7,3},{8,12},{9,13},{10,... | collective-permute-start | bytes 1597448 | tf_op jit(solution)/shard_map/ppermute | solution.py:23
  18.8 31.9 %collective-permute-start.4 = (bf16[1040,256]{1,0:T(8,128)(2,1)S(1)}, bf16[1040,256]{1,0:T(8,128)(2,1)S(1)}, u32[]{:S(2)}, u32[]{:S(2)}) collective-permute-start(bf16[1040,256]{1,0:T(8,128)(2,1)S(1)} %maximum_maximum_fusion.refs_0_), channel_id=1, source_target_pairs={{0,2},{1,3},{2,0},{3,1},{4,6},{5,7},{6,4},{7,5},{8,10},{9,11},{10,... | collective-permute-start | bytes 1597448 | tf_op jit(solution)/shard_map/ppermute | solution.py:23
  39.8 11.1 %collective-permute-start.12 = (bf16[1040,256]{1,0:T(8,128)(2,1)S(1)}, bf16[1040,256]{1,0:T(8,128)(2,1)S(1)}, u32[]{:S(2)}, u32[]{:S(2)}) collective-permute-start(bf16[1040,256]{1,0:T(8,128)(2,1)S(1)} %collective-permute-done.11.refs_2_), channel_id=1, source_target_pairs={{0,1},{1,0},{2,3},{3,2},{4,5},{5,4},{6,7},{7,6},{8,9},{9,8},{10,11... | collective-permute-start | bytes 1597448 | tf_op jit(solution)/shard_map/ppermute | solution.py:23
  54.8 8.5 %collective-permute-start.14 = (bf16[128,1024]{1,0:T(8,128)(2,1)S(1)}, bf16[128,1024]{1,0:T(8,128)(2,1)S(1)}, u32[]{:S(2)}, u32[]{:S(2)}) collective-permute-start(bf16[128,1024]{1,0:T(8,128)(2,1)S(1)} %get-tuple-element.26), channel_id=1, source_target_pairs={{0,16},{8,24},{16,0},{24,8},{1,17},{9,25},{17,1},{25,9},{2,18},{10... | collective-permute-start | bytes 786440 | tf_op jit(solution)/shard_map/ppermute | solution.py:23
  56.0 11.7 %collective-permute-start.15 = (bf16[128,1024]{1,0:T(8,128)(2,1)S(1)}, bf16[128,1024]{1,0:T(8,128)(2,1)S(1)}, u32[]{:S(2)}, u32[]{:S(2)}) collective-permute-start(bf16[128,1024]{1,0:T(8,128)(2,1)S(1)} %get-tuple-element.27), channel_id=1, source_target_pairs={{0,24},{8,16},{16,8},{24,0},{1,25},{9,17},{17,9},{25,1},{2,26},{10... | collective-permute-start | bytes 786440 | tf_op jit(solution)/shard_map/ppermute | solution.py:23
  57.5 14.9 %collective-permute-start.6 = (bf16[128,1024]{1,0:T(8,128)(2,1)S(1)}, bf16[128,1024]{1,0:T(8,128)(2,1)S(1)}, u32[]{:S(2)}, u32[]{:S(2)}) collective-permute-start(bf16[128,1024]{1,0:T(8,128)(2,1)S(1)} %get-tuple-element.21), channel_id=1, source_target_pairs={{0,8},{8,0},{16,24},{24,16},{1,9},{9,1},{17,25},{25,17},{2,10},{10... | collective-permute-start | bytes 786440 | tf_op jit(solution)/shard_map/ppermute | solution.py:23
  58.8 14.4 %collective-permute-start.7 = (bf16[128,1024]{1,0:T(8,128)(2,1)S(1)}, bf16[128,1024]{1,0:T(8,128)(2,1)S(1)}, u32[]{:S(2)}, u32[]{:S(2)}) collective-permute-start(bf16[128,1024]{1,0:T(8,128)(2,1)S(1)} %get-tuple-element.22), channel_id=1, source_target_pairs={{0,16},{8,24},{16,0},{24,8},{1,17},{9,25},{17,1},{25,9},{2,18},{10... | collective-permute-start | bytes 786440 | tf_op jit(solution)/shard_map/ppermute | solution.py:23
  61.1 17.9 %collective-permute-start.8 = (bf16[128,1024]{1,0:T(8,128)(2,1)S(1)}, bf16[128,1024]{1,0:T(8,128)(2,1)S(1)}, u32[]{:S(2)}, u32[]{:S(2)}) collective-permute-start(bf16[128,1024]{1,0:T(8,128)(2,1)S(1)} %get-tuple-element.23), channel_id=1, source_target_pairs={{0,24},{8,16},{16,8},{24,0},{1,25},{9,17},{17,9},{25,1},{2,26},{10... | collective-permute-start | bytes 786440 | tf_op jit(solution)/shard_map/ppermute | solution.py:23
  80.8 34.5 %collective-permute-start.24 = (bf16[128,2048]{1,0:T(8,128)(2,1)S(1)}, bf16[128,2048]{1,0:T(8,128)(2,1)S(1)}, u32[]{:S(2)}, u32[]{:S(2)}) collective-permute-start(bf16[128,2048]{1,0:T(8,128)(2,1)S(1)} %get-tuple-element.29.refs_0_), channel_id=1, source_target_pairs={{0,6},{1,7},{2,4},{3,5},{4,2},{5,3},{6,0},{7,1},{8,14},{9,15},{10,... | collective-permute-start | bytes 1572872 | tf_op jit(solution)/shard_map/ppermute | solution.py:23
  82.1 43.5 %collective-permute-start.22 = (bf16[128,2048]{1,0:T(8,128)(2,1)S(1)}, bf16[128,2048]{1,0:T(8,128)(2,1)S(1)}, u32[]{:S(2)}, u32[]{:S(2)}) collective-permute-start(bf16[128,2048]{1,0:T(8,128)(2,1)S(1)} %get-tuple-element.29.refs_0_), channel_id=1, source_target_pairs={{0,4},{1,5},{2,6},{3,7},{4,0},{5,1},{6,2},{7,3},{8,12},{9,13},{10,... | collective-permute-start | bytes 1572872 | tf_op jit(solution)/shard_map/ppermute | solution.py:23
  86.1 42.0 %collective-permute-start.17 = (bf16[128,2048]{1,0:T(8,128)(2,1)S(1)}, bf16[128,2048]{1,0:T(8,128)(2,1)S(1)}, u32[]{:S(2)}, u32[]{:S(2)}) collective-permute-start(bf16[128,2048]{1,0:T(8,128)(2,1)S(1)} %get-tuple-element.29.refs_0_), channel_id=1, source_target_pairs={{0,2},{1,3},{2,0},{3,1},{4,6},{5,7},{6,4},{7,5},{8,10},{9,11},{10,... | collective-permute-start | bytes 1572872 | tf_op jit(solution)/shard_map/ppermute | solution.py:23
  115.3 13.3 %collective-permute-start.25 = (bf16[128,2048]{1,0:T(8,128)(2,1)S(1)}, bf16[128,2048]{1,0:T(8,128)(2,1)S(1)}, u32[]{:S(2)}, u32[]{:S(2)}) collective-permute-start(bf16[128,2048]{1,0:T(8,128)(2,1)S(1)} %collective-permute-done.24.refs_2_), channel_id=1, source_target_pairs={{0,1},{1,0},{2,3},{3,2},{4,5},{5,4},{6,7},{7,6},{8,9},{9,8},{10,11... | collective-permute-start | bytes 1572872 | tf_op jit(solution)/shard_map/ppermute | solution.py:23
  128.0 14.3 %collective-permute-start.16 = (bf16[128,2048]{1,0:T(8,128)(2,1)S(1)}, bf16[128,2048]{1,0:T(8,128)(2,1)S(1)}, u32[]{:S(2)}, u32[]{:S(2)}) collective-permute-start(bf16[128,2048]{1,0:T(8,128)(2,1)S(1)} %get-tuple-element.29.refs_0_), channel_id=1, source_target_pairs={{0,1},{1,0},{2,3},{3,2},{4,5},{5,4},{6,7},{7,6},{8,9},{9,8},{10,11... | collective-permute-start | bytes 1572872 | tf_op jit(solution)/shard_map/ppermute | solution.py:23
  128.1 14.2 %collective-permute-start.18 = (bf16[128,2048]{1,0:T(8,128)(2,1)S(1)}, bf16[128,2048]{1,0:T(8,128)(2,1)S(1)}, u32[]{:S(2)}, u32[]{:S(2)}) collective-permute-start(bf16[128,2048]{1,0:T(8,128)(2,1)S(1)} %collective-permute-done.17.refs_2_), channel_id=1, source_target_pairs={{0,1},{1,0},{2,3},{3,2},{4,5},{5,4},{6,7},{7,6},{8,9},{9,8},{10,11... | collective-permute-start | bytes 1572872 | tf_op jit(solution)/shard_map/ppermute | solution.py:23
  141.7 13.2 %collective-permute-start.26 = (bf16[128,2048]{1,0:T(8,128)(2,1)S(1)}, bf16[128,2048]{1,0:T(8,128)(2,1)S(1)}, u32[]{:S(2)}, u32[]{:S(2)}) collective-permute-start(bf16[128,2048]{1,0:T(8,128)(2,1)S(1)} %get-tuple-element.35), channel_id=1, source_target_pairs={{0,1},{1,0},{2,3},{3,2},{4,5},{5,4},{6,7},{7,6},{8,9},{9,8},{10,11... | collective-permute-start | bytes 1572872 | tf_op jit(solution)/shard_map/ppermute | solution.py:23
  142.1 16.1 %collective-permute-start.28 = (bf16[128,2048]{1,0:T(8,128)(2,1)S(1)}, bf16[128,2048]{1,0:T(8,128)(2,1)S(1)}, u32[]{:S(2)}, u32[]{:S(2)}) collective-permute-start(bf16[128,2048]{1,0:T(8,128)(2,1)S(1)} %get-tuple-element.37), channel_id=1, source_target_pairs={{0,1},{1,0},{2,3},{3,2},{4,5},{5,4},{6,7},{7,6},{8,9},{9,8},{10,11... | collective-permute-start | bytes 1572872 | tf_op jit(solution)/shard_map/ppermute | solution.py:23
  155.0 36.1 %collective-permute-start.27 = (bf16[128,2048]{1,0:T(8,128)(2,1)S(1)}, bf16[128,2048]{1,0:T(8,128)(2,1)S(1)}, u32[]{:S(2)}, u32[]{:S(2)}) collective-permute-start(bf16[128,2048]{1,0:T(8,128)(2,1)S(1)} %add_convert_fusion.2), channel_id=1, source_target_pairs={{0,4},{1,5},{2,6},{3,7},{4,0},{5,1},{6,2},{7,3},{8,12},{9,13},{10,... | collective-permute-start | bytes 1572872 | tf_op jit(solution)/shard_map/ppermute | solution.py:23
  158.4 46.0 %collective-permute-start.29 = (bf16[128,2048]{1,0:T(8,128)(2,1)S(1)}, bf16[128,2048]{1,0:T(8,128)(2,1)S(1)}, u32[]{:S(2)}, u32[]{:S(2)}) collective-permute-start(bf16[128,2048]{1,0:T(8,128)(2,1)S(1)} %add_convert_fusion.1), channel_id=1, source_target_pairs={{0,6},{1,7},{2,4},{3,5},{4,2},{5,3},{6,0},{7,1},{8,14},{9,15},{10,... | collective-permute-start | bytes 1572872 | tf_op jit(solution)/shard_map/ppermute | solution.py:23
  158.7 45.6 %collective-permute-start.21 = (bf16[128,2048]{1,0:T(8,128)(2,1)S(1)}, bf16[128,2048]{1,0:T(8,128)(2,1)S(1)}, u32[]{:S(2)}, u32[]{:S(2)}) collective-permute-start(bf16[128,2048]{1,0:T(8,128)(2,1)S(1)} %add_convert_fusion.3), channel_id=1, source_target_pairs={{0,2},{1,3},{2,0},{3,1},{4,6},{5,7},{6,4},{7,5},{8,10},{9,11},{10,... | collective-permute-start | bytes 1572872 | tf_op jit(solution)/shard_map/ppermute | solution.py:23
  (14 other events, 310.8 us)

commit v2 on v1

v2 whole, which is shorter than its diff:
```python
import functools

import jax
import jax.numpy as jnp
from jax import lax
from jax.experimental import pallas as pl
from jax.experimental.pallas import tpu as pltpu
from jax.sharding import PartitionSpec as P

QUERY_HEAD_COUNT = 32
KEY_VALUE_HEADS = 4
HEAD_SIZE = 128
TOPK = 8
CAP = 64

norm_eps = 1e-06
mask_fill_value = -1e30
MIB = 1024 * 1024
VMEM_EXPERTS = 14
VMEM_PREPARE = 58


def swap(shard, axis, by):
    devices = lax.axis_size(axis)
    return lax.ppermute(shard, axis, [(i, i ^ by) for i in range(devices)])


def dot(a, b):
    return jnp.dot(a, b, preferred_element_type=jnp.float32)


def prepare_kernel(blocks, kv_heads, experts, marks_ref, q_ref, k_ref, v_ref, w_ref, ids_ref, gates_ref, *refs):
    outs, pack_ref, sems = refs[:blocks], refs[blocks], refs[blocks + 1]
    rows, width = q_ref.shape
    depth, piece = w_ref.shape
    wide, kv_wide = width // blocks, kv_heads * HEAD_SIZE
    group = QUERY_HEAD_COUNT // KEY_VALUE_HEADS
    copies = []
    for j in list(range(1, blocks)) + [0]:
        who = marks_ref[0] ^ j
        at = pl.ds(pl.multiple_of(who * wide, HEAD_SIZE), wide)
        kv_at = lax.div(who * (wide // HEAD_SIZE), group) * HEAD_SIZE
        kv_at = pl.ds(pl.multiple_of(kv_at, HEAD_SIZE), kv_wide)
        copies += [
            pltpu.make_async_copy(q_ref.at[:, at], outs[j].at[:, :wide], sems.at[3 * j]),
            pltpu.make_async_copy(
                k_ref.at[:, kv_at], outs[j].at[:, wide : wide + kv_wide], sems.at[3 * j + 1]
            ),
            pltpu.make_async_copy(
                v_ref.at[:, kv_at], outs[j].at[:, wide + kv_wide :], sems.at[3 * j + 2]
            ),
        ]
    copies.append(pltpu.make_async_copy(w_ref, pack_ref.at[:depth, :], sems.at[3 * blocks]))
    for copy in copies:
        copy.start()
    gates = gates_ref[...]
    shares = gates / jnp.sum(gates, axis=0, keepdims=True)
    expert = lax.broadcasted_iota(jnp.int32, (experts, rows), 0)
    by_expert = jnp.zeros((experts, rows), jnp.float32)
    for n in range(TOPK):
        by_expert += jnp.where(ids_ref[n : n + 1, :] == expert, shares[n : n + 1, :], 0.0)
    high = by_expert.astype(jnp.bfloat16)
    low = (by_expert - high.astype(jnp.float32)).astype(jnp.bfloat16)
    if piece >= 2 * rows:
        pack_ref[depth:, :rows] = high
        pack_ref[depth:, rows : 2 * rows] = low
    else:
        pack_ref[depth : depth + experts, :rows] = high
        pack_ref[depth + experts :, :rows] = low
    for copy in copies:
        copy.wait()


def prepare_call(marks, q, k, v, w, ids, gates, blocks, kv_heads, experts):
    rows, width = q.shape
    depth, piece = w.shape
    extra = experts if piece >= 2 * rows else 2 * experts
    wide = width // blocks + 2 * kv_heads * HEAD_SIZE
    in_vmem = pl.BlockSpec(memory_space=pltpu.VMEM)
    return pl.pallas_call(
        functools.partial(prepare_kernel, blocks, kv_heads, experts),
        out_shape=[pltpu.VMEM((rows, wide), jnp.bfloat16)] * blocks
        + [pltpu.VMEM((depth + extra, piece), jnp.bfloat16)],
        in_specs=[pl.BlockSpec(memory_space=pltpu.SMEM)]
        + [pl.BlockSpec(memory_space=pltpu.HBM)] * 4
        + [in_vmem] * 2,
        out_specs=[in_vmem] * (blocks + 1),
        scratch_shapes=[pltpu.SemaphoreType.DMA((3 * blocks + 1,))],
        compiler_params=pltpu.CompilerParams(vmem_limit_bytes=VMEM_PREPARE * MIB),
        cost_estimate=pl.CostEstimate(
            flops=rows * experts * 4 * TOPK,
            bytes_accessed=4 * (rows * (width + 4 * kv_heads * HEAD_SIZE) + depth * piece),
            transcendentals=0,
        ),
        name="prepare",
    )(marks, q, k, v, w, ids.T, gates.T)


def attention_kernel(blocks, heads, kv_heads, me_ref, *refs):
    ins, out_ref, seq = refs[:blocks], refs[blocks], refs[blocks + 1]
    rows = ins[0].shape[0]
    me = me_ref[0]
    wide = heads * HEAD_SIZE
    for j in range(blocks):
        seq[pl.ds(pl.multiple_of((me ^ j) * rows, rows), rows), :] = ins[j][...]
    row = lax.broadcasted_iota(jnp.int32, (rows, rows), 0)
    col = lax.broadcasted_iota(jnp.int32, (rows, rows), 1)
    allowed = row >= col
    for h in range(heads):
        g = h // (heads // kv_heads)
        key_at = wide + g * HEAD_SIZE
        value_at = wide + (kv_heads + g) * HEAD_SIZE
        for i in range(blocks):
            q = seq[i * rows : (i + 1) * rows, h * HEAD_SIZE : (h + 1) * HEAD_SIZE]
            k = seq[: (i + 1) * rows, key_at : key_at + HEAD_SIZE]
            v = seq[: (i + 1) * rows, value_at : value_at + HEAD_SIZE]
            s = lax.dot_general(
                q, k, (((1,), (1,)), ((), ())), preferred_element_type=jnp.float32
            ) * HEAD_SIZE ** (-0.5)
            last = jnp.where(allowed, s[:, i * rows :], mask_fill_value)
            s = last if i == 0 else jnp.concatenate([s[:, : i * rows], last], axis=1)
            p = jnp.exp(s - jnp.max(s, axis=1, keepdims=True))
            total = jnp.sum(p, axis=1, keepdims=True)
            o = dot(p.astype(jnp.bfloat16), v) / total
            out_ref[
                pl.ds(pl.multiple_of((me ^ i) * rows, rows), rows),
                h * HEAD_SIZE : (h + 1) * HEAD_SIZE,
            ] = o.astype(jnp.bfloat16)


def attention_call(me, ins, heads, kv_heads):
    blocks = len(ins)
    rows, wide_in = ins[0].shape
    length, wide = blocks * rows, heads * HEAD_SIZE
    return pl.pallas_call(
        functools.partial(attention_kernel, blocks, heads, kv_heads),
        out_shape=jax.ShapeDtypeStruct((length, wide), jnp.bfloat16),
        in_specs=[pl.BlockSpec(memory_space=pltpu.SMEM)]
        + [pl.BlockSpec(memory_space=pltpu.VMEM)] * blocks,
        out_specs=pl.BlockSpec(memory_space=pltpu.VMEM),
        scratch_shapes=[pltpu.VMEM((length, wide_in), jnp.bfloat16)],
        compiler_params=pltpu.CompilerParams(vmem_limit_bytes=12 * MIB),
        cost_estimate=pl.CostEstimate(
            flops=4 * length * length * wide,
            bytes_accessed=4 * length * wide_in,
            transcendentals=length * length * heads,
        ),
        name="attention",
    )(me, *ins)


def projection_kernel(pieces, att_ref, *refs):
    ins, outs = refs[:pieces], refs[pieces:]
    rows = outs[0].shape[0]
    depth = att_ref.shape[1]
    piece = ins[0].shape[1]
    for k in range(pieces):
        y = dot(att_ref[...], ins[k][:depth, :]).astype(jnp.bfloat16)
        for j, out in enumerate(outs):
            out[:, k * piece : (k + 1) * piece] = y[j * rows : (j + 1) * rows]


def projection_call(att, packs, blocks):
    length, depth = att.shape
    piece = packs[0].shape[1]
    rows, wide = length // blocks, piece * len(packs)
    return pl.pallas_call(
        functools.partial(projection_kernel, len(packs)),
        out_shape=[jax.ShapeDtypeStruct((rows, wide), jnp.bfloat16)] * blocks,
        in_specs=[pl.BlockSpec(memory_space=pltpu.VMEM)] * (1 + len(packs)),
        out_specs=[pl.BlockSpec(memory_space=pltpu.VMEM)] * blocks,
        compiler_params=pltpu.CompilerParams(vmem_limit_bytes=8 * MIB),
        cost_estimate=pl.CostEstimate(
            flops=2 * length * depth * wide,
            bytes_accessed=2 * (length * depth + depth * wide + length * wide),
            transcendentals=0,
        ),
        name="projection",
    )(att, *packs)


def norm_kernel(chunks, blocks, piece, me_ref, resid_ref, gain_ref, *refs):
    parts, (attn_ref, normed_ref) = refs[: chunks * blocks], refs[chunks * blocks :]
    me = me_ref[0]
    width = resid_ref.shape[1]
    total = None
    order = 0
    for n in range(chunks):
        for k in range(parts[n * blocks].shape[1] // piece):
            at = pl.ds(pl.multiple_of((me ^ order) * piece, piece), piece)
            order += 1
            acc = resid_ref[:, at].astype(jnp.float32)
            for j in range(blocks):
                acc = acc + parts[n * blocks + j][:, k * piece : (k + 1) * piece].astype(
                    jnp.float32
                )
            acc = acc.astype(jnp.bfloat16)
            attn_ref[:, at] = acc
            acc = acc.astype(jnp.float32)
            squares = jnp.sum(acc * acc, axis=1, keepdims=True)
            total = squares if total is None else total + squares
    scale = lax.rsqrt(total / width + norm_eps)
    normed_ref[...] = (attn_ref[...].astype(jnp.float32) * scale * gain_ref[...]).astype(
        jnp.bfloat16
    )


def norm_call(me, resid, gain, parts, blocks, piece):
    rows, width = resid.shape
    return pl.pallas_call(
        functools.partial(norm_kernel, len(parts) // blocks, blocks, piece),
        out_shape=[jax.ShapeDtypeStruct((rows, width), jnp.bfloat16)] * 2,
        in_specs=[pl.BlockSpec(memory_space=pltpu.SMEM)]
        + [pl.BlockSpec(memory_space=pltpu.VMEM)] * (2 + len(parts)),
        out_specs=[pl.BlockSpec(memory_space=pltpu.VMEM)] * 2,
        compiler_params=pltpu.CompilerParams(vmem_limit_bytes=8 * MIB),
        cost_estimate=pl.CostEstimate(
            flops=10 * rows * width, bytes_accessed=2 * rows * width * 8, transcendentals=rows
        ),
        name="resid_norm",
    )(me, resid, gain.reshape(1, width), *parts)


def experts_kernel(sources, local_experts, step, load, mark_ref, share_ref, *refs):
    ins = refs[:sources]
    weights = refs[sources : sources + 3]
    outs = refs[sources + 3 : 2 * sources + 3]
    refs = refs[2 * sources + 3 :]
    copies = [[] for _ in range(local_experts)]
    if load:
        held, refs, sems = refs[:3], refs[3:-1], refs[-1]
        for n in range(local_experts):
            for m in range(3):
                copy = pltpu.make_async_copy(weights[m].at[n], held[m].at[n], sems.at[n, m])
                copy.start()
                copies[n].append(copy)
        weights = held
    gate_ref, up_ref, down_ref = weights
    picked, slot_map, slot_share, hidden_rows, slot_out = refs
    rows = ins[0].shape[0]
    _, width, hidden = gate_ref.shape
    before = (
        lax.broadcasted_iota(jnp.int32, (rows, rows), 0)
        < lax.broadcasted_iota(jnp.int32, (rows, rows), 1)
    ).astype(jnp.bfloat16)
    slot = lax.broadcasted_iota(jnp.int32, (CAP, rows), 0).astype(jnp.float32)
    for s in range(sources):
        both = share_ref[s].astype(jnp.float32)
        if both.shape[1] >= 2 * rows:
            both = both[:, :rows] + both[:, rows : 2 * rows]
        else:
            both = both[: both.shape[0] // 2, :rows] + both[both.shape[0] // 2 :, :rows]
        expert = lax.broadcasted_iota(jnp.int32, both.shape, 0)
        place = lax.broadcasted_iota(jnp.int32, (8, rows), 0)
        share = jnp.zeros((8, rows), jnp.float32)
        for n in range(local_experts):
            mine = jnp.where(expert == mark_ref[0] * local_experts + n, both, 0.0)
            share = jnp.where(place == n, jnp.sum(mine, axis=0, keepdims=True), share)
        rank = dot((share > 0.0).astype(jnp.bfloat16), before)
        rank = jnp.where(share > 0.0, rank, -1.0)
        for n in range(local_experts):
            taken = slot == rank[n : n + 1, :]
            slot_map[s, n * CAP : (n + 1) * CAP, :] = taken.astype(jnp.bfloat16)
            slot_share[n, s * CAP : (s + 1) * CAP, :] = jnp.sum(
                jnp.where(taken, share[n : n + 1, :], 0.0), axis=1, keepdims=True
            )
        rows_picked = dot(slot_map[s], ins[s][...]).astype(jnp.bfloat16)
        for n in range(local_experts):
            picked[n, s * CAP : (s + 1) * CAP, :] = rows_picked[n * CAP : (n + 1) * CAP]
    for n in range(local_experts):
        for copy in copies[n]:
            copy.wait()
        x = picked[n]
        for at in range(0, hidden, step):
            gate_part = dot(x, gate_ref[n, :, at : at + step])
            up_part = dot(x, up_ref[n, :, at : at + step])
            activated = gate_part / (1.0 + jnp.exp(-gate_part)) * up_part * slot_share[n]
            hidden_rows[:, at : at + step] = activated.astype(jnp.bfloat16)
        for at in range(0, width, 2 * step):
            y = dot(hidden_rows[...], down_ref[n, :, at : at + 2 * step]).astype(jnp.bfloat16)
            for s in range(sources):
                slot_out[s, n * CAP : (n + 1) * CAP, at : at + 2 * step] = y[
                    s * CAP : (s + 1) * CAP
                ]
    for s in range(sources):
        outs[s][...] = lax.dot_general(
            slot_map[s], slot_out[s], (((0,), (0,)), ((), ())), preferred_element_type=jnp.float32
        ).astype(jnp.bfloat16)


def experts_call(mark, share, tokens, weights, load, step=256):
    sources = len(tokens)
    rows, width = tokens[0].shape
    local_experts, _, hidden = weights[0].shape
    slots = sources * CAP
    in_vmem = pl.BlockSpec(memory_space=pltpu.VMEM)
    held = [pltpu.VMEM(w.shape, w.dtype) for w in weights] if load else []
    outs = pl.pallas_call(
        functools.partial(experts_kernel, sources, local_experts, step, load),
        out_shape=[jax.ShapeDtypeStruct((rows, width), jnp.bfloat16)] * sources + held,
        in_specs=[pl.BlockSpec(memory_space=pltpu.SMEM)]
        + [in_vmem] * (sources + 1)
        + [pl.BlockSpec(memory_space=pl.ANY) if load else in_vmem] * 3,
        out_specs=[in_vmem] * (sources + len(held)),
        scratch_shapes=[
            pltpu.VMEM((local_experts, slots, width), jnp.bfloat16),
            pltpu.VMEM((sources, local_experts * CAP, rows), jnp.bfloat16),
            pltpu.VMEM((local_experts, slots, 1), jnp.float32),
            pltpu.VMEM((slots, hidden), jnp.bfloat16),
            pltpu.VMEM((sources, local_experts * CAP, width), jnp.bfloat16),
        ]
        + ([pltpu.SemaphoreType.DMA((local_experts, 3))] if load else []),
        compiler_params=pltpu.CompilerParams(vmem_limit_bytes=VMEM_EXPERTS * MIB),
        cost_estimate=pl.CostEstimate(
            flops=6 * local_experts * slots * width * hidden,
            bytes_accessed=2 * (3 * local_experts * width * hidden + 2 * sources * rows * width),
            transcendentals=local_experts * slots * hidden,
        ),
        name="experts_first" if load else "experts",
    )(mark, share, *tokens, *weights)
    return list(outs[:sources]), list(outs[sources:]) if load else weights


def send_near(own, chips):
    return [swap(own, "exp", 2 * k) for k in range(1, 3 if chips == 4 else chips)]


def send_far(own, near, chips, after):
    if chips != 4:
        return near, after
    two, own, after = lax.optimization_barrier((near[1], own, after))
    relayed = lax.ppermute(two, "exp", [(4, 6), (5, 7), (2, 0), (3, 1)])
    middle = lax.ppermute(own, "exp", [(2, 4), (3, 5), (4, 2), (5, 3)])
    return [near[0], two, (relayed, middle)], after


def take_far(arrays, chips, after):
    far, after = lax.optimization_barrier((arrays[-1], after))
    if chips == 4:
        chip = lax.axis_index("exp") // 2
        far = jnp.where((chip == 0) | (chip == 3), *far)
    return far, after


def local(
    queries,
    keys,
    values,
    resid,
    out_weight,
    norm_gain,
    expert_gate,
    expert_up,
    expert_down,
    route_ids,
    route_gates,
):
    rows = queries.shape[1]
    ctx_count = lax.axis_size("ctx")
    exp_count = lax.axis_size("exp")
    chips = exp_count // 2
    ctx_me, exp_me = lax.axis_index("ctx"), lax.axis_index("exp")
    local_experts = expert_gate.shape[0]
    heads = QUERY_HEAD_COUNT // ctx_count
    group = QUERY_HEAD_COUNT // KEY_VALUE_HEADS
    kv_heads = max(1, heads // group)

    ctx_mark, exp_mark = (jnp.full((1,), me, jnp.int32) for me in (ctx_me, exp_me))
    piece = out_weight.shape[1]

    *blocks_out, pack = prepare_call(
        ctx_mark,
        queries[0],
        keys[0],
        values[0],
        out_weight,
        route_ids[0],
        route_gates[0],
        ctx_count,
        kv_heads,
        local_experts * exp_count,
    )
    pack_chips = send_near(pack, chips)
    blocks_in = blocks_out[:1] + [swap(blocks_out[j], "ctx", j) for j in range(1, ctx_count)]

    att = attention_call(ctx_mark, blocks_in, heads, kv_heads)
    pack_chips, att = send_far(pack, pack_chips, chips, att)

    def project(some):
        mine = projection_call(att, some, ctx_count)
        return [mine[0]] + [swap(mine[j], "ctx", j) for j in range(1, ctx_count)]

    def with_pair(arrays):
        return [both for a in arrays for both in (a, swap(a, "exp", 1))]

    last = chips - 1
    packs = with_pair([pack, pack_chips[0]])
    parts = project(packs)
    middle_packs = with_pair(pack_chips[1 : last - 1])
    parts_middle = project(middle_packs)
    pack_last, (parts, parts_middle[0]) = take_far(pack_chips, chips, (parts, parts_middle[0]))
    packs_last = with_pair([pack_last])
    parts = parts + parts_middle + project(packs_last)
    share = jnp.stack([p[out_weight.shape[0] :] for p in packs + middle_packs + packs_last])
    parts[0], share = lax.optimization_barrier((parts[0], share))
    attn_resid, normed = norm_call(exp_mark, resid[0], norm_gain, parts, ctx_count, piece)

    def experts(which, tokens, weights):
        at = slice(2 * which.start, 2 * which.stop)
        return experts_call(exp_mark, share[at], with_pair(tokens), weights, which.start == 0)

    token_near = send_near(normed, chips)
    partial, weights = experts(
        slice(0, 1), [normed], [expert_gate, expert_up, expert_down]
    )
    token_chips, partial = send_far(normed, token_near, chips, partial)
    token_chips[0], partial[0] = lax.optimization_barrier((token_chips[0], partial[0]))
    more, _ = experts(slice(1, last), token_chips[: last - 1], weights)
    partial = partial + more

    def pair_sum(k):
        return partial[2 * k].astype(jnp.float32) + swap(partial[2 * k + 1], "exp", 1).astype(
            jnp.float32
        )

    layer_out = attn_resid.astype(jnp.float32) + pair_sum(0)
    terms = [swap(pair_sum(k).astype(jnp.bfloat16), "exp", 2 * k) for k in range(1, last)]
    token_last, more = take_far(token_chips, chips, more)
    partial += experts(slice(last, chips), [token_last], weights)[0]
    far, terms = lax.optimization_barrier((pair_sum(last).astype(jnp.bfloat16), terms))
    final = swap(far, "exp", 2 * last)
    for s in terms:
        layer_out = layer_out + s.astype(jnp.float32)
    layer_out = lax.optimization_barrier(layer_out) + final.astype(jnp.float32)
    return (attn_resid[None], layer_out.astype(jnp.bfloat16)[None])


def solution(mesh):
    in_specs = (
        P("exp", "ctx", None),
        P("exp", "ctx", None),
        P("exp", "ctx", None),
        P("exp", "ctx", None),
        P("ctx", "exp"),
        P(),
        P("exp", None, None),
        P("exp", None, None),
        P("exp", None, None),
        P("exp", "ctx", None),
        P("exp", "ctx", None),
    )
    out_specs = (P("exp", "ctx", None), P("exp", "ctx", None))
    return jax.shard_map(local, mesh=mesh, in_specs=in_specs, out_specs=out_specs, check_vma=False)
```

time: 206 us -> 176 us (0.85)
  the two profiles are of different devices: /device:TPU:17 before, /device:TPU:16 now
where the time goes in v2:
time: 176 us
  waiting for transfers between devices  99.9 us (57%)
  starting transfers between devices  37.7 us (21%)
  Pallas kernels  30.1 us (17%)
  local copies, waits for them, and re-layouts  5.62 us (3%)
  other arithmetic  1.84 us (1%)
    ppermute x31, waiting for transfers between devices, swap(): return lax.ppermute(shard, axis, [(i, i ^ by) for i in range(devices)])  87.5 us
    ppermute x31, starting transfers between devices, swap(): return lax.ppermute(shard, axis, [(i, i ^ by) for i in range(devices)])  26.9 us
    pallas_call x3, Pallas kernels, experts_call(): pl.pallas_call(functools.partial(experts_kernel, sources, local_experts,...  15.8 us
    ppermute x2, waiting for transfers between devices, send_far(): middle = lax.ppermute(own, 'exp', [(2, 4), (3, 5), (4, 2), (5, 3)])  12.4 us
    pallas_call x1, Pallas kernels, attention_call(): pl.pallas_call(functools.partial(attention_kernel, blocks, heads, kv_head...  8.03 us
    ppermute x2, starting transfers between devices, send_far(): relayed = lax.ppermute(two, 'exp', [(4, 6), (5, 7), (2, 0), (3, 1)])  5.96 us
    unnamed x21, local copies, waits for them, and re-layouts  5.61 us
    ppermute x2, starting transfers between devices, send_far(): middle = lax.ppermute(own, 'exp', [(2, 4), (3, 5), (4, 2), (5, 3)])  4.89 us
  transfers between devices with their start and end apart: 35, of which 16 were waited for; matrix products, arithmetic and copies ran while one was open for 0% of the time, Pallas kernels for 15%

profile of v2, /device:TPU:16, one launch (start us, length us, event | category | flops | bytes accessed | tf_op | source)
XLA Modules:
  0.0 176.2 jit_solution(8135091003243288859)
XLA Ops:
  0.6 2.3 %prepare.1 = (bf16[128,1280]{1,0:T(8,128)(2,1)S(1)}, bf16[128,1280]{1,0:T(8,128)(2,1)S(1)}, bf16[128,1280]{1,0:T(8,128)(2,1)S(1)}, bf16[128,1280]{1,0:T(8,128)(2,1)S(1)}, bf16[1040,256]{1,0:T(8,128)(2,1)S(1)}) custom-call(s32[1]{0:T(128)} %bitcast.3.marks_ref.me_ref, bf16[128,4096]{1,0:T(8,128)(2,1)} %bitcast.48, bf16[128,512]{1,0:T(8,128)(2,1)} %bitcast.50, ...), custom_call_target="tpu_custom_call" | custom-call | flops 65536 | bytes 3407872 | tf_op jit(solution)/shard_map/prepare/pallas_call | solution.py:80
  7.9 4.5 %collective-permute-done.1.refs_1_ = bf16[128,1280]{1,0:T(8,128)(2,1)S(1)} collective-permute-done((bf16[128,1280]{1,0:T(8,128)(2,1)S(1)}, bf16[128,1280]{1,0:T(8,128)(2,1)S(1)}, u32[]{:S(2)}, u32[]{:S(2)}) %collective-permute-start.1) | collective-permute-done | bytes 327712 | tf_op jit(solution)/shard_map/ppermute | solution.py:25
  12.5 2.4 %collective-permute-start.3 = (bf16[128,1280]{1,0:T(8,128)(2,1)S(1)}, bf16[128,1280]{1,0:T(8,128)(2,1)}, u32[]{:S(2)}, u32[]{:S(2)}) collective-permute-start(bf16[128,1280]{1,0:T(8,128)(2,1)S(1)} %get-tuple-element.59), channel_id=1, source_target_pairs={{0,24},{8,16},{16,8},{24,0},{1,25},{9,17},{17,9},{25,1},{2,26},{10... | collective-permute-start | bytes 983048 | tf_op jit(solution)/shard_map/ppermute | solution.py:25
  14.9 12.4 %collective-permute-done.7.refs_2_ = bf16[1040,256]{1,0:T(8,128)(2,1)S(1)} collective-permute-done((bf16[1040,256]{1,0:T(8,128)(2,1)S(1)}, bf16[1040,256]{1,0:T(8,128)(2,1)S(1)}, u32[]{:S(2)}, u32[]{:S(2)}) %collective-permute-start.7) | collective-permute-done | bytes 532512 | tf_op jit(solution)/shard_map/ppermute | solution.py:25
  27.4 8.0 %attention.1.att_ref = bf16[512,1024]{1,0:T(8,128)(2,1)S(1)} custom-call(s32[1]{0:T(128)} %bitcast.3.marks_ref.me_ref, bf16[128,1280]{1,0:T(8,128)(2,1)S(1)} %get-tuple-element.56.refs_0_, bf16[128,1280]{1,0:T(8,128)(2,1)S(1)} %collective-permute-done.1.refs_1_, bf16[128,1280]{1,0:T(8,128)(2,1)} %collective-permute-done.2.refs_2_, ...), custom_call_target="tpu_custom_call" | custom-call | flops 1073741824 | bytes 2621440 | tf_op jit(solution)/shard_map/attention/pallas_call | solution.py:135
  36.0 4.4 %collective-permute-start.4 = (bf16[1040,256]{1,0:T(8,128)(2,1)S(1)}, bf16[1040,256]{1,0:T(8,128)(2,1)S(1)}, u32[]{:S(2)}, u32[]{:S(2)}) collective-permute-start(bf16[1040,256]{1,0:T(8,128)(2,1)S(1)} %collective-permute-done.refs_0_), channel_id=1, source_target_pairs={{4,6},{5,7},{2,0},{3,1},{12,14},{13,15},{10,8},{11,9},{20,22},{21,... | collective-permute-start | bytes 1597448 | tf_op jit(solution)/shard_map/ppermute | solution.py:332
  40.4 2.5 %collective-permute-start.5 = (bf16[1040,256]{1,0:T(8,128)(2,1)S(1)}, bf16[1040,256]{1,0:T(8,128)(2,1)S(1)}, u32[]{:S(2)}, u32[]{:S(2)}) collective-permute-start(bf16[1040,256]{1,0:T(8,128)(2,1)S(1)} %get-tuple-element.61.refs_0_), channel_id=1, source_target_pairs={{2,4},{3,5},{4,2},{5,3},{10,12},{11,13},{12,10},{13,11},{18,20},{1... | collective-permute-start | bytes 1597448 | tf_op jit(solution)/shard_map/ppermute | solution.py:333
  48.6 7.5 %collective-permute-done.5 = bf16[1040,256]{1,0:T(8,128)(2,1)S(1)} collective-permute-done((bf16[1040,256]{1,0:T(8,128)(2,1)S(1)}, bf16[1040,256]{1,0:T(8,128)(2,1)S(1)}, u32[]{:S(2)}, u32[]{:S(2)}) %collective-permute-start.5) | collective-permute-done | bytes 532512 | tf_op jit(solution)/shard_map/ppermute | solution.py:333
  68.5 2.3 %collective-permute-done.17.refs_9_ = bf16[128,512]{1,0:T(8,128)(2,1)S(1)} collective-permute-done((bf16[128,512]{1,0:T(8,128)(2,1)S(1)}, bf16[128,512]{1,0:T(8,128)(2,1)S(1)}, u32[]{:S(2)}, u32[]{:S(2)}) %collective-permute-start.17) | collective-permute-done | bytes 131104 | tf_op jit(solution)/shard_map/ppermute | solution.py:25
  70.8 2.8 %collective-permute-done.18.refs_10_ = bf16[128,512]{1,0:T(8,128)(2,1)S(1)} collective-permute-done((bf16[128,512]{1,0:T(8,128)(2,1)S(1)}, bf16[128,512]{1,0:T(8,128)(2,1)S(1)}, u32[]{:S(2)}, u32[]{:S(2)}) %collective-permute-start.18) | collective-permute-done | bytes 131104 | tf_op jit(solution)/shard_map/ppermute | solution.py:25
  74.9 3.0 %collective-permute-start.20 = (bf16[128,2048]{1,0:T(8,128)(2,1)S(1)}, bf16[128,2048]{1,0:T(8,128)(2,1)S(1)}, u32[]{:S(2)}, u32[]{:S(2)}) collective-permute-start(bf16[128,2048]{1,0:T(8,128)(2,1)S(1)} %get-tuple-element.92.refs_0_), channel_id=1, source_target_pairs={{0,2},{1,3},{2,0},{3,1},{4,6},{5,7},{6,4},{7,5},{8,10},{9,11},{10,... | collective-permute-start | bytes 1572872 | tf_op jit(solution)/shard_map/ppermute | solution.py:25
  77.9 2.8 %copy-done = bf16[2,2048,768]{2,1,0:T(8,128)(2,1)S(1)} copy-done((bf16[2,2048,768]{2,1,0:T(8,128)(2,1)S(1)}, bf16[2,2048,768]{2,1,0:T(8,128)(2,1)}, u32[]{:S(2)}) %copy-start) | copy-done | bytes 6291480
  80.7 2.8 %copy-done.1 = bf16[2,768,2048]{2,1,0:T(8,128)(2,1)S(1)} copy-done((bf16[2,768,2048]{2,1,0:T(8,128)(2,1)S(1)}, bf16[2,768,2048]{2,1,0:T(8,128)(2,1)}, u32[]{:S(2)}) %copy-start.1) | copy-done | bytes 6291480
  83.5 5.3 %experts_first.1 = (bf16[128,2048]{1,0:T(8,128)(2,1)S(1)}, bf16[128,2048]{1,0:T(8,128)(2,1)S(1)}, bf16[2,2048,768]{2,1,0:T(8,128)(2,1)S(1)}, bf16[2,2048,768]{2,1,0:T(8,128)(2,1)S(1)}, bf16[2,768,2048]{2,1,0:T(8,128)(2,1)S(1)}) custom-call(s32[1]{0:T(128)} %bitcast.me_ref.mark_ref, bf16[2,16,256]{2,1,0:T(8,128)(2,1)S(1)} %get-tuple-element.108.share_ref, ...), custom_call_target="tpu_custom_call" | custom-call | flops 2415919104 | bytes 20971520 | tf_op jit(solution)/shard_map/experts_first/pallas_call | solution.py:298
  88.8 9.4 %collective-permute-done.21.refs_2_ = bf16[128,2048]{1,0:T(8,128)(2,1)S(1)} collective-permute-done((bf16[128,2048]{1,0:T(8,128)(2,1)S(1)}, bf16[128,2048]{1,0:T(8,128)(2,1)S(1)}, u32[]{:S(2)}, u32[]{:S(2)}) %collective-permute-start.21) | collective-permute-done | bytes 524320 | tf_op jit(solution)/shard_map/ppermute | solution.py:25
  98.2 3.3 %collective-permute-done.20.refs_0_ = bf16[128,2048]{1,0:T(8,128)(2,1)S(1)} collective-permute-done((bf16[128,2048]{1,0:T(8,128)(2,1)S(1)}, bf16[128,2048]{1,0:T(8,128)(2,1)S(1)}, u32[]{:S(2)}, u32[]{:S(2)}) %collective-permute-start.20) | collective-permute-done | bytes 524320 | tf_op jit(solution)/shard_map/ppermute | solution.py:25
  102.0 2.4 %collective-permute-start.25 = (bf16[128,2048]{1,0:T(8,128)(2,1)S(1)}, bf16[128,2048]{1,0:T(8,128)(2,1)S(1)}, u32[]{:S(2)}, u32[]{:S(2)}) collective-permute-start(bf16[128,2048]{1,0:T(8,128)(2,1)S(1)} %get-tuple-element.92.refs_0_), channel_id=1, source_target_pairs={{2,4},{3,5},{4,2},{5,3},{10,12},{11,13},{12,10},{13,11},{18,20},{1... | collective-permute-start | bytes 1572872 | tf_op jit(solution)/shard_map/ppermute | solution.py:333
  105.9 6.9 %experts.2 = (bf16[128,2048]{1,0:T(8,128)(2,1)S(1)}, bf16[128,2048]{1,0:T(8,128)(2,1)S(1)}, bf16[128,2048]{1,0:T(8,128)(2,1)S(1)}, bf16[128,2048]{1,0:T(8,128)(2,1)S(1)}) custom-call(s32[1]{0:T(128)} %bitcast.me_ref.mark_ref, bf16[4,16,256]{2,1,0:T(8,128)(2,1)S(1)} %slice.43.share_ref, bf16[128,2048]{1,0:T(8,128)(2,1)S(1)} %collective-permute-done.20.refs_0_, ...), custom_call_target="tpu_custom_call" | custom-call | flops 4831838208 | bytes 23068672 | tf_op jit(solution)/shard_map/experts/pallas_call | solution.py:298
  112.8 4.9 %collective-permute-done.25 = bf16[128,2048]{1,0:T(8,128)(2,1)S(1)} collective-permute-done((bf16[128,2048]{1,0:T(8,128)(2,1)S(1)}, bf16[128,2048]{1,0:T(8,128)(2,1)S(1)}, u32[]{:S(2)}, u32[]{:S(2)}) %collective-permute-start.25) | collective-permute-done | bytes 524320 | tf_op jit(solution)/shard_map/ppermute | solution.py:333
  119.7 3.7 %experts.3 = (bf16[128,2048]{1,0:T(8,128)(2,1)S(1)}, bf16[128,2048]{1,0:T(8,128)(2,1)S(1)}) custom-call(s32[1]{0:T(128)} %bitcast.me_ref.mark_ref, bf16[2,16,256]{2,1,0:T(8,128)(2,1)S(1)} %get-tuple-element.109.share_ref, bf16[128,2048]{1,0:T(8,128)(2,1)S(1)} %broadcast_select_fusion.1.refs_0_, bf16[128,2048]{1,0:T(8,128)(2,1)S(1)} %collective-permute-done.28.refs_1_, ...), custom_call_target="tpu_custom_call" | custom-call | flops 2415919104 | bytes 20971520 | tf_op jit(solution)/shard_map/experts/pallas_call | solution.py:298
  123.7 1.8 %collective-permute-start.31 = (bf16[128,2048]{1,0:T(8,128)(2,1)S(1)}, bf16[128,2048]{1,0:T(8,128)(2,1)S(1)}, u32[]{:S(2)}, u32[]{:S(2)}) collective-permute-start(bf16[128,2048]{1,0:T(8,128)(2,1)S(1)} %add_convert_fusion.2), channel_id=1, source_target_pairs={{0,2},{1,3},{2,0},{3,1},{4,6},{5,7},{6,4},{7,5},{8,10},{9,11},{10,... | collective-permute-start | bytes 1572872 | tf_op jit(solution)/shard_map/ppermute | solution.py:25
  127.1 21.0 %collective-permute-done.31 = bf16[128,2048]{1,0:T(8,128)(2,1)S(1)} collective-permute-done((bf16[128,2048]{1,0:T(8,128)(2,1)S(1)}, bf16[128,2048]{1,0:T(8,128)(2,1)S(1)}, u32[]{:S(2)}, u32[]{:S(2)}) %collective-permute-start.31) | collective-permute-done | bytes 524320 | tf_op jit(solution)/shard_map/ppermute | solution.py:25
  148.1 2.3 %collective-permute-done.33 = bf16[128,2048]{1,0:T(8,128)(2,1)S(1)} collective-permute-done((bf16[128,2048]{1,0:T(8,128)(2,1)S(1)}, bf16[128,2048]{1,0:T(8,128)(2,1)S(1)}, u32[]{:S(2)}, u32[]{:S(2)}) %collective-permute-start.33) | collective-permute-done | bytes 524320 | tf_op jit(solution)/shard_map/ppermute | solution.py:25
  151.2 24.0 %collective-permute-done.34 = bf16[128,2048]{1,0:T(8,128)(2,1)S(1)} collective-permute-done((bf16[128,2048]{1,0:T(8,128)(2,1)S(1)}, bf16[128,2048]{1,0:T(8,128)(2,1)S(1)}, u32[]{:S(2)}, u32[]{:S(2)}) %collective-permute-start.34) | collective-permute-done | bytes 524320 | tf_op jit(solution)/shard_map/ppermute | solution.py:25
  (87 shorter events, 32.4 us)
Async XLA Ops:
  3.0 9.5 %collective-permute-start.1 = (bf16[128,1280]{1,0:T(8,128)(2,1)S(1)}, bf16[128,1280]{1,0:T(8,128)(2,1)S(1)}, u32[]{:S(2)}, u32[]{:S(2)}) collective-permute-start(bf16[128,1280]{1,0:T(8,128)(2,1)S(1)} %get-tuple-element.57), channel_id=1, source_target_pairs={{0,8},{8,0},{16,24},{24,16},{1,9},{9,1},{17,25},{25,17},{2,10},{10... | collective-permute-start | bytes 983048 | tf_op jit(solution)/shard_map/ppermute | solution.py:25
  4.5 22.8 %collective-permute-start.7 = (bf16[1040,256]{1,0:T(8,128)(2,1)S(1)}, bf16[1040,256]{1,0:T(8,128)(2,1)S(1)}, u32[]{:S(2)}, u32[]{:S(2)}) collective-permute-start(bf16[1040,256]{1,0:T(8,128)(2,1)S(1)} %get-tuple-element.61.refs_0_), channel_id=1, source_target_pairs={{0,2},{1,3},{2,0},{3,1},{4,6},{5,7},{6,4},{7,5},{8,10},{9,11},{10,... | collective-permute-start | bytes 1597448 | tf_op jit(solution)/shard_map/ppermute | solution.py:25
  6.1 29.3 %collective-permute-start = (bf16[1040,256]{1,0:T(8,128)(2,1)S(1)}, bf16[1040,256]{1,0:T(8,128)(2,1)S(1)}, u32[]{:S(2)}, u32[]{:S(2)}) collective-permute-start(bf16[1040,256]{1,0:T(8,128)(2,1)S(1)} %get-tuple-element.61.refs_0_), channel_id=1, source_target_pairs={{0,4},{1,5},{2,6},{3,7},{4,0},{5,1},{6,2},{7,3},{8,12},{9,13},{10,... | collective-permute-start | bytes 1597448 | tf_op jit(solution)/shard_map/ppermute | solution.py:25
  6.4 36.5 %collective-permute-start.6 = (bf16[1040,256]{1,0:T(8,128)(2,1)S(1)}, bf16[1040,256]{1,0:T(8,128)(2,1)S(1)}, u32[]{:S(2)}, u32[]{:S(2)}) collective-permute-start(bf16[1040,256]{1,0:T(8,128)(2,1)S(1)} %get-tuple-element.61.refs_0_), channel_id=1, source_target_pairs={{0,1},{1,0},{2,3},{3,2},{4,5},{5,4},{6,7},{7,6},{8,9},{9,8},{10,11... | collective-permute-start | bytes 1597448 | tf_op jit(solution)/shard_map/ppermute | solution.py:25
  6.4 20.9 %collective-permute-start.2 = (bf16[128,1280]{1,0:T(8,128)(2,1)S(1)}, bf16[128,1280]{1,0:T(8,128)(2,1)}, u32[]{:S(2)}, u32[]{:S(2)}) collective-permute-start(bf16[128,1280]{1,0:T(8,128)(2,1)S(1)} %get-tuple-element.58), channel_id=1, source_target_pairs={{0,16},{8,24},{16,0},{24,8},{1,17},{9,25},{17,1},{25,9},{2,18},{10... | collective-permute-start | bytes 983048 | tf_op jit(solution)/shard_map/ppermute | solution.py:25
  12.5 14.9 %collective-permute-start.3 = (bf16[128,1280]{1,0:T(8,128)(2,1)S(1)}, bf16[128,1280]{1,0:T(8,128)(2,1)}, u32[]{:S(2)}, u32[]{:S(2)}) collective-permute-start(bf16[128,1280]{1,0:T(8,128)(2,1)S(1)} %get-tuple-element.59), channel_id=1, source_target_pairs={{0,24},{8,16},{16,8},{24,0},{1,25},{9,17},{17,9},{25,1},{2,26},{10... | collective-permute-start | bytes 983048 | tf_op jit(solution)/shard_map/ppermute | solution.py:25
  27.3 15.7 %collective-permute-start.8 = (bf16[1040,256]{1,0:T(8,128)(2,1)S(1)}, bf16[1040,256]{1,0:T(8,128)(2,1)S(1)}, u32[]{:S(2)}, u32[]{:S(2)}) collective-permute-start(bf16[1040,256]{1,0:T(8,128)(2,1)S(1)} %collective-permute-done.7.refs_2_), channel_id=1, source_target_pairs={{0,1},{1,0},{2,3},{3,2},{4,5},{5,4},{6,7},{7,6},{8,9},{9,8},{10,11... | collective-permute-start | bytes 1597448 | tf_op jit(solution)/shard_map/ppermute | solution.py:25
  35.4 11.0 %collective-permute-start.12 = (bf16[1040,256]{1,0:T(8,128)(2,1)S(1)}, bf16[1040,256]{1,0:T(8,128)(2,1)S(1)}, u32[]{:S(2)}, u32[]{:S(2)}) collective-permute-start(bf16[1040,256]{1,0:T(8,128)(2,1)S(1)} %collective-permute-done.refs_0_), channel_id=1, source_target_pairs={{0,1},{1,0},{2,3},{3,2},{4,5},{5,4},{6,7},{7,6},{8,9},{9,8},{10,11... | collective-permute-start | bytes 1597448 | tf_op jit(solution)/shard_map/ppermute | solution.py:25
  36.0 20.1 %collective-permute-start.4 = (bf16[1040,256]{1,0:T(8,128)(2,1)S(1)}, bf16[1040,256]{1,0:T(8,128)(2,1)S(1)}, u32[]{:S(2)}, u32[]{:S(2)}) collective-permute-start(bf16[1040,256]{1,0:T(8,128)(2,1)S(1)} %collective-permute-done.refs_0_), channel_id=1, source_target_pairs={{4,6},{5,7},{2,0},{3,1},{12,14},{13,15},{10,8},{11,9},{20,22},{21,... | collective-permute-start | bytes 1597448 | tf_op jit(solution)/shard_map/ppermute | solution.py:332
  40.4 15.6 %collective-permute-start.5 = (bf16[1040,256]{1,0:T(8,128)(2,1)S(1)}, bf16[1040,256]{1,0:T(8,128)(2,1)S(1)}, u32[]{:S(2)}, u32[]{:S(2)}) collective-permute-start(bf16[1040,256]{1,0:T(8,128)(2,1)S(1)} %get-tuple-element.61.refs_0_), channel_id=1, source_target_pairs={{2,4},{3,5},{4,2},{5,3},{10,12},{11,13},{12,10},{13,11},{18,20},{1... | collective-permute-start | bytes 1597448 | tf_op jit(solution)/shard_map/ppermute | solution.py:333
  44.3 11.8 %collective-permute-start.9 = (bf16[128,1024]{1,0:T(8,128)(2,1)S(1)}, bf16[128,1024]{1,0:T(8,128)(2,1)S(1)}, u32[]{:S(2)}, u32[]{:S(2)}) collective-permute-start(bf16[128,1024]{1,0:T(8,128)(2,1)S(1)} %get-tuple-element.64), channel_id=1, source_target_pairs={{0,8},{8,0},{16,24},{24,16},{1,9},{9,1},{17,25},{25,17},{2,10},{10... | collective-permute-start | bytes 786440 | tf_op jit(solution)/shard_map/ppermute | solution.py:25
  44.7 12.3 %collective-permute-start.10 = (bf16[128,1024]{1,0:T(8,128)(2,1)S(1)}, bf16[128,1024]{1,0:T(8,128)(2,1)S(1)}, u32[]{:S(2)}, u32[]{:S(2)}) collective-permute-start(bf16[128,1024]{1,0:T(8,128)(2,1)S(1)} %get-tuple-element.65), channel_id=1, source_target_pairs={{0,16},{8,24},{16,0},{24,8},{1,17},{9,25},{17,1},{25,9},{2,18},{10... | collective-permute-start | bytes 786440 | tf_op jit(solution)/shard_map/ppermute | solution.py:25
  46.4 12.2 %collective-permute-start.11 = (bf16[128,1024]{1,0:T(8,128)(2,1)S(1)}, bf16[128,1024]{1,0:T(8,128)(2,1)S(1)}, u32[]{:S(2)}, u32[]{:S(2)}) collective-permute-start(bf16[128,1024]{1,0:T(8,128)(2,1)S(1)} %get-tuple-element.66), channel_id=1, source_target_pairs={{0,24},{8,16},{16,8},{24,0},{1,25},{9,17},{17,9},{25,1},{2,26},{10... | collective-permute-start | bytes 786440 | tf_op jit(solution)/shard_map/ppermute | solution.py:25
  59.6 8.1 %collective-permute-start.15 = (bf16[128,512]{1,0:T(8,128)(2,1)S(1)}, bf16[128,512]{1,0:T(8,128)(2,1)S(1)}, u32[]{:S(2)}, u32[]{:S(2)}) collective-permute-start(bf16[128,512]{1,0:T(8,128)(2,1)S(1)} %get-tuple-element.77), channel_id=1, source_target_pairs={{0,16},{8,24},{16,0},{24,8},{1,17},{9,25},{17,1},{25,9},{2,18},{10... | collective-permute-start | bytes 393224 | tf_op jit(solution)/shard_map/ppermute | solution.py:25
  63.9 9.7 %collective-permute-start.18 = (bf16[128,512]{1,0:T(8,128)(2,1)S(1)}, bf16[128,512]{1,0:T(8,128)(2,1)S(1)}, u32[]{:S(2)}, u32[]{:S(2)}) collective-permute-start(bf16[128,512]{1,0:T(8,128)(2,1)S(1)} %get-tuple-element.81), channel_id=1, source_target_pairs={{0,16},{8,24},{16,0},{24,8},{1,17},{9,25},{17,1},{25,9},{2,18},{10... | collective-permute-start | bytes 393224 | tf_op jit(solution)/shard_map/ppermute | solution.py:25
  65.4 8.2 %collective-permute-start.19 = (bf16[128,512]{1,0:T(8,128)(2,1)S(1)}, bf16[128,512]{1,0:T(8,128)(2,1)S(1)}, u32[]{:S(2)}, u32[]{:S(2)}) collective-permute-start(bf16[128,512]{1,0:T(8,128)(2,1)S(1)} %get-tuple-element.82), channel_id=1, source_target_pairs={{0,24},{8,16},{16,8},{24,0},{1,25},{9,17},{17,9},{25,1},{2,26},{10... | collective-permute-start | bytes 393224 | tf_op jit(solution)/shard_map/ppermute | solution.py:25
  74.9 23.4 %collective-permute-start.21 = (bf16[128,2048]{1,0:T(8,128)(2,1)S(1)}, bf16[128,2048]{1,0:T(8,128)(2,1)S(1)}, u32[]{:S(2)}, u32[]{:S(2)}) collective-permute-start(bf16[128,2048]{1,0:T(8,128)(2,1)S(1)} %get-tuple-element.92.refs_0_), channel_id=1, source_target_pairs={{0,4},{1,5},{2,6},{3,7},{4,0},{5,1},{6,2},{7,3},{8,12},{9,13},{10,... | collective-permute-start | bytes 1572872 | tf_op jit(solution)/shard_map/ppermute | solution.py:25
  74.9 26.6 %collective-permute-start.20 = (bf16[128,2048]{1,0:T(8,128)(2,1)S(1)}, bf16[128,2048]{1,0:T(8,128)(2,1)S(1)}, u32[]{:S(2)}, u32[]{:S(2)}) collective-permute-start(bf16[128,2048]{1,0:T(8,128)(2,1)S(1)} %get-tuple-element.92.refs_0_), channel_id=1, source_target_pairs={{0,2},{1,3},{2,0},{3,1},{4,6},{5,7},{6,4},{7,5},{8,10},{9,11},{10,... | collective-permute-start | bytes 1572872 | tf_op jit(solution)/shard_map/ppermute | solution.py:25
  102.0 15.7 %collective-permute-start.25 = (bf16[128,2048]{1,0:T(8,128)(2,1)S(1)}, bf16[128,2048]{1,0:T(8,128)(2,1)S(1)}, u32[]{:S(2)}, u32[]{:S(2)}) collective-permute-start(bf16[128,2048]{1,0:T(8,128)(2,1)S(1)} %get-tuple-element.92.refs_0_), channel_id=1, source_target_pairs={{2,4},{3,5},{4,2},{5,3},{10,12},{11,13},{12,10},{13,11},{18,20},{1... | collective-permute-start | bytes 1572872 | tf_op jit(solution)/shard_map/ppermute | solution.py:333
  104.3 13.4 %collective-permute-start.24 = (bf16[128,2048]{1,0:T(8,128)(2,1)S(1)}, bf16[128,2048]{1,0:T(8,128)(2,1)S(1)}, u32[]{:S(2)}, u32[]{:S(2)}) collective-permute-start(bf16[128,2048]{1,0:T(8,128)(2,1)S(1)} %collective-permute-done.21.refs_2_), channel_id=1, source_target_pairs={{4,6},{5,7},{2,0},{3,1},{12,14},{13,15},{10,8},{11,9},{20,22},{21,... | collective-permute-start | bytes 1572872 | tf_op jit(solution)/shard_map/ppermute | solution.py:332
  123.7 24.3 %collective-permute-start.31 = (bf16[128,2048]{1,0:T(8,128)(2,1)S(1)}, bf16[128,2048]{1,0:T(8,128)(2,1)S(1)}, u32[]{:S(2)}, u32[]{:S(2)}) collective-permute-start(bf16[128,2048]{1,0:T(8,128)(2,1)S(1)} %add_convert_fusion.2), channel_id=1, source_target_pairs={{0,2},{1,3},{2,0},{3,1},{4,6},{5,7},{6,4},{7,5},{8,10},{9,11},{10,... | collective-permute-start | bytes 1572872 | tf_op jit(solution)/shard_map/ppermute | solution.py:25
  125.7 24.7 %collective-permute-start.33 = (bf16[128,2048]{1,0:T(8,128)(2,1)S(1)}, bf16[128,2048]{1,0:T(8,128)(2,1)S(1)}, u32[]{:S(2)}, u32[]{:S(2)}) collective-permute-start(bf16[128,2048]{1,0:T(8,128)(2,1)S(1)} %add_convert_fusion.1), channel_id=1, source_target_pairs={{0,4},{1,5},{2,6},{3,7},{4,0},{5,1},{6,2},{7,3},{8,12},{9,13},{10,... | collective-permute-start | bytes 1572872 | tf_op jit(solution)/shard_map/ppermute | solution.py:25
  126.8 24.0 %collective-permute-start.23 = (bf16[128,2048]{1,0:T(8,128)(2,1)S(1)}, bf16[128,2048]{1,0:T(8,128)(2,1)S(1)}, u32[]{:S(2)}, u32[]{:S(2)}) collective-permute-start(bf16[128,2048]{1,0:T(8,128)(2,1)S(1)} %get-tuple-element.90), channel_id=1, source_target_pairs={{0,1},{1,0},{2,3},{3,2},{4,5},{5,4},{6,7},{7,6},{8,9},{9,8},{10,11... | collective-permute-start | bytes 1572872 | tf_op jit(solution)/shard_map/ppermute | solution.py:25
  150.4 24.8 %collective-permute-start.34 = (bf16[128,2048]{1,0:T(8,128)(2,1)S(1)}, bf16[128,2048]{1,0:T(8,128)(2,1)S(1)}, u32[]{:S(2)}, u32[]{:S(2)}) collective-permute-start(bf16[128,2048]{1,0:T(8,128)(2,1)S(1)} %add_convert_fusion.3), channel_id=1, source_target_pairs={{0,6},{1,7},{2,4},{3,5},{4,2},{5,3},{6,0},{7,1},{8,14},{9,15},{10,... | collective-permute-start | bytes 1572872 | tf_op jit(solution)/shard_map/ppermute | solution.py:25
  (18 other events, 267.0 us)

commit v3 on v2

--- a/solution.py
+++ b/solution.py
@@ -17,6 +17,7 @@
 mask_fill_value = -1e30
 MIB = 1024 * 1024
 VMEM_EXPERTS = 14
+VMEM_EXPERTS_FIRST = 32
 VMEM_PREPARE = 58
 
 
@@ -225,7 +226,8 @@
     ins = refs[:sources]
     weights = refs[sources : sources + 3]
     outs = refs[sources + 3 : 2 * sources + 3]
-    refs = refs[2 * sources + 3 :]
+    refs[2 * sources + 3][0] = mark_ref[0]
+    refs = refs[2 * sources + 4 :]
     copies = [[] for _ in range(local_experts)]
     if load:
         held, refs, sems = refs[:3], refs[3:-1], refs[-1]
@@ -297,11 +299,15 @@
     held = [pltpu.VMEM(w.shape, w.dtype) for w in weights] if load else []
     outs = pl.pallas_call(
         functools.partial(experts_kernel, sources, local_experts, step, load),
-        out_shape=[jax.ShapeDtypeStruct((rows, width), jnp.bfloat16)] * sources + held,
+        out_shape=[jax.ShapeDtypeStruct((rows, width), jnp.bfloat16)] * sources
+        + [jax.ShapeDtypeStruct((1,), jnp.int32)]
+        + held,
         in_specs=[pl.BlockSpec(memory_space=pltpu.SMEM)]
         + [in_vmem] * (sources + 1)
         + [pl.BlockSpec(memory_space=pl.ANY) if load else in_vmem] * 3,
-        out_specs=[in_vmem] * (sources + len(held)),
+        out_specs=[in_vmem] * sources
+        + [pl.BlockSpec(memory_space=pltpu.SMEM)]
+        + [in_vmem] * len(held),
         scratch_shapes=[
             pltpu.VMEM((local_experts, slots, width), jnp.bfloat16),
             pltpu.VMEM((sources, local_experts * CAP, rows), jnp.bfloat16),
@@ -310,7 +316,7 @@
             pltpu.VMEM((sources, local_experts * CAP, width), jnp.bfloat16),
         ]
         + ([pltpu.SemaphoreType.DMA((local_experts, 3))] if load else []),
-        compiler_params=pltpu.CompilerParams(vmem_limit_bytes=VMEM_EXPERTS * MIB),
+        compiler_params=pltpu.CompilerParams(vmem_limit_bytes=(VMEM_EXPERTS_FIRST if load else VMEM_EXPERTS) * MIB),
         cost_estimate=pl.CostEstimate(
             flops=6 * local_experts * slots * width * hidden,
             bytes_accessed=2 * (3 * local_experts * width * hidden + 2 * sources * rows * width),
@@ -318,28 +324,39 @@
         ),
         name="experts_first" if load else "experts",
     )(mark, share, *tokens, *weights)
-    return list(outs[:sources]), list(outs[sources:]) if load else weights
-
-
-def send_near(own, chips):
-    return [swap(own, "exp", 2 * k) for k in range(1, 3 if chips == 4 else chips)]
-
-
-def send_far(own, near, chips, after):
+    return list(outs[:sources]), outs[sources], list(outs[sources + 1 :]) if load else weights
+
+
+def over_line(array, pairs):
+    return lax.ppermute(array, "exp", [(2 * a + c, 2 * b + c) for a, b in pairs for c in (0, 1)])
+
+
+def pick_kernel(mark_ref, relayed_ref, middle_ref, out_ref):
+    chip = lax.div(mark_ref[0], 2)
+    at_end = (chip == 0) | (chip == 3)
+
+    @pl.when(at_end)
+    def _():
+        out_ref[...] = relayed_ref[...]
+
+    @pl.when(jnp.logical_not(at_end))
+    def _():
+        out_ref[...] = middle_ref[...]
+
+
+def take_far(far, mark, chips):
     if chips != 4:
-        return near, after
-    two, own, after = lax.optimization_barrier((near[1], own, after))
-    relayed = lax.ppermute(two, "exp", [(4, 6), (5, 7), (2, 0), (3, 1)])
-    middle = lax.ppermute(own, "exp", [(2, 4), (3, 5), (4, 2), (5, 3)])
-    return [near[0], two, (relayed, middle)], after
-
-
-def take_far(arrays, chips, after):
-    far, after = lax.optimization_barrier((arrays[-1], after))
-    if chips == 4:
-        chip = lax.axis_index("exp") // 2
-        far = jnp.where((chip == 0) | (chip == 3), *far)
-    return far, after
+        return lax.optimization_barrier((far, mark))[0]
+    in_vmem = pl.BlockSpec(memory_space=pltpu.VMEM)
+    return pl.pallas_call(
+        pick_kernel,
+        out_shape=jax.ShapeDtypeStruct(far[0].shape, far[0].dtype),
+        in_specs=[pl.BlockSpec(memory_space=pltpu.SMEM)] + [in_vmem] * 2,
+        out_specs=in_vmem,
+        compiler_params=pltpu.CompilerParams(vmem_limit_bytes=4 * MIB),
+        cost_estimate=pl.CostEstimate(flops=0, bytes_accessed=6 * far[0].size, transcendentals=0),
+        name="pick_far",
+    )(mark, *far)
 
 
 def local(
@@ -380,11 +397,21 @@
         kv_heads,
         local_experts * exp_count,
     )
-    pack_chips = send_near(pack, chips)
     blocks_in = blocks_out[:1] + [swap(blocks_out[j], "ctx", j) for j in range(1, ctx_count)]
+    last = chips - 1
+    pack_chips = [swap(pack, "exp", 2 * k) for k in range(1, last)]
 
     att = attention_call(ctx_mark, blocks_in, heads, kv_heads)
-    pack_chips, att = send_far(pack, pack_chips, chips, att)
+    pack_mine, pack_chips[0], att = lax.optimization_barrier((pack, pack_chips[0], att))
+    if chips == 4:
+        two, pack_mine, att = lax.optimization_barrier((pack_chips[1], pack_mine, att))
+        pack_chips[1] = two
+        pack_far = (
+            over_line(two, [(2, 3), (1, 0)]),
+            over_line(pack_mine, [(1, 2), (2, 1)]),
+        )
+    else:
+        pack_far = swap(pack, "exp", 2 * last)
 
     def project(some):
         mine = projection_call(att, some, ctx_count)
@@ -393,42 +420,49 @@
     def with_pair(arrays):
         return [both for a in arrays for both in (a, swap(a, "exp", 1))]
 
-    last = chips - 1
-    packs = with_pair([pack, pack_chips[0]])
+    packs = with_pair([pack_mine, pack_chips[0]])
     parts = project(packs)
-    middle_packs = with_pair(pack_chips[1 : last - 1])
-    parts_middle = project(middle_packs)
-    pack_last, (parts, parts_middle[0]) = take_far(pack_chips, chips, (parts, parts_middle[0]))
-    packs_last = with_pair([pack_last])
+    packs_middle = with_pair(pack_chips[1:])
+    parts_middle = project(packs_middle)
+    pack_far, parts, parts_middle[0] = lax.optimization_barrier((pack_far, parts, parts_middle[0]))
+    packs_last = with_pair([take_far(pack_far, exp_mark, chips)])
     parts = parts + parts_middle + project(packs_last)
-    share = jnp.stack([p[out_weight.shape[0] :] for p in packs + middle_packs + packs_last])
+    share = jnp.stack([p[out_weight.shape[0] :] for p in packs + packs_middle + packs_last])
     parts[0], share = lax.optimization_barrier((parts[0], share))
     attn_resid, normed = norm_call(exp_mark, resid[0], norm_gain, parts, ctx_count, piece)
 
-    def experts(which, tokens, weights):
+    def experts(which, mark, tokens, weights):
         at = slice(2 * which.start, 2 * which.stop)
-        return experts_call(exp_mark, share[at], with_pair(tokens), weights, which.start == 0)
-
-    token_near = send_near(normed, chips)
-    partial, weights = experts(
-        slice(0, 1), [normed], [expert_gate, expert_up, expert_down]
+        return experts_call(mark, share[at], with_pair(tokens), weights, which.start == 0)
+
+    def pair_sum(both):
+        return both[0].astype(jnp.float32) + swap(both[1], "exp", 1).astype(jnp.float32)
+
+    near = [swap(normed, "exp", 2 * k) for k in range(1, last)]
+    partial, mark, weights = experts(
+        slice(0, 1), exp_mark, [normed], [expert_gate, expert_up, expert_down]
     )
-    token_chips, partial = send_far(normed, token_near, chips, partial)
-    token_chips[0], partial[0] = lax.optimization_barrier((token_chips[0], partial[0]))
-    more, _ = experts(slice(1, last), token_chips[: last - 1], weights)
-    partial = partial + more
-
-    def pair_sum(k):
-        return partial[2 * k].astype(jnp.float32) + swap(partial[2 * k + 1], "exp", 1).astype(
-            jnp.float32
+    if chips == 4:
+        near[1], normed, mark = lax.optimization_barrier((near[1], normed, mark))
+        far = (
+            over_line(near[1], [(2, 3), (1, 0)]),
+            over_line(normed, [(1, 2), (2, 1)]),
         )
-
-    layer_out = attn_resid.astype(jnp.float32) + pair_sum(0)
-    terms = [swap(pair_sum(k).astype(jnp.bfloat16), "exp", 2 * k) for k in range(1, last)]
-    token_last, more = take_far(token_chips, chips, more)
-    partial += experts(slice(last, chips), [token_last], weights)[0]
-    far, terms = lax.optimization_barrier((pair_sum(last).astype(jnp.bfloat16), terms))
-    final = swap(far, "exp", 2 * last)
+    else:
+        far = swap(normed, "exp", 2 * last)
+    layer_out = attn_resid.astype(jnp.float32) + pair_sum(partial)
+    partial, mark, _ = experts(slice(1, last), mark, near, weights)
+    sums = [pair_sum(partial[2 * k :]).astype(jnp.bfloat16) for k in range(last - 1)]
+    partial, _, _ = experts(slice(last, chips), mark, [take_far(far, mark, chips)], weights)
+    sum_far = pair_sum(partial).astype(jnp.bfloat16)
+    if chips == 4:
+        relayed = over_line(sum_far, [(3, 2), (0, 1)])
+        terms = [swap(sums[0], "exp", 2), over_line(sum_far, [(1, 2), (2, 1)])]
+        both = sums[1].astype(jnp.float32) + relayed.astype(jnp.float32)
+        final = swap(both.astype(jnp.bfloat16), "exp", 4)
+    else:
+        terms = [swap(p, "exp", 2 * k) for k, p in enumerate(sums, 1)]
+        final = swap(sum_far, "exp", 2 * last)
     for s in terms:
         layer_out = layer_out + s.astype(jnp.float32)
     layer_out = lax.optimization_barrier(layer_out) + final.astype(jnp.float32)

time: 176 us -> 170 us (0.966)
  the two profiles are of different devices: /device:TPU:16 before, /device:TPU:0 now
where the time goes in v3:
time: 170 us
  waiting for transfers between devices  91.1 us (54%)
  starting transfers between devices  38.5 us (23%)
  Pallas kernels  35.9 us (21%)
  other arithmetic  1.84 us (1%)
    ppermute x30, waiting for transfers between devices, swap(): return lax.ppermute(shard, axis, [(i, i ^ by) for i in range(devices)])  67.7 us
    ppermute x30, starting transfers between devices, swap(): return lax.ppermute(shard, axis, [(i, i ^ by) for i in range(devices)])  28.3 us
    ppermute x6, waiting for transfers between devices, over_line(): lax.ppermute(array, 'exp', [(2 * a + c, 2 * b + c) for a, b in pairs for...  23.4 us
    pallas_call x3, Pallas kernels, experts_call(): pl.pallas_call(functools.partial(experts_kernel, sources, local_experts,...  20.5 us
    ppermute x6, starting transfers between devices, over_line(): lax.ppermute(array, 'exp', [(2 * a + c, 2 * b + c) for a, b in pairs for...  10.3 us
    pallas_call x1, Pallas kernels, attention_call(): pl.pallas_call(functools.partial(attention_kernel, blocks, heads, kv_head...  6.84 us
    pallas_call x3, Pallas kernels, projection_call(): pl.pallas_call(functools.partial(projection_kernel, len(packs)), out_shap...  3.88 us
  transfers between devices with their start and end apart: 36, of which 20 were waited for; matrix products, arithmetic and copies ran while one was open for 1% of the time, Pallas kernels for 16%

profile of v3, /device:TPU:0, one launch (start us, length us, event | category | flops | bytes accessed | tf_op | source)
XLA Modules:
  0.0 169.7 jit_solution(1575887005677935164)
XLA Ops:
  0.6 2.3 %prepare.1 = (bf16[128,1280]{1,0:T(8,128)(2,1)S(1)}, bf16[128,1280]{1,0:T(8,128)(2,1)S(1)}, bf16[128,1280]{1,0:T(8,128)(2,1)S(1)}, bf16[128,1280]{1,0:T(8,128)(2,1)S(1)}, bf16[1040,256]{1,0:T(8,128)(2,1)S(1)}) custom-call(s32[1]{0:T(128)} %bitcast.3.marks_ref.me_ref, bf16[128,4096]{1,0:T(8,128)(2,1)} %bitcast.44, bf16[128,512]{1,0:T(8,128)(2,1)} %bitcast.46, ...), custom_call_target="tpu_custom_call" | custom-call | flops 65536 | bytes 3407872 | tf_op jit(solution)/shard_map/prepare/pallas_call | solution.py:81
  3.0 3.1 %collective-permute-start.1 = (bf16[1040,256]{1,0:T(8,128)(2,1)S(1)}, bf16[1040,256]{1,0:T(8,128)(2,1)S(1)}, u32[]{:S(2)}, u32[]{:S(2)}) collective-permute-start(bf16[1040,256]{1,0:T(8,128)(2,1)S(1)} %get-tuple-element.60.refs_0_), channel_id=1, source_target_pairs={{0,2},{1,3},{2,0},{3,1},{4,6},{5,7},{6,4},{7,5},{8,10},{9,11},{10,... | collective-permute-start | bytes 1597448 | tf_op jit(solution)/shard_map/ppermute | solution.py:26
  6.0 2.6 %collective-permute-start = (bf16[1040,256]{1,0:T(8,128)(2,1)S(1)}, bf16[1040,256]{1,0:T(8,128)(2,1)S(1)}, u32[]{:S(2)}, u32[]{:S(2)}) collective-permute-start(bf16[1040,256]{1,0:T(8,128)(2,1)S(1)} %get-tuple-element.60.refs_0_), channel_id=1, source_target_pairs={{0,4},{1,5},{2,6},{3,7},{4,0},{5,1},{6,2},{7,3},{8,12},{9,13},{10,... | collective-permute-start | bytes 1597448 | tf_op jit(solution)/shard_map/ppermute | solution.py:26
  12.1 7.2 %collective-permute-done.2.refs_1_ = bf16[128,1280]{1,0:T(8,128)(2,1)S(1)} collective-permute-done((bf16[128,1280]{1,0:T(8,128)(2,1)S(1)}, bf16[128,1280]{1,0:T(8,128)(2,1)S(1)}, u32[]{:S(2)}, u32[]{:S(2)}) %collective-permute-start.2) | collective-permute-done | bytes 327712 | tf_op jit(solution)/shard_map/ppermute | solution.py:26
  19.3 6.5 %collective-permute-done.3.refs_2_ = bf16[128,1280]{1,0:T(8,128)(2,1)S(1)} collective-permute-done((bf16[128,1280]{1,0:T(8,128)(2,1)S(1)}, bf16[128,1280]{1,0:T(8,128)(2,1)S(1)}, u32[]{:S(2)}, u32[]{:S(2)}) %collective-permute-start.3) | collective-permute-done | bytes 327712 | tf_op jit(solution)/shard_map/ppermute | solution.py:26
  25.8 6.8 %attention.1.att_ref = bf16[512,1024]{1,0:T(8,128)(2,1)S(1)} custom-call(s32[1]{0:T(128)} %bitcast.3.marks_ref.me_ref, bf16[128,1280]{1,0:T(8,128)(2,1)S(1)} %get-tuple-element.53.refs_0_, bf16[128,1280]{1,0:T(8,128)(2,1)S(1)} %collective-permute-done.2.refs_1_, bf16[128,1280]{1,0:T(8,128)(2,1)S(1)} %collective-permute-done.3.refs_2_, ...), custom_call_target="tpu_custom_call" | custom-call | flops 1073741824 | bytes 2621440 | tf_op jit(solution)/shard_map/attention/pallas_call | solution.py:136
  35.5 2.5 %projection.3 = (bf16[128,1024]{1,0:T(8,128)(2,1)S(1)}, bf16[128,1024]{1,0:T(8,128)(2,1)S(1)}, bf16[128,1024]{1,0:T(8,128)(2,1)S(1)}, bf16[128,1024]{1,0:T(8,128)(2,1)S(1)}) custom-call(bf16[512,1024]{1,0:T(8,128)(2,1)S(1)} %attention.1.att_ref, bf16[1040,256]{1,0:T(8,128)(2,1)S(1)} %get-tuple-element.60.refs_0_, ...), custom_call_target="tpu_custom_call" | custom-call | flops 1073741824 | bytes 4194304 | tf_op jit(solution)/shard_map/projection/pallas_call | solution.py:168
  43.7 6.2 %collective-permute-done.5.relayed_ref = bf16[1040,256]{1,0:T(8,128)(2,1)S(1)} collective-permute-done((bf16[1040,256]{1,0:T(8,128)(2,1)S(1)}, bf16[1040,256]{1,0:T(8,128)(2,1)S(1)}, u32[]{:S(2)}, u32[]{:S(2)}) %collective-permute-start.5) | collective-permute-done | bytes 532512 | tf_op jit(solution)/shard_map/ppermute | solution.py:331
  49.9 1.8 %collective-permute-done.10.refs_2_ = bf16[128,1024]{1,0:T(8,128)(2,1)S(1)} collective-permute-done((bf16[128,1024]{1,0:T(8,128)(2,1)S(1)}, bf16[128,1024]{1,0:T(8,128)(2,1)S(1)}, u32[]{:S(2)}, u32[]{:S(2)}) %collective-permute-start.10) | collective-permute-done | bytes 262176 | tf_op jit(solution)/shard_map/ppermute | solution.py:26
  54.3 1.5 collective-permute-start.15
  63.1 2.3 %collective-permute-done.17.refs_9_ = bf16[128,512]{1,0:T(8,128)(2,1)S(1)} collective-permute-done((bf16[128,512]{1,0:T(8,128)(2,1)S(1)}, bf16[128,512]{1,0:T(8,128)(2,1)S(1)}, u32[]{:S(2)}, u32[]{:S(2)}) %collective-permute-start.17) | collective-permute-done | bytes 131104 | tf_op jit(solution)/shard_map/ppermute | solution.py:26
  65.5 1.9 %collective-permute-done.18.refs_10_ = bf16[128,512]{1,0:T(8,128)(2,1)S(1)} collective-permute-done((bf16[128,512]{1,0:T(8,128)(2,1)S(1)}, bf16[128,512]{1,0:T(8,128)(2,1)S(1)}, u32[]{:S(2)}, u32[]{:S(2)}) %collective-permute-start.18) | collective-permute-done | bytes 131104 | tf_op jit(solution)/shard_map/ppermute | solution.py:26
  69.5 3.7 %collective-permute-start.22 = (bf16[128,2048]{1,0:T(8,128)(2,1)S(1)}, bf16[128,2048]{1,0:T(8,128)(2,1)S(1)}, u32[]{:S(2)}, u32[]{:S(2)}) collective-permute-start(bf16[128,2048]{1,0:T(8,128)(2,1)S(1)} %get-tuple-element.97.refs_0_), channel_id=1, source_target_pairs={{0,4},{1,5},{2,6},{3,7},{4,0},{5,1},{6,2},{7,3},{8,12},{9,13},{10,... | collective-permute-start | bytes 1572872 | tf_op jit(solution)/shard_map/ppermute | solution.py:26
  73.2 8.4 %experts_first.1 = (bf16[128,2048]{1,0:T(8,128)(2,1)S(1)}, bf16[128,2048]{1,0:T(8,128)(2,1)S(1)}, s32[1]{0:T(128)}, bf16[2,2048,768]{2,1,0:T(8,128)(2,1)S(1)}, b...) custom-call(s32[1]{0:T(128)} %bitcast.mark_ref.me_ref, ...), custom_call_target="tpu_custom_call" | custom-call | flops 2415919104 | bytes 20971520 | tf_op jit(solution)/shard_map/experts_first/pallas_call | solution.py:300
  81.6 15.5 %collective-permute-done.22.refs_2_ = bf16[128,2048]{1,0:T(8,128)(2,1)S(1)} collective-permute-done((bf16[128,2048]{1,0:T(8,128)(2,1)S(1)}, bf16[128,2048]{1,0:T(8,128)(2,1)S(1)}, u32[]{:S(2)}, u32[]{:S(2)}) %collective-permute-start.22) | collective-permute-done | bytes 524320 | tf_op jit(solution)/shard_map/ppermute | solution.py:26
  100.0 7.6 %experts.2 = (bf16[128,2048]{1,0:T(8,128)(2,1)S(1)}, bf16[128,2048]{1,0:T(8,128)(2,1)S(1)}, bf16[128,2048]{1,0:T(8,128)(2,1)S(1)}, bf16[128,2048]{1,0:T(8,128)(2,1)S(1)}, s32[1]{0:T(128)}) custom-call(s32[1]{0:T(128)} %get-tuple-element.89.mark_ref, bf16[4,16,256]{2,1,0:T(8,128)(2,1)S(1)} %slice.42.share_ref, ...), custom_call_target="tpu_custom_call" | custom-call | flops 4831838208 | bytes 23068672 | tf_op jit(solution)/shard_map/experts/pallas_call | solution.py:300
  107.6 5.9 %collective-permute-done.28.relayed_ref = bf16[128,2048]{1,0:T(8,128)(2,1)S(1)} collective-permute-done((bf16[128,2048]{1,0:T(8,128)(2,1)S(1)}, bf16[128,2048]{1,0:T(8,128)(2,1)S(1)}, u32[]{:S(2)}, u32[]{:S(2)}) %collective-permute-start.28) | collective-permute-done | bytes 524320 | tf_op jit(solution)/shard_map/ppermute | solution.py:331
  114.5 1.9 %collective-permute-done.30.refs_1_ = bf16[128,2048]{1,0:T(8,128)(2,1)S(1)} collective-permute-done((bf16[128,2048]{1,0:T(8,128)(2,1)S(1)}, bf16[128,2048]{1,0:T(8,128)(2,1)S(1)}, u32[]{:S(2)}, u32[]{:S(2)}) %collective-permute-start.30) | collective-permute-done | bytes 524320 | tf_op jit(solution)/shard_map/ppermute | solution.py:26
  116.4 4.4 %experts.3 = (bf16[128,2048]{1,0:T(8,128)(2,1)S(1)}, bf16[128,2048]{1,0:T(8,128)(2,1)S(1)}, s32[1]{0:T(128)}) custom-call(s32[1]{0:T(128)} %get-tuple-element.96.mark_ref, bf16[2,16,256]{2,1,0:T(8,128)(2,1)S(1)} %get-tuple-element.102.share_ref, bf16[128,2048]{1,0:T(8,128)(2,1)S(1)} %pick_far.3.refs_0_, ...), custom_call_target="tpu_custom_call" | custom-call | flops 2415919104 | bytes 20971520 | tf_op jit(solution)/shard_map/experts/pallas_call | solution.py:300
  123.0 5.6 %collective-permute-start.34 = (bf16[128,2048]{1,0:T(8,128)(2,1)S(1)}, bf16[128,2048]{1,0:T(8,128)(2,1)S(1)}, u32[]{:S(2)}, u32[]{:S(2)}) collective-permute-start(bf16[128,2048]{1,0:T(8,128)(2,1)S(1)} %add_convert_fusion.3), channel_id=1, source_target_pairs={{6,4},{7,5},{0,2},{1,3},{14,12},{15,13},{8,10},{9,11},{22,20},{23,... | collective-permute-start | bytes 1572872 | tf_op jit(solution)/shard_map/ppermute | solution.py:331
  129.6 11.2 %collective-permute-done.34 = bf16[128,2048]{1,0:T(8,128)(2,1)S(1)} collective-permute-done((bf16[128,2048]{1,0:T(8,128)(2,1)S(1)}, bf16[128,2048]{1,0:T(8,128)(2,1)S(1)}, u32[]{:S(2)}, u32[]{:S(2)}) %collective-permute-start.34) | collective-permute-done | bytes 524320 | tf_op jit(solution)/shard_map/ppermute | solution.py:331
  141.1 2.3 %collective-permute-start.35 = (bf16[128,2048]{1,0:T(8,128)(2,1)S(1)}, bf16[128,2048]{1,0:T(8,128)(2,1)S(1)}, u32[]{:S(2)}, u32[]{:S(2)}) collective-permute-start(bf16[128,2048]{1,0:T(8,128)(2,1)S(1)} %add_convert_fusion.1), channel_id=1, source_target_pairs={{0,4},{1,5},{2,6},{3,7},{4,0},{5,1},{6,2},{7,3},{8,12},{9,13},{10,... | collective-permute-start | bytes 1572872 | tf_op jit(solution)/shard_map/ppermute | solution.py:26
  143.4 8.7 %collective-permute-done.27 = bf16[128,2048]{1,0:T(8,128)(2,1)S(1)} collective-permute-done((bf16[128,2048]{1,0:T(8,128)(2,1)S(1)}, bf16[128,2048]{1,0:T(8,128)(2,1)S(1)}, u32[]{:S(2)}, u32[]{:S(2)}) %collective-permute-start.27) | collective-permute-done | bytes 524320 | tf_op jit(solution)/shard_map/ppermute | solution.py:26
  152.5 16.2 %collective-permute-done.35 = bf16[128,2048]{1,0:T(8,128)(2,1)S(1)} collective-permute-done((bf16[128,2048]{1,0:T(8,128)(2,1)S(1)}, bf16[128,2048]{1,0:T(8,128)(2,1)S(1)}, u32[]{:S(2)}, u32[]{:S(2)}) %collective-permute-start.35) | collective-permute-done | bytes 524320 | tf_op jit(solution)/shard_map/ppermute | solution.py:26
  (80 shorter events, 32.5 us)
Async XLA Ops:
  3.0 29.7 %collective-permute-start.1 = (bf16[1040,256]{1,0:T(8,128)(2,1)S(1)}, bf16[1040,256]{1,0:T(8,128)(2,1)S(1)}, u32[]{:S(2)}, u32[]{:S(2)}) collective-permute-start(bf16[1040,256]{1,0:T(8,128)(2,1)S(1)} %get-tuple-element.60.refs_0_), channel_id=1, source_target_pairs={{0,2},{1,3},{2,0},{3,1},{4,6},{5,7},{6,4},{7,5},{8,10},{9,11},{10,... | collective-permute-start | bytes 1597448 | tf_op jit(solution)/shard_map/ppermute | solution.py:26
  6.0 26.6 %collective-permute-start = (bf16[1040,256]{1,0:T(8,128)(2,1)S(1)}, bf16[1040,256]{1,0:T(8,128)(2,1)S(1)}, u32[]{:S(2)}, u32[]{:S(2)}) collective-permute-start(bf16[1040,256]{1,0:T(8,128)(2,1)S(1)} %get-tuple-element.60.refs_0_), channel_id=1, source_target_pairs={{0,4},{1,5},{2,6},{3,7},{4,0},{5,1},{6,2},{7,3},{8,12},{9,13},{10,... | collective-permute-start | bytes 1597448 | tf_op jit(solution)/shard_map/ppermute | solution.py:26
  8.6 10.7 %collective-permute-start.2 = (bf16[128,1280]{1,0:T(8,128)(2,1)S(1)}, bf16[128,1280]{1,0:T(8,128)(2,1)S(1)}, u32[]{:S(2)}, u32[]{:S(2)}) collective-permute-start(bf16[128,1280]{1,0:T(8,128)(2,1)S(1)} %get-tuple-element.54), channel_id=1, source_target_pairs={{0,8},{8,0},{16,24},{24,16},{1,9},{9,1},{17,25},{25,17},{2,10},{10... | collective-permute-start | bytes 983048 | tf_op jit(solution)/shard_map/ppermute | solution.py:26
  10.1 15.6 %collective-permute-start.3 = (bf16[128,1280]{1,0:T(8,128)(2,1)S(1)}, bf16[128,1280]{1,0:T(8,128)(2,1)S(1)}, u32[]{:S(2)}, u32[]{:S(2)}) collective-permute-start(bf16[128,1280]{1,0:T(8,128)(2,1)S(1)} %get-tuple-element.55), channel_id=1, source_target_pairs={{0,16},{8,24},{16,0},{24,8},{1,17},{9,25},{17,1},{25,9},{2,18},{10... | collective-permute-start | bytes 983048 | tf_op jit(solution)/shard_map/ppermute | solution.py:26
  11.6 14.1 %collective-permute-start.4 = (bf16[128,1280]{1,0:T(8,128)(2,1)S(1)}, bf16[128,1280]{1,0:T(8,128)(2,1)S(1)}, u32[]{:S(2)}, u32[]{:S(2)}) collective-permute-start(bf16[128,1280]{1,0:T(8,128)(2,1)S(1)} %get-tuple-element.56), channel_id=1, source_target_pairs={{0,24},{8,16},{16,8},{24,0},{1,25},{9,17},{17,9},{25,1},{2,26},{10... | collective-permute-start | bytes 983048 | tf_op jit(solution)/shard_map/ppermute | solution.py:26
  33.2 16.7 %collective-permute-start.6 = (bf16[1040,256]{1,0:T(8,128)(2,1)S(1)}, bf16[1040,256]{1,0:T(8,128)(2,1)S(1)}, u32[]{:S(2)}, u32[]{:S(2)}) collective-permute-start(bf16[1040,256]{1,0:T(8,128)(2,1)S(1)} %get-tuple-element.60.refs_0_), channel_id=1, source_target_pairs={{2,4},{3,5},{4,2},{5,3},{10,12},{11,13},{12,10},{13,11},{18,20},{1... | collective-permute-start | bytes 1597448 | tf_op jit(solution)/shard_map/ppermute | solution.py:331
  33.9 16.0 %collective-permute-start.5 = (bf16[1040,256]{1,0:T(8,128)(2,1)S(1)}, bf16[1040,256]{1,0:T(8,128)(2,1)S(1)}, u32[]{:S(2)}, u32[]{:S(2)}) collective-permute-start(bf16[1040,256]{1,0:T(8,128)(2,1)S(1)} %collective-permute-done.refs_0_), channel_id=1, source_target_pairs={{4,6},{5,7},{2,0},{3,1},{12,14},{13,15},{10,8},{11,9},{20,22},{21,... | collective-permute-start | bytes 1597448 | tf_op jit(solution)/shard_map/ppermute | solution.py:331
  38.0 11.9 %collective-permute-start.9 = (bf16[128,1024]{1,0:T(8,128)(2,1)S(1)}, bf16[128,1024]{1,0:T(8,128)(2,1)S(1)}, u32[]{:S(2)}, u32[]{:S(2)}) collective-permute-start(bf16[128,1024]{1,0:T(8,128)(2,1)S(1)} %get-tuple-element.64), channel_id=1, source_target_pairs={{0,8},{8,0},{16,24},{24,16},{1,9},{9,1},{17,25},{25,17},{2,10},{10... | collective-permute-start | bytes 786440 | tf_op jit(solution)/shard_map/ppermute | solution.py:26
  39.2 12.5 %collective-permute-start.10 = (bf16[128,1024]{1,0:T(8,128)(2,1)S(1)}, bf16[128,1024]{1,0:T(8,128)(2,1)S(1)}, u32[]{:S(2)}, u32[]{:S(2)}) collective-permute-start(bf16[128,1024]{1,0:T(8,128)(2,1)S(1)} %get-tuple-element.65), channel_id=1, source_target_pairs={{0,16},{8,24},{16,0},{24,8},{1,17},{9,25},{17,1},{25,9},{2,18},{10... | collective-permute-start | bytes 786440 | tf_op jit(solution)/shard_map/ppermute | solution.py:26
  41.0 12.1 %collective-permute-start.11 = (bf16[128,1024]{1,0:T(8,128)(2,1)S(1)}, bf16[128,1024]{1,0:T(8,128)(2,1)S(1)}, u32[]{:S(2)}, u32[]{:S(2)}) collective-permute-start(bf16[128,1024]{1,0:T(8,128)(2,1)S(1)} %get-tuple-element.66), channel_id=1, source_target_pairs={{0,24},{8,16},{16,8},{24,0},{1,25},{9,17},{17,9},{25,1},{2,26},{10... | collective-permute-start | bytes 786440 | tf_op jit(solution)/shard_map/ppermute | solution.py:26
  54.3 7.7 %collective-permute-start.15 = (bf16[128,512]{1,0:T(8,128)(2,1)S(1)}, bf16[128,512]{1,0:T(8,128)(2,1)S(1)}, u32[]{:S(2)}, u32[]{:S(2)}) collective-permute-start(bf16[128,512]{1,0:T(8,128)(2,1)S(1)} %get-tuple-element.77), channel_id=1, source_target_pairs={{0,16},{8,24},{16,0},{24,8},{1,17},{9,25},{17,1},{25,9},{2,18},{10... | collective-permute-start | bytes 393224 | tf_op jit(solution)/shard_map/ppermute | solution.py:26
  57.7 7.8 %collective-permute-start.17 = (bf16[128,512]{1,0:T(8,128)(2,1)S(1)}, bf16[128,512]{1,0:T(8,128)(2,1)S(1)}, u32[]{:S(2)}, u32[]{:S(2)}) collective-permute-start(bf16[128,512]{1,0:T(8,128)(2,1)S(1)} %get-tuple-element.80), channel_id=1, source_target_pairs={{0,8},{8,0},{16,24},{24,16},{1,9},{9,1},{17,25},{25,17},{2,10},{10... | collective-permute-start | bytes 393224 | tf_op jit(solution)/shard_map/ppermute | solution.py:26
  58.6 8.8 %collective-permute-start.18 = (bf16[128,512]{1,0:T(8,128)(2,1)S(1)}, bf16[128,512]{1,0:T(8,128)(2,1)S(1)}, u32[]{:S(2)}, u32[]{:S(2)}) collective-permute-start(bf16[128,512]{1,0:T(8,128)(2,1)S(1)} %get-tuple-element.81), channel_id=1, source_target_pairs={{0,16},{8,24},{16,0},{24,8},{1,17},{9,25},{17,1},{25,9},{2,18},{10... | collective-permute-start | bytes 393224 | tf_op jit(solution)/shard_map/ppermute | solution.py:26
  60.1 8.2 %collective-permute-start.19 = (bf16[128,512]{1,0:T(8,128)(2,1)S(1)}, bf16[128,512]{1,0:T(8,128)(2,1)S(1)}, u32[]{:S(2)}, u32[]{:S(2)}) collective-permute-start(bf16[128,512]{1,0:T(8,128)(2,1)S(1)} %get-tuple-element.82), channel_id=1, source_target_pairs={{0,24},{8,16},{16,8},{24,0},{1,25},{9,17},{17,9},{25,1},{2,26},{10... | collective-permute-start | bytes 393224 | tf_op jit(solution)/shard_map/ppermute | solution.py:26
  69.5 27.6 %collective-permute-start.22 = (bf16[128,2048]{1,0:T(8,128)(2,1)S(1)}, bf16[128,2048]{1,0:T(8,128)(2,1)S(1)}, u32[]{:S(2)}, u32[]{:S(2)}) collective-permute-start(bf16[128,2048]{1,0:T(8,128)(2,1)S(1)} %get-tuple-element.97.refs_0_), channel_id=1, source_target_pairs={{0,4},{1,5},{2,6},{3,7},{4,0},{5,1},{6,2},{7,3},{8,12},{9,13},{10,... | collective-permute-start | bytes 1572872 | tf_op jit(solution)/shard_map/ppermute | solution.py:26
  73.2 24.1 %collective-permute-start.23 = (bf16[128,2048]{1,0:T(8,128)(2,1)S(1)}, bf16[128,2048]{1,0:T(8,128)(2,1)S(1)}, u32[]{:S(2)}, u32[]{:S(2)}) collective-permute-start(bf16[128,2048]{1,0:T(8,128)(2,1)S(1)} %get-tuple-element.97.refs_0_), channel_id=1, source_target_pairs={{0,2},{1,3},{2,0},{3,1},{4,6},{5,7},{6,4},{7,5},{8,10},{9,11},{10,... | collective-permute-start | bytes 1572872 | tf_op jit(solution)/shard_map/ppermute | solution.py:26
  97.8 15.7 %collective-permute-start.28 = (bf16[128,2048]{1,0:T(8,128)(2,1)S(1)}, bf16[128,2048]{1,0:T(8,128)(2,1)S(1)}, u32[]{:S(2)}, u32[]{:S(2)}) collective-permute-start(bf16[128,2048]{1,0:T(8,128)(2,1)S(1)} %collective-permute-done.22.refs_2_), channel_id=1, source_target_pairs={{4,6},{5,7},{2,0},{3,1},{12,14},{13,15},{10,8},{11,9},{20,22},{21,... | collective-permute-start | bytes 1572872 | tf_op jit(solution)/shard_map/ppermute | solution.py:331
  99.1 14.4 %collective-permute-start.29 = (bf16[128,2048]{1,0:T(8,128)(2,1)S(1)}, bf16[128,2048]{1,0:T(8,128)(2,1)S(1)}, u32[]{:S(2)}, u32[]{:S(2)}) collective-permute-start(bf16[128,2048]{1,0:T(8,128)(2,1)S(1)} %get-tuple-element.97.refs_0_), channel_id=1, source_target_pairs={{2,4},{3,5},{4,2},{5,3},{10,12},{11,13},{12,10},{13,11},{18,20},{1... | collective-permute-start | bytes 1572872 | tf_op jit(solution)/shard_map/ppermute | solution.py:331
  121.4 8.2 %collective-permute-start.33 = (bf16[128,2048]{1,0:T(8,128)(2,1)S(1)}, bf16[128,2048]{1,0:T(8,128)(2,1)S(1)}, u32[]{:S(2)}, u32[]{:S(2)}) collective-permute-start(bf16[128,2048]{1,0:T(8,128)(2,1)S(1)} %get-tuple-element.101), channel_id=1, source_target_pairs={{0,1},{1,0},{2,3},{3,2},{4,5},{5,4},{6,7},{7,6},{8,9},{9,8},{10,11... | collective-permute-start | bytes 1572872 | tf_op jit(solution)/shard_map/ppermute | solution.py:26
  123.0 17.9 %collective-permute-start.34 = (bf16[128,2048]{1,0:T(8,128)(2,1)S(1)}, bf16[128,2048]{1,0:T(8,128)(2,1)S(1)}, u32[]{:S(2)}, u32[]{:S(2)}) collective-permute-start(bf16[128,2048]{1,0:T(8,128)(2,1)S(1)} %add_convert_fusion.3), channel_id=1, source_target_pairs={{6,4},{7,5},{0,2},{1,3},{14,12},{15,13},{8,10},{9,11},{22,20},{23,... | collective-permute-start | bytes 1572872 | tf_op jit(solution)/shard_map/ppermute | solution.py:331
  128.6 14.8 %collective-permute-start.21 = (bf16[128,2048]{1,0:T(8,128)(2,1)S(1)}, bf16[128,2048]{1,0:T(8,128)(2,1)S(1)}, u32[]{:S(2)}, u32[]{:S(2)}) collective-permute-start(bf16[128,2048]{1,0:T(8,128)(2,1)S(1)} %get-tuple-element.87), channel_id=1, source_target_pairs={{0,1},{1,0},{2,3},{3,2},{4,5},{5,4},{6,7},{7,6},{8,9},{9,8},{10,11... | collective-permute-start | bytes 1572872 | tf_op jit(solution)/shard_map/ppermute | solution.py:26
  128.8 23.2 %collective-permute-start.27 = (bf16[128,2048]{1,0:T(8,128)(2,1)S(1)}, bf16[128,2048]{1,0:T(8,128)(2,1)S(1)}, u32[]{:S(2)}, u32[]{:S(2)}) collective-permute-start(bf16[128,2048]{1,0:T(8,128)(2,1)S(1)} %add_convert_fusion.4), channel_id=1, source_target_pairs={{0,2},{1,3},{2,0},{3,1},{4,6},{5,7},{6,4},{7,5},{8,10},{9,11},{10,... | collective-permute-start | bytes 1572872 | tf_op jit(solution)/shard_map/ppermute | solution.py:26
  128.9 23.2 %collective-permute-start.32 = (bf16[128,2048]{1,0:T(8,128)(2,1)S(1)}, bf16[128,2048]{1,0:T(8,128)(2,1)S(1)}, u32[]{:S(2)}, u32[]{:S(2)}) collective-permute-start(bf16[128,2048]{1,0:T(8,128)(2,1)S(1)} %add_convert_fusion.3), channel_id=1, source_target_pairs={{2,4},{3,5},{4,2},{5,3},{10,12},{11,13},{12,10},{13,11},{18,20},{1... | collective-permute-start | bytes 1572872 | tf_op jit(solution)/shard_map/ppermute | solution.py:331
  141.1 27.7 %collective-permute-start.35 = (bf16[128,2048]{1,0:T(8,128)(2,1)S(1)}, bf16[128,2048]{1,0:T(8,128)(2,1)S(1)}, u32[]{:S(2)}, u32[]{:S(2)}) collective-permute-start(bf16[128,2048]{1,0:T(8,128)(2,1)S(1)} %add_convert_fusion.1), channel_id=1, source_target_pairs={{0,4},{1,5},{2,6},{3,7},{4,0},{5,1},{6,2},{7,3},{8,12},{9,13},{10,... | collective-permute-start | bytes 1572872 | tf_op jit(solution)/shard_map/ppermute | solution.py:26
  (15 other events, 170.1 us)

commit v4 on v3

--- a/solution.py
+++ b/solution.py
@@ -1,4 +1,5 @@
 import functools
+import math
 
 import jax
 import jax.numpy as jnp
@@ -97,36 +98,50 @@
     )(marks, q, k, v, w, ids.T, gates.T)
 
 
+STACK = 4
+
+
 def attention_kernel(blocks, heads, kv_heads, me_ref, *refs):
-    ins, out_ref, seq = refs[:blocks], refs[blocks], refs[blocks + 1]
+    ins, out_ref = refs[:blocks], refs[blocks]
+    query_rows, key_rows, value_rows = refs[blocks + 1 :]
     rows = ins[0].shape[0]
     me = me_ref[0]
     wide = heads * HEAD_SIZE
+    value_rows[:, :, HEAD_SIZE:] = jnp.ones(value_rows.shape[:2] + (HEAD_SIZE,), jnp.bfloat16)
     for j in range(blocks):
-        seq[pl.ds(pl.multiple_of((me ^ j) * rows, rows), rows), :] = ins[j][...]
+        at = pl.ds(pl.multiple_of((me ^ j) * rows, rows), rows)
+        for h in range(heads):
+            query_rows[h, at, :] = ins[j][:, h * HEAD_SIZE : (h + 1) * HEAD_SIZE]
+        for g in range(kv_heads):
+            key_at, value_at = wide + g * HEAD_SIZE, wide + (kv_heads + g) * HEAD_SIZE
+            key_rows[g, at, :] = ins[j][:, key_at : key_at + HEAD_SIZE]
+            value_rows[g, at, :HEAD_SIZE] = ins[j][:, value_at : value_at + HEAD_SIZE]
+    group = heads // kv_heads
+    stack = min(STACK, group)
     row = lax.broadcasted_iota(jnp.int32, (rows, rows), 0)
     col = lax.broadcasted_iota(jnp.int32, (rows, rows), 1)
-    allowed = row >= col
-    for h in range(heads):
-        g = h // (heads // kv_heads)
-        key_at = wide + g * HEAD_SIZE
-        value_at = wide + (kv_heads + g) * HEAD_SIZE
+    allowed = jnp.concatenate([row >= col] * stack, axis=0)
+    factor = HEAD_SIZE ** (-0.5) * math.log2(math.e)
+    for h in range(0, heads, stack):
+        g = h // group
         for i in range(blocks):
-            q = seq[i * rows : (i + 1) * rows, h * HEAD_SIZE : (h + 1) * HEAD_SIZE]
-            k = seq[: (i + 1) * rows, key_at : key_at + HEAD_SIZE]
-            v = seq[: (i + 1) * rows, value_at : value_at + HEAD_SIZE]
+            q = query_rows[h : h + stack, i * rows : (i + 1) * rows, :]
             s = lax.dot_general(
-                q, k, (((1,), (1,)), ((), ())), preferred_element_type=jnp.float32
-            ) * HEAD_SIZE ** (-0.5)
+                q.reshape(stack * rows, HEAD_SIZE),
+                key_rows[g, : (i + 1) * rows, :],
+                (((1,), (1,)), ((), ())),
+                preferred_element_type=jnp.float32,
+            )
             last = jnp.where(allowed, s[:, i * rows :], mask_fill_value)
             s = last if i == 0 else jnp.concatenate([s[:, : i * rows], last], axis=1)
-            p = jnp.exp(s - jnp.max(s, axis=1, keepdims=True))
-            total = jnp.sum(p, axis=1, keepdims=True)
-            o = dot(p.astype(jnp.bfloat16), v) / total
-            out_ref[
-                pl.ds(pl.multiple_of((me ^ i) * rows, rows), rows),
-                h * HEAD_SIZE : (h + 1) * HEAD_SIZE,
-            ] = o.astype(jnp.bfloat16)
+            p = jnp.exp2((s - jnp.max(s, axis=1, keepdims=True)) * factor)
+            o = dot(p.astype(jnp.bfloat16), value_rows[g, : (i + 1) * rows, :])
+            o = (o[:, :HEAD_SIZE] / o[:, HEAD_SIZE:]).astype(jnp.bfloat16)
+            at = pl.ds(pl.multiple_of((me ^ i) * rows, rows), rows)
+            for n in range(stack):
+                out_ref[at, (h + n) * HEAD_SIZE : (h + n + 1) * HEAD_SIZE] = o[
+                    n * rows : (n + 1) * rows
+                ]
 
 
 def attention_call(me, ins, heads, kv_heads):
@@ -139,8 +154,12 @@
         in_specs=[pl.BlockSpec(memory_space=pltpu.SMEM)]
         + [pl.BlockSpec(memory_space=pltpu.VMEM)] * blocks,
         out_specs=pl.BlockSpec(memory_space=pltpu.VMEM),
-        scratch_shapes=[pltpu.VMEM((length, wide_in), jnp.bfloat16)],
-        compiler_params=pltpu.CompilerParams(vmem_limit_bytes=12 * MIB),
+        scratch_shapes=[
+            pltpu.VMEM((heads, length, HEAD_SIZE), jnp.bfloat16),
+            pltpu.VMEM((kv_heads, length, HEAD_SIZE), jnp.bfloat16),
+            pltpu.VMEM((kv_heads, length, 2 * HEAD_SIZE), jnp.bfloat16),
+        ],
+        compiler_params=pltpu.CompilerParams(vmem_limit_bytes=24 * MIB),
         cost_estimate=pl.CostEstimate(
             flops=4 * length * length * wide,
             bytes_accessed=4 * length * wide_in,
@@ -406,10 +425,8 @@
     if chips == 4:
         two, pack_mine, att = lax.optimization_barrier((pack_chips[1], pack_mine, att))
         pack_chips[1] = two
-        pack_far = (
-            over_line(two, [(2, 3), (1, 0)]),
-            over_line(pack_mine, [(1, 2), (2, 1)]),
-        )
+        middle = over_line(pack_mine, [(1, 2), (2, 1)])
+        pack_far = (over_line(two, [(2, 3), (1, 0)]), middle)
     else:
         pack_far = swap(pack, "exp", 2 * last)
 

time: 170 us -> 170 us (level)
  Pallas kernels: 35.9 us -> 31.1 us
  waiting for transfers between devices: 91.1 us -> 95.7 us
    ppermute x30, waiting for transfers between devices: 67.7 us -> 72.5 us  [swap(): return lax.ppermute(shard, axis, [(i, i ^ by) for i in range(devices)])]
    pallas_call x1, Pallas kernels: 6.84 us -> 2.45 us  [attention_call(): pl.pallas_call(functools.partial(attention_kernel, blocks, heads, kv_head...]
  transfers between devices with their start and end apart: 36 -> 36, of which waited for: 20 -> 19; matrix products, arithmetic and copies ran while one was open for 1% -> 1% of each run, Pallas kernels for 16% -> 13%
where the time goes in v4:
time: 170 us; the launch traced here: 169 us
  waiting for transfers between devices  95.7 us (56%)
  starting transfers between devices  38.3 us (23%)
  Pallas kernels  31.1 us (18%)
  other arithmetic  1.84 us (1%)
    ppermute x30, waiting for transfers between devices, swap(): return lax.ppermute(shard, axis, [(i, i ^ by) for i in range(devices)])  72.5 us
    ppermute x30, starting transfers between devices, swap(): return lax.ppermute(shard, axis, [(i, i ^ by) for i in range(devices)])  27.9 us
    ppermute x6, waiting for transfers between devices, over_line(): lax.ppermute(array, 'exp', [(2 * a + c, 2 * b + c) for a, b in pairs for...  23.2 us
    pallas_call x3, Pallas kernels, experts_call(): pl.pallas_call(functools.partial(experts_kernel, sources, local_experts,...  20.5 us
    ppermute x6, starting transfers between devices, over_line(): lax.ppermute(array, 'exp', [(2 * a + c, 2 * b + c) for a, b in pairs for...  10.4 us
    pallas_call x3, Pallas kernels, projection_call(): pl.pallas_call(functools.partial(projection_kernel, len(packs)), out_shap...  3.88 us
  transfers between devices with their start and end apart: 36, of which 19 were waited for; matrix products, arithmetic and copies ran while one was open for 1% of the time, Pallas kernels for 13%

profile of v4, /device:TPU:0, one launch (start us, length us, event | category | flops | bytes accessed | tf_op | source)
XLA Modules:
  0.0 169.3 jit_solution(5139259764922923503)
XLA Ops:
  0.6 2.3 %prepare.1 = (bf16[128,1280]{1,0:T(8,128)(2,1)S(1)}, bf16[128,1280]{1,0:T(8,128)(2,1)S(1)}, bf16[128,1280]{1,0:T(8,128)(2,1)S(1)}, bf16[128,1280]{1,0:T(8,128)(2,1)S(1)}, bf16[1040,256]{1,0:T(8,128)(2,1)S(1)}) custom-call(s32[1]{0:T(128)} %bitcast.3.marks_ref.me_ref, bf16[128,4096]{1,0:T(8,128)(2,1)} %bitcast.44, bf16[128,512]{1,0:T(8,128)(2,1)} %bitcast.46, ...), custom_call_target="tpu_custom_call" | custom-call | flops 65536 | bytes 3407872 | tf_op jit(solution)/shard_map/prepare/pallas_call | solution.py:82
  3.0 3.1 %collective-permute-start.1 = (bf16[1040,256]{1,0:T(8,128)(2,1)S(1)}, bf16[1040,256]{1,0:T(8,128)(2,1)S(1)}, u32[]{:S(2)}, u32[]{:S(2)}) collective-permute-start(bf16[1040,256]{1,0:T(8,128)(2,1)S(1)} %get-tuple-element.60.refs_0_), channel_id=1, source_target_pairs={{0,2},{1,3},{2,0},{3,1},{4,6},{5,7},{6,4},{7,5},{8,10},{9,11},{10,... | collective-permute-start | bytes 1597448 | tf_op jit(solution)/shard_map/ppermute | solution.py:27
  6.0 2.6 %collective-permute-start = (bf16[1040,256]{1,0:T(8,128)(2,1)S(1)}, bf16[1040,256]{1,0:T(8,128)(2,1)S(1)}, u32[]{:S(2)}, u32[]{:S(2)}) collective-permute-start(bf16[1040,256]{1,0:T(8,128)(2,1)S(1)} %get-tuple-element.60.refs_0_), channel_id=1, source_target_pairs={{0,4},{1,5},{2,6},{3,7},{4,0},{5,1},{6,2},{7,3},{8,12},{9,13},{10,... | collective-permute-start | bytes 1597448 | tf_op jit(solution)/shard_map/ppermute | solution.py:27
  12.1 7.2 %collective-permute-done.2.refs_1_ = bf16[128,1280]{1,0:T(8,128)(2,1)S(1)} collective-permute-done((bf16[128,1280]{1,0:T(8,128)(2,1)S(1)}, bf16[128,1280]{1,0:T(8,128)(2,1)S(1)}, u32[]{:S(2)}, u32[]{:S(2)}) %collective-permute-start.2) | collective-permute-done | bytes 327712 | tf_op jit(solution)/shard_map/ppermute | solution.py:27
  19.3 6.5 %collective-permute-done.3.refs_2_ = bf16[128,1280]{1,0:T(8,128)(2,1)S(1)} collective-permute-done((bf16[128,1280]{1,0:T(8,128)(2,1)S(1)}, bf16[128,1280]{1,0:T(8,128)(2,1)S(1)}, u32[]{:S(2)}, u32[]{:S(2)}) %collective-permute-start.3) | collective-permute-done | bytes 327712 | tf_op jit(solution)/shard_map/ppermute | solution.py:27
  25.8 2.4 %attention.1.att_ref = bf16[512,1024]{1,0:T(8,128)(2,1)S(1)} custom-call(s32[1]{0:T(128)} %bitcast.3.marks_ref.me_ref, bf16[128,1280]{1,0:T(8,128)(2,1)S(1)} %get-tuple-element.53.refs_0_, bf16[128,1280]{1,0:T(8,128)(2,1)S(1)} %collective-permute-done.2.refs_1_, bf16[128,1280]{1,0:T(8,128)(2,1)S(1)} %collective-permute-done.3.refs_2_, ...), custom_call_target="tpu_custom_call" | custom-call | flops 1073741824 | bytes 2621440 | tf_op jit(solution)/shard_map/attention/pallas_call | solution.py:151
  29.4 2.5 %collective-permute-done.refs_0_ = bf16[1040,256]{1,0:T(8,128)(2,1)S(1)} collective-permute-done((bf16[1040,256]{1,0:T(8,128)(2,1)S(1)}, bf16[1040,256]{1,0:T(8,128)(2,1)S(1)}, u32[]{:S(2)}, u32[]{:S(2)}) %collective-permute-start) | collective-permute-done | bytes 532512 | tf_op jit(solution)/shard_map/ppermute | solution.py:27
  34.8 2.5 %projection.3 = (bf16[128,1024]{1,0:T(8,128)(2,1)S(1)}, bf16[128,1024]{1,0:T(8,128)(2,1)S(1)}, bf16[128,1024]{1,0:T(8,128)(2,1)S(1)}, bf16[128,1024]{1,0:T(8,128)(2,1)S(1)}) custom-call(bf16[512,1024]{1,0:T(8,128)(2,1)S(1)} %attention.1.att_ref, bf16[1040,256]{1,0:T(8,128)(2,1)S(1)} %get-tuple-element.60.refs_0_, ...), custom_call_target="tpu_custom_call" | custom-call | flops 1073741824 | bytes 4194304 | tf_op jit(solution)/shard_map/projection/pallas_call | solution.py:187
  42.9 6.1 %collective-permute-done.5.relayed_ref = bf16[1040,256]{1,0:T(8,128)(2,1)S(1)} collective-permute-done((bf16[1040,256]{1,0:T(8,128)(2,1)S(1)}, bf16[1040,256]{1,0:T(8,128)(2,1)S(1)}, u32[]{:S(2)}, u32[]{:S(2)}) %collective-permute-start.5) | collective-permute-done | bytes 532512 | tf_op jit(solution)/shard_map/ppermute | solution.py:350
  49.1 3.6 %collective-permute-done.10.refs_2_ = bf16[128,1024]{1,0:T(8,128)(2,1)S(1)} collective-permute-done((bf16[128,1024]{1,0:T(8,128)(2,1)S(1)}, bf16[128,1024]{1,0:T(8,128)(2,1)S(1)}, u32[]{:S(2)}, u32[]{:S(2)}) %collective-permute-start.10) | collective-permute-done | bytes 262176 | tf_op jit(solution)/shard_map/ppermute | solution.py:27
  60.6 2.3 %collective-permute-done.16.refs_7_ = bf16[128,512]{1,0:T(8,128)(2,1)S(1)} collective-permute-done((bf16[128,512]{1,0:T(8,128)(2,1)S(1)}, bf16[128,512]{1,0:T(8,128)(2,1)S(1)}, u32[]{:S(2)}, u32[]{:S(2)}) %collective-permute-start.16) | collective-permute-done | bytes 131104 | tf_op jit(solution)/shard_map/ppermute | solution.py:27
  65.7 2.4 %collective-permute-done.19.refs_11_ = bf16[128,512]{1,0:T(8,128)(2,1)S(1)} collective-permute-done((bf16[128,512]{1,0:T(8,128)(2,1)S(1)}, bf16[128,512]{1,0:T(8,128)(2,1)S(1)}, u32[]{:S(2)}, u32[]{:S(2)}) %collective-permute-start.19) | collective-permute-done | bytes 131104 | tf_op jit(solution)/shard_map/ppermute | solution.py:27
  69.3 3.7 %collective-permute-start.22 = (bf16[128,2048]{1,0:T(8,128)(2,1)S(1)}, bf16[128,2048]{1,0:T(8,128)(2,1)S(1)}, u32[]{:S(2)}, u32[]{:S(2)}) collective-permute-start(bf16[128,2048]{1,0:T(8,128)(2,1)S(1)} %get-tuple-element.97.refs_0_), channel_id=1, source_target_pairs={{0,4},{1,5},{2,6},{3,7},{4,0},{5,1},{6,2},{7,3},{8,12},{9,13},{10,... | collective-permute-start | bytes 1572872 | tf_op jit(solution)/shard_map/ppermute | solution.py:27
  73.0 8.4 %experts_first.1 = (bf16[128,2048]{1,0:T(8,128)(2,1)S(1)}, bf16[128,2048]{1,0:T(8,128)(2,1)S(1)}, s32[1]{0:T(128)}, bf16[2,2048,768]{2,1,0:T(8,128)(2,1)S(1)}, b...) custom-call(s32[1]{0:T(128)} %bitcast.mark_ref.me_ref, ...), custom_call_target="tpu_custom_call" | custom-call | flops 2415919104 | bytes 20971520 | tf_op jit(solution)/shard_map/experts_first/pallas_call | solution.py:319
  81.4 15.5 %collective-permute-done.22.refs_2_ = bf16[128,2048]{1,0:T(8,128)(2,1)S(1)} collective-permute-done((bf16[128,2048]{1,0:T(8,128)(2,1)S(1)}, bf16[128,2048]{1,0:T(8,128)(2,1)S(1)}, u32[]{:S(2)}, u32[]{:S(2)}) %collective-permute-start.22) | collective-permute-done | bytes 524320 | tf_op jit(solution)/shard_map/ppermute | solution.py:27
  99.9 7.6 %experts.2 = (bf16[128,2048]{1,0:T(8,128)(2,1)S(1)}, bf16[128,2048]{1,0:T(8,128)(2,1)S(1)}, bf16[128,2048]{1,0:T(8,128)(2,1)S(1)}, bf16[128,2048]{1,0:T(8,128)(2,1)S(1)}, s32[1]{0:T(128)}) custom-call(s32[1]{0:T(128)} %get-tuple-element.89.mark_ref, bf16[4,16,256]{2,1,0:T(8,128)(2,1)S(1)} %slice.42.share_ref, ...), custom_call_target="tpu_custom_call" | custom-call | flops 4831838208 | bytes 23068672 | tf_op jit(solution)/shard_map/experts/pallas_call | solution.py:319
  107.5 5.9 %collective-permute-done.28.relayed_ref = bf16[128,2048]{1,0:T(8,128)(2,1)S(1)} collective-permute-done((bf16[128,2048]{1,0:T(8,128)(2,1)S(1)}, bf16[128,2048]{1,0:T(8,128)(2,1)S(1)}, u32[]{:S(2)}, u32[]{:S(2)}) %collective-permute-start.28) | collective-permute-done | bytes 524320 | tf_op jit(solution)/shard_map/ppermute | solution.py:350
  114.1 1.9 %collective-permute-done.30.refs_1_ = bf16[128,2048]{1,0:T(8,128)(2,1)S(1)} collective-permute-done((bf16[128,2048]{1,0:T(8,128)(2,1)S(1)}, bf16[128,2048]{1,0:T(8,128)(2,1)S(1)}, u32[]{:S(2)}, u32[]{:S(2)}) %collective-permute-start.30) | collective-permute-done | bytes 524320 | tf_op jit(solution)/shard_map/ppermute | solution.py:27
  116.0 4.4 %experts.3 = (bf16[128,2048]{1,0:T(8,128)(2,1)S(1)}, bf16[128,2048]{1,0:T(8,128)(2,1)S(1)}, s32[1]{0:T(128)}) custom-call(s32[1]{0:T(128)} %get-tuple-element.96.mark_ref, bf16[2,16,256]{2,1,0:T(8,128)(2,1)S(1)} %get-tuple-element.102.share_ref, bf16[128,2048]{1,0:T(8,128)(2,1)S(1)} %pick_far.3.refs_0_, ...), custom_call_target="tpu_custom_call" | custom-call | flops 2415919104 | bytes 20971520 | tf_op jit(solution)/shard_map/experts/pallas_call | solution.py:319
  122.6 5.6 %collective-permute-start.34 = (bf16[128,2048]{1,0:T(8,128)(2,1)S(1)}, bf16[128,2048]{1,0:T(8,128)(2,1)S(1)}, u32[]{:S(2)}, u32[]{:S(2)}) collective-permute-start(bf16[128,2048]{1,0:T(8,128)(2,1)S(1)} %add_convert_fusion.3), channel_id=1, source_target_pairs={{6,4},{7,5},{0,2},{1,3},{14,12},{15,13},{8,10},{9,11},{22,20},{23,... | collective-permute-start | bytes 1572872 | tf_op jit(solution)/shard_map/ppermute | solution.py:350
  129.3 11.2 %collective-permute-done.34 = bf16[128,2048]{1,0:T(8,128)(2,1)S(1)} collective-permute-done((bf16[128,2048]{1,0:T(8,128)(2,1)S(1)}, bf16[128,2048]{1,0:T(8,128)(2,1)S(1)}, u32[]{:S(2)}, u32[]{:S(2)}) %collective-permute-start.34) | collective-permute-done | bytes 524320 | tf_op jit(solution)/shard_map/ppermute | solution.py:350
  140.7 2.3 %collective-permute-start.35 = (bf16[128,2048]{1,0:T(8,128)(2,1)S(1)}, bf16[128,2048]{1,0:T(8,128)(2,1)S(1)}, u32[]{:S(2)}, u32[]{:S(2)}) collective-permute-start(bf16[128,2048]{1,0:T(8,128)(2,1)S(1)} %add_convert_fusion.1), channel_id=1, source_target_pairs={{0,4},{1,5},{2,6},{3,7},{4,0},{5,1},{6,2},{7,3},{8,12},{9,13},{10,... | collective-permute-start | bytes 1572872 | tf_op jit(solution)/shard_map/ppermute | solution.py:27
  143.0 8.7 %collective-permute-done.27 = bf16[128,2048]{1,0:T(8,128)(2,1)S(1)} collective-permute-done((bf16[128,2048]{1,0:T(8,128)(2,1)S(1)}, bf16[128,2048]{1,0:T(8,128)(2,1)S(1)}, u32[]{:S(2)}, u32[]{:S(2)}) %collective-permute-start.27) | collective-permute-done | bytes 524320 | tf_op jit(solution)/shard_map/ppermute | solution.py:27
  152.1 16.2 %collective-permute-done.35 = bf16[128,2048]{1,0:T(8,128)(2,1)S(1)} collective-permute-done((bf16[128,2048]{1,0:T(8,128)(2,1)S(1)}, bf16[128,2048]{1,0:T(8,128)(2,1)S(1)}, u32[]{:S(2)}, u32[]{:S(2)}) %collective-permute-start.35) | collective-permute-done | bytes 524320 | tf_op jit(solution)/shard_map/ppermute | solution.py:27
  (80 shorter events, 33.4 us)
Async XLA Ops:
  3.0 26.5 %collective-permute-start.1 = (bf16[1040,256]{1,0:T(8,128)(2,1)S(1)}, bf16[1040,256]{1,0:T(8,128)(2,1)S(1)}, u32[]{:S(2)}, u32[]{:S(2)}) collective-permute-start(bf16[1040,256]{1,0:T(8,128)(2,1)S(1)} %get-tuple-element.60.refs_0_), channel_id=1, source_target_pairs={{0,2},{1,3},{2,0},{3,1},{4,6},{5,7},{6,4},{7,5},{8,10},{9,11},{10,... | collective-permute-start | bytes 1597448 | tf_op jit(solution)/shard_map/ppermute | solution.py:27
  6.0 25.9 %collective-permute-start = (bf16[1040,256]{1,0:T(8,128)(2,1)S(1)}, bf16[1040,256]{1,0:T(8,128)(2,1)S(1)}, u32[]{:S(2)}, u32[]{:S(2)}) collective-permute-start(bf16[1040,256]{1,0:T(8,128)(2,1)S(1)} %get-tuple-element.60.refs_0_), channel_id=1, source_target_pairs={{0,4},{1,5},{2,6},{3,7},{4,0},{5,1},{6,2},{7,3},{8,12},{9,13},{10,... | collective-permute-start | bytes 1597448 | tf_op jit(solution)/shard_map/ppermute | solution.py:27
  8.6 10.7 %collective-permute-start.2 = (bf16[128,1280]{1,0:T(8,128)(2,1)S(1)}, bf16[128,1280]{1,0:T(8,128)(2,1)S(1)}, u32[]{:S(2)}, u32[]{:S(2)}) collective-permute-start(bf16[128,1280]{1,0:T(8,128)(2,1)S(1)} %get-tuple-element.54), channel_id=1, source_target_pairs={{0,8},{8,0},{16,24},{24,16},{1,9},{9,1},{17,25},{25,17},{2,10},{10... | collective-permute-start | bytes 983048 | tf_op jit(solution)/shard_map/ppermute | solution.py:27
  10.1 15.6 %collective-permute-start.3 = (bf16[128,1280]{1,0:T(8,128)(2,1)S(1)}, bf16[128,1280]{1,0:T(8,128)(2,1)S(1)}, u32[]{:S(2)}, u32[]{:S(2)}) collective-permute-start(bf16[128,1280]{1,0:T(8,128)(2,1)S(1)} %get-tuple-element.55), channel_id=1, source_target_pairs={{0,16},{8,24},{16,0},{24,8},{1,17},{9,25},{17,1},{25,9},{2,18},{10... | collective-permute-start | bytes 983048 | tf_op jit(solution)/shard_map/ppermute | solution.py:27
  11.6 14.1 %collective-permute-start.4 = (bf16[128,1280]{1,0:T(8,128)(2,1)S(1)}, bf16[128,1280]{1,0:T(8,128)(2,1)S(1)}, u32[]{:S(2)}, u32[]{:S(2)}) collective-permute-start(bf16[128,1280]{1,0:T(8,128)(2,1)S(1)} %get-tuple-element.56), channel_id=1, source_target_pairs={{0,24},{8,16},{16,8},{24,0},{1,25},{9,17},{17,9},{25,1},{2,26},{10... | collective-permute-start | bytes 983048 | tf_op jit(solution)/shard_map/ppermute | solution.py:27
  32.5 16.6 %collective-permute-start.6 = (bf16[1040,256]{1,0:T(8,128)(2,1)S(1)}, bf16[1040,256]{1,0:T(8,128)(2,1)S(1)}, u32[]{:S(2)}, u32[]{:S(2)}) collective-permute-start(bf16[1040,256]{1,0:T(8,128)(2,1)S(1)} %get-tuple-element.60.refs_0_), channel_id=1, source_target_pairs={{2,4},{3,5},{4,2},{5,3},{10,12},{11,13},{12,10},{13,11},{18,20},{1... | collective-permute-start | bytes 1597448 | tf_op jit(solution)/shard_map/ppermute | solution.py:350
  33.2 15.9 %collective-permute-start.5 = (bf16[1040,256]{1,0:T(8,128)(2,1)S(1)}, bf16[1040,256]{1,0:T(8,128)(2,1)S(1)}, u32[]{:S(2)}, u32[]{:S(2)}) collective-permute-start(bf16[1040,256]{1,0:T(8,128)(2,1)S(1)} %collective-permute-done.refs_0_), channel_id=1, source_target_pairs={{4,6},{5,7},{2,0},{3,1},{12,14},{13,15},{10,8},{11,9},{20,22},{21,... | collective-permute-start | bytes 1597448 | tf_op jit(solution)/shard_map/ppermute | solution.py:350
  37.3 11.8 %collective-permute-start.9 = (bf16[128,1024]{1,0:T(8,128)(2,1)S(1)}, bf16[128,1024]{1,0:T(8,128)(2,1)S(1)}, u32[]{:S(2)}, u32[]{:S(2)}) collective-permute-start(bf16[128,1024]{1,0:T(8,128)(2,1)S(1)} %get-tuple-element.64), channel_id=1, source_target_pairs={{0,8},{8,0},{16,24},{24,16},{1,9},{9,1},{17,25},{25,17},{2,10},{10... | collective-permute-start | bytes 786440 | tf_op jit(solution)/shard_map/ppermute | solution.py:27
  38.8 13.8 %collective-permute-start.10 = (bf16[128,1024]{1,0:T(8,128)(2,1)S(1)}, bf16[128,1024]{1,0:T(8,128)(2,1)S(1)}, u32[]{:S(2)}, u32[]{:S(2)}) collective-permute-start(bf16[128,1024]{1,0:T(8,128)(2,1)S(1)} %get-tuple-element.65), channel_id=1, source_target_pairs={{0,16},{8,24},{16,0},{24,8},{1,17},{9,25},{17,1},{25,9},{2,18},{10... | collective-permute-start | bytes 786440 | tf_op jit(solution)/shard_map/ppermute | solution.py:27
  41.0 11.6 %collective-permute-start.11 = (bf16[128,1024]{1,0:T(8,128)(2,1)S(1)}, bf16[128,1024]{1,0:T(8,128)(2,1)S(1)}, u32[]{:S(2)}, u32[]{:S(2)}) collective-permute-start(bf16[128,1024]{1,0:T(8,128)(2,1)S(1)} %get-tuple-element.66), channel_id=1, source_target_pairs={{0,24},{8,16},{16,8},{24,0},{1,25},{9,17},{17,9},{25,1},{2,26},{10... | collective-permute-start | bytes 786440 | tf_op jit(solution)/shard_map/ppermute | solution.py:27
  54.9 8.0 %collective-permute-start.16 = (bf16[128,512]{1,0:T(8,128)(2,1)S(1)}, bf16[128,512]{1,0:T(8,128)(2,1)S(1)}, u32[]{:S(2)}, u32[]{:S(2)}) collective-permute-start(bf16[128,512]{1,0:T(8,128)(2,1)S(1)} %get-tuple-element.78), channel_id=1, source_target_pairs={{0,24},{8,16},{16,8},{24,0},{1,25},{9,17},{17,9},{25,1},{2,26},{10... | collective-permute-start | bytes 393224 | tf_op jit(solution)/shard_map/ppermute | solution.py:27
  57.1 7.7 %collective-permute-start.17 = (bf16[128,512]{1,0:T(8,128)(2,1)S(1)}, bf16[128,512]{1,0:T(8,128)(2,1)S(1)}, u32[]{:S(2)}, u32[]{:S(2)}) collective-permute-start(bf16[128,512]{1,0:T(8,128)(2,1)S(1)} %get-tuple-element.80), channel_id=1, source_target_pairs={{0,8},{8,0},{16,24},{24,16},{1,9},{9,1},{17,25},{25,17},{2,10},{10... | collective-permute-start | bytes 393224 | tf_op jit(solution)/shard_map/ppermute | solution.py:27
  59.2 8.9 %collective-permute-start.19 = (bf16[128,512]{1,0:T(8,128)(2,1)S(1)}, bf16[128,512]{1,0:T(8,128)(2,1)S(1)}, u32[]{:S(2)}, u32[]{:S(2)}) collective-permute-start(bf16[128,512]{1,0:T(8,128)(2,1)S(1)} %get-tuple-element.82), channel_id=1, source_target_pairs={{0,24},{8,16},{16,8},{24,0},{1,25},{9,17},{17,9},{25,1},{2,26},{10... | collective-permute-start | bytes 393224 | tf_op jit(solution)/shard_map/ppermute | solution.py:27
  69.3 27.6 %collective-permute-start.22 = (bf16[128,2048]{1,0:T(8,128)(2,1)S(1)}, bf16[128,2048]{1,0:T(8,128)(2,1)S(1)}, u32[]{:S(2)}, u32[]{:S(2)}) collective-permute-start(bf16[128,2048]{1,0:T(8,128)(2,1)S(1)} %get-tuple-element.97.refs_0_), channel_id=1, source_target_pairs={{0,4},{1,5},{2,6},{3,7},{4,0},{5,1},{6,2},{7,3},{8,12},{9,13},{10,... | collective-permute-start | bytes 1572872 | tf_op jit(solution)/shard_map/ppermute | solution.py:27
  73.0 24.1 %collective-permute-start.23 = (bf16[128,2048]{1,0:T(8,128)(2,1)S(1)}, bf16[128,2048]{1,0:T(8,128)(2,1)S(1)}, u32[]{:S(2)}, u32[]{:S(2)}) collective-permute-start(bf16[128,2048]{1,0:T(8,128)(2,1)S(1)} %get-tuple-element.97.refs_0_), channel_id=1, source_target_pairs={{0,2},{1,3},{2,0},{3,1},{4,6},{5,7},{6,4},{7,5},{8,10},{9,11},{10,... | collective-permute-start | bytes 1572872 | tf_op jit(solution)/shard_map/ppermute | solution.py:27
  97.6 15.7 %collective-permute-start.28 = (bf16[128,2048]{1,0:T(8,128)(2,1)S(1)}, bf16[128,2048]{1,0:T(8,128)(2,1)S(1)}, u32[]{:S(2)}, u32[]{:S(2)}) collective-permute-start(bf16[128,2048]{1,0:T(8,128)(2,1)S(1)} %collective-permute-done.22.refs_2_), channel_id=1, source_target_pairs={{4,6},{5,7},{2,0},{3,1},{12,14},{13,15},{10,8},{11,9},{20,22},{21,... | collective-permute-start | bytes 1572872 | tf_op jit(solution)/shard_map/ppermute | solution.py:350
  98.9 14.4 %collective-permute-start.29 = (bf16[128,2048]{1,0:T(8,128)(2,1)S(1)}, bf16[128,2048]{1,0:T(8,128)(2,1)S(1)}, u32[]{:S(2)}, u32[]{:S(2)}) collective-permute-start(bf16[128,2048]{1,0:T(8,128)(2,1)S(1)} %get-tuple-element.97.refs_0_), channel_id=1, source_target_pairs={{2,4},{3,5},{4,2},{5,3},{10,12},{11,13},{12,10},{13,11},{18,20},{1... | collective-permute-start | bytes 1572872 | tf_op jit(solution)/shard_map/ppermute | solution.py:350
  120.7 7.6 %collective-permute-start.26 = (bf16[128,2048]{1,0:T(8,128)(2,1)S(1)}, bf16[128,2048]{1,0:T(8,128)(2,1)S(1)}, u32[]{:S(2)}, u32[]{:S(2)}) collective-permute-start(bf16[128,2048]{1,0:T(8,128)(2,1)S(1)} %get-tuple-element.95), channel_id=1, source_target_pairs={{0,1},{1,0},{2,3},{3,2},{4,5},{5,4},{6,7},{7,6},{8,9},{9,8},{10,11... | collective-permute-start | bytes 1572872 | tf_op jit(solution)/shard_map/ppermute | solution.py:27
  121.1 8.2 %collective-permute-start.33 = (bf16[128,2048]{1,0:T(8,128)(2,1)S(1)}, bf16[128,2048]{1,0:T(8,128)(2,1)S(1)}, u32[]{:S(2)}, u32[]{:S(2)}) collective-permute-start(bf16[128,2048]{1,0:T(8,128)(2,1)S(1)} %get-tuple-element.101), channel_id=1, source_target_pairs={{0,1},{1,0},{2,3},{3,2},{4,5},{5,4},{6,7},{7,6},{8,9},{9,8},{10,11... | collective-permute-start | bytes 1572872 | tf_op jit(solution)/shard_map/ppermute | solution.py:27
  122.6 17.9 %collective-permute-start.34 = (bf16[128,2048]{1,0:T(8,128)(2,1)S(1)}, bf16[128,2048]{1,0:T(8,128)(2,1)S(1)}, u32[]{:S(2)}, u32[]{:S(2)}) collective-permute-start(bf16[128,2048]{1,0:T(8,128)(2,1)S(1)} %add_convert_fusion.3), channel_id=1, source_target_pairs={{6,4},{7,5},{0,2},{1,3},{14,12},{15,13},{8,10},{9,11},{22,20},{23,... | collective-permute-start | bytes 1572872 | tf_op jit(solution)/shard_map/ppermute | solution.py:350
  128.2 14.8 %collective-permute-start.21 = (bf16[128,2048]{1,0:T(8,128)(2,1)S(1)}, bf16[128,2048]{1,0:T(8,128)(2,1)S(1)}, u32[]{:S(2)}, u32[]{:S(2)}) collective-permute-start(bf16[128,2048]{1,0:T(8,128)(2,1)S(1)} %get-tuple-element.87), channel_id=1, source_target_pairs={{0,1},{1,0},{2,3},{3,2},{4,5},{5,4},{6,7},{7,6},{8,9},{9,8},{10,11... | collective-permute-start | bytes 1572872 | tf_op jit(solution)/shard_map/ppermute | solution.py:27
  128.5 23.2 %collective-permute-start.27 = (bf16[128,2048]{1,0:T(8,128)(2,1)S(1)}, bf16[128,2048]{1,0:T(8,128)(2,1)S(1)}, u32[]{:S(2)}, u32[]{:S(2)}) collective-permute-start(bf16[128,2048]{1,0:T(8,128)(2,1)S(1)} %add_convert_fusion.4), channel_id=1, source_target_pairs={{0,2},{1,3},{2,0},{3,1},{4,6},{5,7},{6,4},{7,5},{8,10},{9,11},{10,... | collective-permute-start | bytes 1572872 | tf_op jit(solution)/shard_map/ppermute | solution.py:27
  128.5 23.2 %collective-permute-start.32 = (bf16[128,2048]{1,0:T(8,128)(2,1)S(1)}, bf16[128,2048]{1,0:T(8,128)(2,1)S(1)}, u32[]{:S(2)}, u32[]{:S(2)}) collective-permute-start(bf16[128,2048]{1,0:T(8,128)(2,1)S(1)} %add_convert_fusion.3), channel_id=1, source_target_pairs={{2,4},{3,5},{4,2},{5,3},{10,12},{11,13},{12,10},{13,11},{18,20},{1... | collective-permute-start | bytes 1572872 | tf_op jit(solution)/shard_map/ppermute | solution.py:350
  140.7 27.7 %collective-permute-start.35 = (bf16[128,2048]{1,0:T(8,128)(2,1)S(1)}, bf16[128,2048]{1,0:T(8,128)(2,1)S(1)}, u32[]{:S(2)}, u32[]{:S(2)}) collective-permute-start(bf16[128,2048]{1,0:T(8,128)(2,1)S(1)} %add_convert_fusion.1), channel_id=1, source_target_pairs={{0,4},{1,5},{2,6},{3,7},{4,0},{5,1},{6,2},{7,3},{8,12},{9,13},{10,... | collective-permute-start | bytes 1572872 | tf_op jit(solution)/shard_map/ppermute | solution.py:27
  (15 other events, 169.3 us)

commit v5 on v4

--- a/solution.py
+++ b/solution.py
@@ -473,10 +473,15 @@
     partial, _, _ = experts(slice(last, chips), mark, [take_far(far, mark, chips)], weights)
     sum_far = pair_sum(partial).astype(jnp.bfloat16)
     if chips == 4:
+        def add(a, b):
+            return (a.astype(jnp.float32) + b.astype(jnp.float32)).astype(jnp.bfloat16)
+
         relayed = over_line(sum_far, [(3, 2), (0, 1)])
-        terms = [swap(sums[0], "exp", 2), over_line(sum_far, [(1, 2), (2, 1)])]
-        both = sums[1].astype(jnp.float32) + relayed.astype(jnp.float32)
-        final = swap(both.astype(jnp.bfloat16), "exp", 4)
+        early = over_line(sums[1], [(0, 1), (3, 2)])
+        middle = over_line(add(sum_far, early), [(1, 2), (2, 1)])
+        both, middle = lax.optimization_barrier((add(sums[1], relayed), middle))
+        terms = [swap(sums[0], "exp", 2), middle]
+        final = over_line(both, [(2, 0), (1, 3)])
     else:
         terms = [swap(p, "exp", 2 * k) for k, p in enumerate(sums, 1)]
         final = swap(sum_far, "exp", 2 * last)

time: 170 us -> 166 us (0.976)
  waiting for transfers between devices: 95.7 us -> 87.7 us
  starting transfers between devices: 38.3 us -> 42.6 us
    ppermute x30 -> x29, waiting for transfers between devices: 72.5 us -> 52.9 us  [swap(): return lax.ppermute(shard, axis, [(i, i ^ by) for i in range(devices)])]
    ppermute x6 -> x8, waiting for transfers between devices: 23.2 us -> 34.8 us  [over_line(): lax.ppermute(array, 'exp', [(2 * a + c, 2 * b + c) for a, b in pairs for...]
    ppermute x6 -> x8, starting transfers between devices: 10.4 us -> 16.2 us  [over_line(): lax.ppermute(array, 'exp', [(2 * a + c, 2 * b + c) for a, b in pairs for...]
    ppermute x30 -> x29, starting transfers between devices: 27.9 us -> 26.5 us  [swap(): return lax.ppermute(shard, axis, [(i, i ^ by) for i in range(devices)])]
  transfers between devices with their start and end apart: 36 -> 37, of which waited for: 19 -> 18; matrix products, arithmetic and copies ran while one was open for 1% -> 1% of each run, Pallas kernels for 13% -> 17%
where the time goes in v5:
time: 166 us
  waiting for transfers between devices  87.7 us (53%)
  starting transfers between devices  42.6 us (26%)
  Pallas kernels  31.1 us (19%)
  other arithmetic  2 us (1%)
    ppermute x29, waiting for transfers between devices, swap(): return lax.ppermute(shard, axis, [(i, i ^ by) for i in range(devices)])  52.9 us
    ppermute x8, waiting for transfers between devices, over_line(): lax.ppermute(array, 'exp', [(2 * a + c, 2 * b + c) for a, b in pairs for...  34.8 us
    ppermute x29, starting transfers between devices, swap(): return lax.ppermute(shard, axis, [(i, i ^ by) for i in range(devices)])  26.5 us
    pallas_call x3, Pallas kernels, experts_call(): pl.pallas_call(functools.partial(experts_kernel, sources, local_experts,...  20.5 us
    ppermute x8, starting transfers between devices, over_line(): lax.ppermute(array, 'exp', [(2 * a + c, 2 * b + c) for a, b in pairs for...  16.2 us
    pallas_call x3, Pallas kernels, projection_call(): pl.pallas_call(functools.partial(projection_kernel, len(packs)), out_shap...  3.88 us
  transfers between devices with their start and end apart: 37, of which 18 were waited for; matrix products, arithmetic and copies ran while one was open for 1% of the time, Pallas kernels for 17%

profile of v5, /device:TPU:0, one launch (start us, length us, event | category | flops | bytes accessed | tf_op | source)
XLA Modules:
  0.0 165.8 jit_solution(14665043994160488799)
XLA Ops:
  0.6 2.3 %prepare.1 = (bf16[128,1280]{1,0:T(8,128)(2,1)S(1)}, bf16[128,1280]{1,0:T(8,128)(2,1)S(1)}, bf16[128,1280]{1,0:T(8,128)(2,1)S(1)}, bf16[128,1280]{1,0:T(8,128)(2,1)S(1)}, bf16[1040,256]{1,0:T(8,128)(2,1)S(1)}) custom-call(s32[1]{0:T(128)} %bitcast.3.marks_ref.me_ref, bf16[128,4096]{1,0:T(8,128)(2,1)} %bitcast.44, bf16[128,512]{1,0:T(8,128)(2,1)} %bitcast.46, ...), custom_call_target="tpu_custom_call" | custom-call | flops 65536 | bytes 3407872 | tf_op jit(solution)/shard_map/prepare/pallas_call | solution.py:82
  3.0 3.1 %collective-permute-start.1 = (bf16[1040,256]{1,0:T(8,128)(2,1)S(1)}, bf16[1040,256]{1,0:T(8,128)(2,1)S(1)}, u32[]{:S(2)}, u32[]{:S(2)}) collective-permute-start(bf16[1040,256]{1,0:T(8,128)(2,1)S(1)} %get-tuple-element.62.refs_0_), channel_id=1, source_target_pairs={{0,2},{1,3},{2,0},{3,1},{4,6},{5,7},{6,4},{7,5},{8,10},{9,11},{10,... | collective-permute-start | bytes 1597448 | tf_op jit(solution)/shard_map/ppermute | solution.py:27
  6.0 2.6 %collective-permute-start = (bf16[1040,256]{1,0:T(8,128)(2,1)S(1)}, bf16[1040,256]{1,0:T(8,128)(2,1)S(1)}, u32[]{:S(2)}, u32[]{:S(2)}) collective-permute-start(bf16[1040,256]{1,0:T(8,128)(2,1)S(1)} %get-tuple-element.62.refs_0_), channel_id=1, source_target_pairs={{0,4},{1,5},{2,6},{3,7},{4,0},{5,1},{6,2},{7,3},{8,12},{9,13},{10,... | collective-permute-start | bytes 1597448 | tf_op jit(solution)/shard_map/ppermute | solution.py:27
  12.1 7.2 %collective-permute-done.2.refs_1_ = bf16[128,1280]{1,0:T(8,128)(2,1)S(1)} collective-permute-done((bf16[128,1280]{1,0:T(8,128)(2,1)S(1)}, bf16[128,1280]{1,0:T(8,128)(2,1)S(1)}, u32[]{:S(2)}, u32[]{:S(2)}) %collective-permute-start.2) | collective-permute-done | bytes 327712 | tf_op jit(solution)/shard_map/ppermute | solution.py:27
  19.3 6.5 %collective-permute-done.3.refs_2_ = bf16[128,1280]{1,0:T(8,128)(2,1)S(1)} collective-permute-done((bf16[128,1280]{1,0:T(8,128)(2,1)S(1)}, bf16[128,1280]{1,0:T(8,128)(2,1)S(1)}, u32[]{:S(2)}, u32[]{:S(2)}) %collective-permute-start.3) | collective-permute-done | bytes 327712 | tf_op jit(solution)/shard_map/ppermute | solution.py:27
  25.8 2.4 %attention.1.att_ref = bf16[512,1024]{1,0:T(8,128)(2,1)S(1)} custom-call(s32[1]{0:T(128)} %bitcast.3.marks_ref.me_ref, bf16[128,1280]{1,0:T(8,128)(2,1)S(1)} %get-tuple-element.55.refs_0_, bf16[128,1280]{1,0:T(8,128)(2,1)S(1)} %collective-permute-done.2.refs_1_, bf16[128,1280]{1,0:T(8,128)(2,1)S(1)} %collective-permute-done.3.refs_2_, ...), custom_call_target="tpu_custom_call" | custom-call | flops 1073741824 | bytes 2621440 | tf_op jit(solution)/shard_map/attention/pallas_call | solution.py:151
  29.4 2.5 %collective-permute-done.refs_0_ = bf16[1040,256]{1,0:T(8,128)(2,1)S(1)} collective-permute-done((bf16[1040,256]{1,0:T(8,128)(2,1)S(1)}, bf16[1040,256]{1,0:T(8,128)(2,1)S(1)}, u32[]{:S(2)}, u32[]{:S(2)}) %collective-permute-start) | collective-permute-done | bytes 532512 | tf_op jit(solution)/shard_map/ppermute | solution.py:27
  34.8 2.5 %projection.3 = (bf16[128,1024]{1,0:T(8,128)(2,1)S(1)}, bf16[128,1024]{1,0:T(8,128)(2,1)S(1)}, bf16[128,1024]{1,0:T(8,128)(2,1)S(1)}, bf16[128,1024]{1,0:T(8,128)(2,1)S(1)}) custom-call(bf16[512,1024]{1,0:T(8,128)(2,1)S(1)} %attention.1.att_ref, bf16[1040,256]{1,0:T(8,128)(2,1)S(1)} %get-tuple-element.62.refs_0_, ...), custom_call_target="tpu_custom_call" | custom-call | flops 1073741824 | bytes 4194304 | tf_op jit(solution)/shard_map/projection/pallas_call | solution.py:187
  42.9 6.1 %collective-permute-done.5.relayed_ref = bf16[1040,256]{1,0:T(8,128)(2,1)S(1)} collective-permute-done((bf16[1040,256]{1,0:T(8,128)(2,1)S(1)}, bf16[1040,256]{1,0:T(8,128)(2,1)S(1)}, u32[]{:S(2)}, u32[]{:S(2)}) %collective-permute-start.5) | collective-permute-done | bytes 532512 | tf_op jit(solution)/shard_map/ppermute | solution.py:350
  49.1 3.6 %collective-permute-done.10.refs_2_ = bf16[128,1024]{1,0:T(8,128)(2,1)S(1)} collective-permute-done((bf16[128,1024]{1,0:T(8,128)(2,1)S(1)}, bf16[128,1024]{1,0:T(8,128)(2,1)S(1)}, u32[]{:S(2)}, u32[]{:S(2)}) %collective-permute-start.10) | collective-permute-done | bytes 262176 | tf_op jit(solution)/shard_map/ppermute | solution.py:27
  60.6 2.3 %collective-permute-done.16.refs_7_ = bf16[128,512]{1,0:T(8,128)(2,1)S(1)} collective-permute-done((bf16[128,512]{1,0:T(8,128)(2,1)S(1)}, bf16[128,512]{1,0:T(8,128)(2,1)S(1)}, u32[]{:S(2)}, u32[]{:S(2)}) %collective-permute-start.16) | collective-permute-done | bytes 131104 | tf_op jit(solution)/shard_map/ppermute | solution.py:27
  65.7 2.4 %collective-permute-done.19.refs_11_ = bf16[128,512]{1,0:T(8,128)(2,1)S(1)} collective-permute-done((bf16[128,512]{1,0:T(8,128)(2,1)S(1)}, bf16[128,512]{1,0:T(8,128)(2,1)S(1)}, u32[]{:S(2)}, u32[]{:S(2)}) %collective-permute-start.19) | collective-permute-done | bytes 131104 | tf_op jit(solution)/shard_map/ppermute | solution.py:27
  69.3 3.7 %collective-permute-start.22 = (bf16[128,2048]{1,0:T(8,128)(2,1)S(1)}, bf16[128,2048]{1,0:T(8,128)(2,1)S(1)}, u32[]{:S(2)}, u32[]{:S(2)}) collective-permute-start(bf16[128,2048]{1,0:T(8,128)(2,1)S(1)} %get-tuple-element.101.refs_0_), channel_id=1, source_target_pairs={{0,4},{1,5},{2,6},{3,7},{4,0},{5,1},{6,2},{7,3},{8,12},{9,13},{10,... | collective-permute-start | bytes 1572872 | tf_op jit(solution)/shard_map/ppermute | solution.py:27
  73.0 8.4 %experts_first.1 = (bf16[128,2048]{1,0:T(8,128)(2,1)S(1)}, bf16[128,2048]{1,0:T(8,128)(2,1)S(1)}, s32[1]{0:T(128)}, bf16[2,2048,768]{2,1,0:T(8,128)(2,1)S(1)}, b...) custom-call(s32[1]{0:T(128)} %bitcast.mark_ref.me_ref, ...), custom_call_target="tpu_custom_call" | custom-call | flops 2415919104 | bytes 20971520 | tf_op jit(solution)/shard_map/experts_first/pallas_call | solution.py:319
  81.4 15.5 %collective-permute-done.22.refs_2_ = bf16[128,2048]{1,0:T(8,128)(2,1)S(1)} collective-permute-done((bf16[128,2048]{1,0:T(8,128)(2,1)S(1)}, bf16[128,2048]{1,0:T(8,128)(2,1)S(1)}, u32[]{:S(2)}, u32[]{:S(2)}) %collective-permute-start.22) | collective-permute-done | bytes 524320 | tf_op jit(solution)/shard_map/ppermute | solution.py:27
  99.8 7.7 %experts.2 = (bf16[128,2048]{1,0:T(8,128)(2,1)S(1)}, bf16[128,2048]{1,0:T(8,128)(2,1)S(1)}, bf16[128,2048]{1,0:T(8,128)(2,1)S(1)}, bf16[128,2048]{1,0:T(8,128)(2,1)S(1)}, s32[1]{0:T(128)}) custom-call(s32[1]{0:T(128)} %get-tuple-element.91.mark_ref, bf16[4,16,256]{2,1,0:T(8,128)(2,1)S(1)} %slice.42.share_ref, ...), custom_call_target="tpu_custom_call" | custom-call | flops 4831838208 | bytes 23068672 | tf_op jit(solution)/shard_map/experts/pallas_call | solution.py:319
  107.7 5.7 %collective-permute-done.29.relayed_ref = bf16[128,2048]{1,0:T(8,128)(2,1)S(1)} collective-permute-done((bf16[128,2048]{1,0:T(8,128)(2,1)S(1)}, bf16[128,2048]{1,0:T(8,128)(2,1)S(1)}, u32[]{:S(2)}, u32[]{:S(2)}) %collective-permute-start.29) | collective-permute-done | bytes 524320 | tf_op jit(solution)/shard_map/ppermute | solution.py:350
  114.3 5.6 %collective-permute-start.34 = (bf16[128,2048]{1,0:T(8,128)(2,1)S(1)}, bf16[128,2048]{1,0:T(8,128)(2,1)S(1)}, u32[]{:S(2)}, u32[]{:S(2)}) collective-permute-start(bf16[128,2048]{1,0:T(8,128)(2,1)S(1)} %add_convert_fusion.4), channel_id=1, source_target_pairs={{0,2},{1,3},{6,4},{7,5},{8,10},{9,11},{14,12},{15,13},{16,18},{17,... | collective-permute-start | bytes 1572872 | tf_op jit(solution)/shard_map/ppermute | solution.py:350
  119.9 4.4 %experts.3 = (bf16[128,2048]{1,0:T(8,128)(2,1)S(1)}, bf16[128,2048]{1,0:T(8,128)(2,1)S(1)}, s32[1]{0:T(128)}) custom-call(s32[1]{0:T(128)} %get-tuple-element.100.mark_ref, bf16[2,16,256]{2,1,0:T(8,128)(2,1)S(1)} %get-tuple-element.108.share_ref, bf16[128,2048]{1,0:T(8,128)(2,1)S(1)} %pick_far.3.refs_0_, ...), custom_call_target="tpu_custom_call" | custom-call | flops 2415919104 | bytes 20971520 | tf_op jit(solution)/shard_map/experts/pallas_call | solution.py:319
  125.0 6.7 %collective-permute-done.34 = bf16[128,2048]{1,0:T(8,128)(2,1)S(1)} collective-permute-done((bf16[128,2048]{1,0:T(8,128)(2,1)S(1)}, bf16[128,2048]{1,0:T(8,128)(2,1)S(1)}, u32[]{:S(2)}, u32[]{:S(2)}) %collective-permute-start.34) | collective-permute-done | bytes 524320 | tf_op jit(solution)/shard_map/ppermute | solution.py:350
  132.0 4.4 %collective-permute-start.33 = (bf16[128,2048]{1,0:T(8,128)(2,1)S(1)}, bf16[128,2048]{1,0:T(8,128)(2,1)S(1)}, u32[]{:S(2)}, u32[]{:S(2)}) collective-permute-start(bf16[128,2048]{1,0:T(8,128)(2,1)S(1)} %get-tuple-element.107), channel_id=1, source_target_pairs={{6,4},{7,5},{0,2},{1,3},{14,12},{15,13},{8,10},{9,11},{22,20},{23,... | collective-permute-start | bytes 1572872 | tf_op jit(solution)/shard_map/ppermute | solution.py:350
  138.3 10.4 %collective-permute-done.33 = bf16[128,2048]{1,0:T(8,128)(2,1)S(1)} collective-permute-done((bf16[128,2048]{1,0:T(8,128)(2,1)S(1)}, bf16[128,2048]{1,0:T(8,128)(2,1)S(1)}, u32[]{:S(2)}, u32[]{:S(2)}) %collective-permute-start.33) | collective-permute-done | bytes 524320 | tf_op jit(solution)/shard_map/ppermute | solution.py:350
  150.2 8.5 %collective-permute-done.27 = bf16[128,2048]{1,0:T(8,128)(2,1)S(1)} collective-permute-done((bf16[128,2048]{1,0:T(8,128)(2,1)S(1)}, bf16[128,2048]{1,0:T(8,128)(2,1)S(1)}, u32[]{:S(2)}, u32[]{:S(2)}) %collective-permute-start.27) | collective-permute-done | bytes 524320 | tf_op jit(solution)/shard_map/ppermute | solution.py:27
  159.1 5.8 %collective-permute-done.36 = bf16[128,2048]{1,0:T(8,128)(2,1)S(1)} collective-permute-done((bf16[128,2048]{1,0:T(8,128)(2,1)S(1)}, bf16[128,2048]{1,0:T(8,128)(2,1)S(1)}, u32[]{:S(2)}, u32[]{:S(2)}) %collective-permute-start.36) | collective-permute-done | bytes 524320 | tf_op jit(solution)/shard_map/ppermute | solution.py:350
  (83 shorter events, 34.5 us)
Async XLA Ops:
  3.0 26.5 %collective-permute-start.1 = (bf16[1040,256]{1,0:T(8,128)(2,1)S(1)}, bf16[1040,256]{1,0:T(8,128)(2,1)S(1)}, u32[]{:S(2)}, u32[]{:S(2)}) collective-permute-start(bf16[1040,256]{1,0:T(8,128)(2,1)S(1)} %get-tuple-element.62.refs_0_), channel_id=1, source_target_pairs={{0,2},{1,3},{2,0},{3,1},{4,6},{5,7},{6,4},{7,5},{8,10},{9,11},{10,... | collective-permute-start | bytes 1597448 | tf_op jit(solution)/shard_map/ppermute | solution.py:27
  6.0 25.9 %collective-permute-start = (bf16[1040,256]{1,0:T(8,128)(2,1)S(1)}, bf16[1040,256]{1,0:T(8,128)(2,1)S(1)}, u32[]{:S(2)}, u32[]{:S(2)}) collective-permute-start(bf16[1040,256]{1,0:T(8,128)(2,1)S(1)} %get-tuple-element.62.refs_0_), channel_id=1, source_target_pairs={{0,4},{1,5},{2,6},{3,7},{4,0},{5,1},{6,2},{7,3},{8,12},{9,13},{10,... | collective-permute-start | bytes 1597448 | tf_op jit(solution)/shard_map/ppermute | solution.py:27
  8.6 10.7 %collective-permute-start.2 = (bf16[128,1280]{1,0:T(8,128)(2,1)S(1)}, bf16[128,1280]{1,0:T(8,128)(2,1)S(1)}, u32[]{:S(2)}, u32[]{:S(2)}) collective-permute-start(bf16[128,1280]{1,0:T(8,128)(2,1)S(1)} %get-tuple-element.56), channel_id=1, source_target_pairs={{0,8},{8,0},{16,24},{24,16},{1,9},{9,1},{17,25},{25,17},{2,10},{10... | collective-permute-start | bytes 983048 | tf_op jit(solution)/shard_map/ppermute | solution.py:27
  10.1 15.6 %collective-permute-start.3 = (bf16[128,1280]{1,0:T(8,128)(2,1)S(1)}, bf16[128,1280]{1,0:T(8,128)(2,1)S(1)}, u32[]{:S(2)}, u32[]{:S(2)}) collective-permute-start(bf16[128,1280]{1,0:T(8,128)(2,1)S(1)} %get-tuple-element.57), channel_id=1, source_target_pairs={{0,16},{8,24},{16,0},{24,8},{1,17},{9,25},{17,1},{25,9},{2,18},{10... | collective-permute-start | bytes 983048 | tf_op jit(solution)/shard_map/ppermute | solution.py:27
  11.6 14.1 %collective-permute-start.4 = (bf16[128,1280]{1,0:T(8,128)(2,1)S(1)}, bf16[128,1280]{1,0:T(8,128)(2,1)S(1)}, u32[]{:S(2)}, u32[]{:S(2)}) collective-permute-start(bf16[128,1280]{1,0:T(8,128)(2,1)S(1)} %get-tuple-element.58), channel_id=1, source_target_pairs={{0,24},{8,16},{16,8},{24,0},{1,25},{9,17},{17,9},{25,1},{2,26},{10... | collective-permute-start | bytes 983048 | tf_op jit(solution)/shard_map/ppermute | solution.py:27
  32.5 16.6 %collective-permute-start.6 = (bf16[1040,256]{1,0:T(8,128)(2,1)S(1)}, bf16[1040,256]{1,0:T(8,128)(2,1)S(1)}, u32[]{:S(2)}, u32[]{:S(2)}) collective-permute-start(bf16[1040,256]{1,0:T(8,128)(2,1)S(1)} %get-tuple-element.62.refs_0_), channel_id=1, source_target_pairs={{2,4},{3,5},{4,2},{5,3},{10,12},{11,13},{12,10},{13,11},{18,20},{1... | collective-permute-start | bytes 1597448 | tf_op jit(solution)/shard_map/ppermute | solution.py:350
  33.2 15.9 %collective-permute-start.5 = (bf16[1040,256]{1,0:T(8,128)(2,1)S(1)}, bf16[1040,256]{1,0:T(8,128)(2,1)S(1)}, u32[]{:S(2)}, u32[]{:S(2)}) collective-permute-start(bf16[1040,256]{1,0:T(8,128)(2,1)S(1)} %collective-permute-done.refs_0_), channel_id=1, source_target_pairs={{4,6},{5,7},{2,0},{3,1},{12,14},{13,15},{10,8},{11,9},{20,22},{21,... | collective-permute-start | bytes 1597448 | tf_op jit(solution)/shard_map/ppermute | solution.py:350
  37.3 11.8 %collective-permute-start.9 = (bf16[128,1024]{1,0:T(8,128)(2,1)S(1)}, bf16[128,1024]{1,0:T(8,128)(2,1)S(1)}, u32[]{:S(2)}, u32[]{:S(2)}) collective-permute-start(bf16[128,1024]{1,0:T(8,128)(2,1)S(1)} %get-tuple-element.66), channel_id=1, source_target_pairs={{0,8},{8,0},{16,24},{24,16},{1,9},{9,1},{17,25},{25,17},{2,10},{10... | collective-permute-start | bytes 786440 | tf_op jit(solution)/shard_map/ppermute | solution.py:27
  38.8 13.8 %collective-permute-start.10 = (bf16[128,1024]{1,0:T(8,128)(2,1)S(1)}, bf16[128,1024]{1,0:T(8,128)(2,1)S(1)}, u32[]{:S(2)}, u32[]{:S(2)}) collective-permute-start(bf16[128,1024]{1,0:T(8,128)(2,1)S(1)} %get-tuple-element.67), channel_id=1, source_target_pairs={{0,16},{8,24},{16,0},{24,8},{1,17},{9,25},{17,1},{25,9},{2,18},{10... | collective-permute-start | bytes 786440 | tf_op jit(solution)/shard_map/ppermute | solution.py:27
  41.0 11.6 %collective-permute-start.11 = (bf16[128,1024]{1,0:T(8,128)(2,1)S(1)}, bf16[128,1024]{1,0:T(8,128)(2,1)S(1)}, u32[]{:S(2)}, u32[]{:S(2)}) collective-permute-start(bf16[128,1024]{1,0:T(8,128)(2,1)S(1)} %get-tuple-element.68), channel_id=1, source_target_pairs={{0,24},{8,16},{16,8},{24,0},{1,25},{9,17},{17,9},{25,1},{2,26},{10... | collective-permute-start | bytes 786440 | tf_op jit(solution)/shard_map/ppermute | solution.py:27
  54.9 8.0 %collective-permute-start.16 = (bf16[128,512]{1,0:T(8,128)(2,1)S(1)}, bf16[128,512]{1,0:T(8,128)(2,1)S(1)}, u32[]{:S(2)}, u32[]{:S(2)}) collective-permute-start(bf16[128,512]{1,0:T(8,128)(2,1)S(1)} %get-tuple-element.80), channel_id=1, source_target_pairs={{0,24},{8,16},{16,8},{24,0},{1,25},{9,17},{17,9},{25,1},{2,26},{10... | collective-permute-start | bytes 393224 | tf_op jit(solution)/shard_map/ppermute | solution.py:27
  57.1 7.7 %collective-permute-start.17 = (bf16[128,512]{1,0:T(8,128)(2,1)S(1)}, bf16[128,512]{1,0:T(8,128)(2,1)S(1)}, u32[]{:S(2)}, u32[]{:S(2)}) collective-permute-start(bf16[128,512]{1,0:T(8,128)(2,1)S(1)} %get-tuple-element.82), channel_id=1, source_target_pairs={{0,8},{8,0},{16,24},{24,16},{1,9},{9,1},{17,25},{25,17},{2,10},{10... | collective-permute-start | bytes 393224 | tf_op jit(solution)/shard_map/ppermute | solution.py:27
  59.2 8.9 %collective-permute-start.19 = (bf16[128,512]{1,0:T(8,128)(2,1)S(1)}, bf16[128,512]{1,0:T(8,128)(2,1)S(1)}, u32[]{:S(2)}, u32[]{:S(2)}) collective-permute-start(bf16[128,512]{1,0:T(8,128)(2,1)S(1)} %get-tuple-element.84), channel_id=1, source_target_pairs={{0,24},{8,16},{16,8},{24,0},{1,25},{9,17},{17,9},{25,1},{2,26},{10... | collective-permute-start | bytes 393224 | tf_op jit(solution)/shard_map/ppermute | solution.py:27
  69.3 27.6 %collective-permute-start.22 = (bf16[128,2048]{1,0:T(8,128)(2,1)S(1)}, bf16[128,2048]{1,0:T(8,128)(2,1)S(1)}, u32[]{:S(2)}, u32[]{:S(2)}) collective-permute-start(bf16[128,2048]{1,0:T(8,128)(2,1)S(1)} %get-tuple-element.101.refs_0_), channel_id=1, source_target_pairs={{0,4},{1,5},{2,6},{3,7},{4,0},{5,1},{6,2},{7,3},{8,12},{9,13},{10,... | collective-permute-start | bytes 1572872 | tf_op jit(solution)/shard_map/ppermute | solution.py:27
  73.0 24.1 %collective-permute-start.23 = (bf16[128,2048]{1,0:T(8,128)(2,1)S(1)}, bf16[128,2048]{1,0:T(8,128)(2,1)S(1)}, u32[]{:S(2)}, u32[]{:S(2)}) collective-permute-start(bf16[128,2048]{1,0:T(8,128)(2,1)S(1)} %get-tuple-element.101.refs_0_), channel_id=1, source_target_pairs={{0,2},{1,3},{2,0},{3,1},{4,6},{5,7},{6,4},{7,5},{8,10},{9,11},{10,... | collective-permute-start | bytes 1572872 | tf_op jit(solution)/shard_map/ppermute | solution.py:27
  97.7 15.7 %collective-permute-start.29 = (bf16[128,2048]{1,0:T(8,128)(2,1)S(1)}, bf16[128,2048]{1,0:T(8,128)(2,1)S(1)}, u32[]{:S(2)}, u32[]{:S(2)}) collective-permute-start(bf16[128,2048]{1,0:T(8,128)(2,1)S(1)} %collective-permute-done.22.refs_2_), channel_id=1, source_target_pairs={{4,6},{5,7},{2,0},{3,1},{12,14},{13,15},{10,8},{11,9},{20,22},{21,... | collective-permute-start | bytes 1572872 | tf_op jit(solution)/shard_map/ppermute | solution.py:350
  98.9 14.4 %collective-permute-start.30 = (bf16[128,2048]{1,0:T(8,128)(2,1)S(1)}, bf16[128,2048]{1,0:T(8,128)(2,1)S(1)}, u32[]{:S(2)}, u32[]{:S(2)}) collective-permute-start(bf16[128,2048]{1,0:T(8,128)(2,1)S(1)} %get-tuple-element.101.refs_0_), channel_id=1, source_target_pairs={{2,4},{3,5},{4,2},{5,3},{10,12},{11,13},{12,10},{13,11},{18,20},{1... | collective-permute-start | bytes 1572872 | tf_op jit(solution)/shard_map/ppermute | solution.py:350
  114.3 17.4 %collective-permute-start.34 = (bf16[128,2048]{1,0:T(8,128)(2,1)S(1)}, bf16[128,2048]{1,0:T(8,128)(2,1)S(1)}, u32[]{:S(2)}, u32[]{:S(2)}) collective-permute-start(bf16[128,2048]{1,0:T(8,128)(2,1)S(1)} %add_convert_fusion.4), channel_id=1, source_target_pairs={{0,2},{1,3},{6,4},{7,5},{8,10},{9,11},{14,12},{15,13},{16,18},{17,... | collective-permute-start | bytes 1572872 | tf_op jit(solution)/shard_map/ppermute | solution.py:350
  124.7 12.5 %collective-permute-start.26 = (bf16[128,2048]{1,0:T(8,128)(2,1)S(1)}, bf16[128,2048]{1,0:T(8,128)(2,1)S(1)}, u32[]{:S(2)}, u32[]{:S(2)}) collective-permute-start(bf16[128,2048]{1,0:T(8,128)(2,1)S(1)} %get-tuple-element.97), channel_id=1, source_target_pairs={{0,1},{1,0},{2,3},{3,2},{4,5},{5,4},{6,7},{7,6},{8,9},{9,8},{10,11... | collective-permute-start | bytes 1572872 | tf_op jit(solution)/shard_map/ppermute | solution.py:27
  132.0 16.7 %collective-permute-start.33 = (bf16[128,2048]{1,0:T(8,128)(2,1)S(1)}, bf16[128,2048]{1,0:T(8,128)(2,1)S(1)}, u32[]{:S(2)}, u32[]{:S(2)}) collective-permute-start(bf16[128,2048]{1,0:T(8,128)(2,1)S(1)} %get-tuple-element.107), channel_id=1, source_target_pairs={{6,4},{7,5},{0,2},{1,3},{14,12},{15,13},{8,10},{9,11},{22,20},{23,... | collective-permute-start | bytes 1572872 | tf_op jit(solution)/shard_map/ppermute | solution.py:350
  136.4 13.7 %collective-permute-start.21 = (bf16[128,2048]{1,0:T(8,128)(2,1)S(1)}, bf16[128,2048]{1,0:T(8,128)(2,1)S(1)}, u32[]{:S(2)}, u32[]{:S(2)}) collective-permute-start(bf16[128,2048]{1,0:T(8,128)(2,1)S(1)} %get-tuple-element.89), channel_id=1, source_target_pairs={{0,1},{1,0},{2,3},{3,2},{4,5},{5,4},{6,7},{7,6},{8,9},{9,8},{10,11... | collective-permute-start | bytes 1572872 | tf_op jit(solution)/shard_map/ppermute | solution.py:27
  136.5 12.4 %collective-permute-start.35 = (bf16[128,2048]{1,0:T(8,128)(2,1)S(1)}, bf16[128,2048]{1,0:T(8,128)(2,1)S(1)}, u32[]{:S(2)}, u32[]{:S(2)}) collective-permute-start(bf16[128,2048]{1,0:T(8,128)(2,1)S(1)} %get-tuple-element.106), channel_id=1, source_target_pairs={{2,4},{3,5},{4,2},{5,3},{10,12},{11,13},{12,10},{13,11},{18,20},{1... | collective-permute-start | bytes 1572872 | tf_op jit(solution)/shard_map/ppermute | solution.py:350
  137.3 21.3 %collective-permute-start.27 = (bf16[128,2048]{1,0:T(8,128)(2,1)S(1)}, bf16[128,2048]{1,0:T(8,128)(2,1)S(1)}, u32[]{:S(2)}, u32[]{:S(2)}) collective-permute-start(bf16[128,2048]{1,0:T(8,128)(2,1)S(1)} %add_convert_fusion.5), channel_id=1, source_target_pairs={{0,2},{1,3},{2,0},{3,1},{4,6},{5,7},{6,4},{7,5},{8,10},{9,11},{10,... | collective-permute-start | bytes 1572872 | tf_op jit(solution)/shard_map/ppermute | solution.py:27
  148.9 16.0 %collective-permute-start.36 = (bf16[128,2048]{1,0:T(8,128)(2,1)S(1)}, bf16[128,2048]{1,0:T(8,128)(2,1)S(1)}, u32[]{:S(2)}, u32[]{:S(2)}) collective-permute-start(bf16[128,2048]{1,0:T(8,128)(2,1)S(1)} %add_convert_fusion.2), channel_id=1, source_target_pairs={{4,0},{5,1},{2,6},{3,7},{12,8},{13,9},{10,14},{11,15},{20,16},{21,... | collective-permute-start | bytes 1572872 | tf_op jit(solution)/shard_map/ppermute | solution.py:350
  (16 other events, 188.2 us)

commit v6 on v5

--- a/solution.py
+++ b/solution.py
@@ -477,7 +477,7 @@
             return (a.astype(jnp.float32) + b.astype(jnp.float32)).astype(jnp.bfloat16)
 
         relayed = over_line(sum_far, [(3, 2), (0, 1)])
-        early = over_line(sums[1], [(0, 1), (3, 2)])
+        early = swap(sums[1], "exp", 2)
         middle = over_line(add(sum_far, early), [(1, 2), (2, 1)])
         both, middle = lax.optimization_barrier((add(sums[1], relayed), middle))
         terms = [swap(sums[0], "exp", 2), middle]

time: 166 us -> 164 us (0.988)
  starting transfers between devices: 42.6 us -> 40 us
    ppermute x29 -> x30, waiting for transfers between devices: 52.9 us -> 60.4 us  [swap(): return lax.ppermute(shard, axis, [(i, i ^ by) for i in range(devices)])]
    ppermute x8 -> x7, waiting for transfers between devices: 34.8 us -> 28 us  [over_line(): lax.ppermute(array, 'exp', [(2 * a + c, 2 * b + c) for a, b in pairs for...]
    ppermute x8 -> x7, starting transfers between devices: 16.2 us -> 9.79 us  [over_line(): lax.ppermute(array, 'exp', [(2 * a + c, 2 * b + c) for a, b in pairs for...]
    ppermute x29 -> x30, starting transfers between devices: 26.5 us -> 30.2 us  [swap(): return lax.ppermute(shard, axis, [(i, i ^ by) for i in range(devices)])]
  transfers between devices with their start and end apart: 37 -> 37, of which waited for: 18 -> 18; matrix products, arithmetic and copies ran while one was open for 1% -> 2% of each run, Pallas kernels for 17% -> 17%
where the time goes in v6:
time: 164 us
  waiting for transfers between devices  88.5 us (54%)
  starting transfers between devices  40 us (24%)
  Pallas kernels  31.1 us (19%)
  other arithmetic  2 us (1%)
    ppermute x30, waiting for transfers between devices, swap(): return lax.ppermute(shard, axis, [(i, i ^ by) for i in range(devices)])  60.4 us
    ppermute x30, starting transfers between devices, swap(): return lax.ppermute(shard, axis, [(i, i ^ by) for i in range(devices)])  30.2 us
    ppermute x7, waiting for transfers between devices, over_line(): lax.ppermute(array, 'exp', [(2 * a + c, 2 * b + c) for a, b in pairs for...  28 us
    pallas_call x3, Pallas kernels, experts_call(): pl.pallas_call(functools.partial(experts_kernel, sources, local_experts,...  20.5 us
    ppermute x7, starting transfers between devices, over_line(): lax.ppermute(array, 'exp', [(2 * a + c, 2 * b + c) for a, b in pairs for...  9.79 us
    pallas_call x3, Pallas kernels, projection_call(): pl.pallas_call(functools.partial(projection_kernel, len(packs)), out_shap...  3.88 us
  transfers between devices with their start and end apart: 37, of which 18 were waited for; matrix products, arithmetic and copies ran while one was open for 2% of the time, Pallas kernels for 17%

profile of v6, /device:TPU:0, one launch (start us, length us, event | category | flops | bytes accessed | tf_op | source)
XLA Modules:
  0.0 163.9 jit_solution(5626600059652325070)
XLA Ops:
  0.6 2.3 %prepare.1 = (bf16[128,1280]{1,0:T(8,128)(2,1)S(1)}, bf16[128,1280]{1,0:T(8,128)(2,1)S(1)}, bf16[128,1280]{1,0:T(8,128)(2,1)S(1)}, bf16[128,1280]{1,0:T(8,128)(2,1)S(1)}, bf16[1040,256]{1,0:T(8,128)(2,1)S(1)}) custom-call(s32[1]{0:T(128)} %bitcast.3.marks_ref.me_ref, bf16[128,4096]{1,0:T(8,128)(2,1)} %bitcast.44, bf16[128,512]{1,0:T(8,128)(2,1)} %bitcast.46, ...), custom_call_target="tpu_custom_call" | custom-call | flops 65536 | bytes 3407872 | tf_op jit(solution)/shard_map/prepare/pallas_call | solution.py:82
  3.0 3.1 %collective-permute-start.1 = (bf16[1040,256]{1,0:T(8,128)(2,1)S(1)}, bf16[1040,256]{1,0:T(8,128)(2,1)S(1)}, u32[]{:S(2)}, u32[]{:S(2)}) collective-permute-start(bf16[1040,256]{1,0:T(8,128)(2,1)S(1)} %get-tuple-element.62.refs_0_), channel_id=1, source_target_pairs={{0,2},{1,3},{2,0},{3,1},{4,6},{5,7},{6,4},{7,5},{8,10},{9,11},{10,... | collective-permute-start | bytes 1597448 | tf_op jit(solution)/shard_map/ppermute | solution.py:27
  6.0 2.6 %collective-permute-start = (bf16[1040,256]{1,0:T(8,128)(2,1)S(1)}, bf16[1040,256]{1,0:T(8,128)(2,1)S(1)}, u32[]{:S(2)}, u32[]{:S(2)}) collective-permute-start(bf16[1040,256]{1,0:T(8,128)(2,1)S(1)} %get-tuple-element.62.refs_0_), channel_id=1, source_target_pairs={{0,4},{1,5},{2,6},{3,7},{4,0},{5,1},{6,2},{7,3},{8,12},{9,13},{10,... | collective-permute-start | bytes 1597448 | tf_op jit(solution)/shard_map/ppermute | solution.py:27
  12.1 7.2 %collective-permute-done.2.refs_1_ = bf16[128,1280]{1,0:T(8,128)(2,1)S(1)} collective-permute-done((bf16[128,1280]{1,0:T(8,128)(2,1)S(1)}, bf16[128,1280]{1,0:T(8,128)(2,1)S(1)}, u32[]{:S(2)}, u32[]{:S(2)}) %collective-permute-start.2) | collective-permute-done | bytes 327712 | tf_op jit(solution)/shard_map/ppermute | solution.py:27
  19.3 6.5 %collective-permute-done.3.refs_2_ = bf16[128,1280]{1,0:T(8,128)(2,1)S(1)} collective-permute-done((bf16[128,1280]{1,0:T(8,128)(2,1)S(1)}, bf16[128,1280]{1,0:T(8,128)(2,1)S(1)}, u32[]{:S(2)}, u32[]{:S(2)}) %collective-permute-start.3) | collective-permute-done | bytes 327712 | tf_op jit(solution)/shard_map/ppermute | solution.py:27
  25.8 2.4 %attention.1.att_ref = bf16[512,1024]{1,0:T(8,128)(2,1)S(1)} custom-call(s32[1]{0:T(128)} %bitcast.3.marks_ref.me_ref, bf16[128,1280]{1,0:T(8,128)(2,1)S(1)} %get-tuple-element.55.refs_0_, bf16[128,1280]{1,0:T(8,128)(2,1)S(1)} %collective-permute-done.2.refs_1_, bf16[128,1280]{1,0:T(8,128)(2,1)S(1)} %collective-permute-done.3.refs_2_, ...), custom_call_target="tpu_custom_call" | custom-call | flops 1073741824 | bytes 2621440 | tf_op jit(solution)/shard_map/attention/pallas_call | solution.py:151
  29.4 2.5 %collective-permute-done.refs_0_ = bf16[1040,256]{1,0:T(8,128)(2,1)S(1)} collective-permute-done((bf16[1040,256]{1,0:T(8,128)(2,1)S(1)}, bf16[1040,256]{1,0:T(8,128)(2,1)S(1)}, u32[]{:S(2)}, u32[]{:S(2)}) %collective-permute-start) | collective-permute-done | bytes 532512 | tf_op jit(solution)/shard_map/ppermute | solution.py:27
  34.8 2.5 %projection.3 = (bf16[128,1024]{1,0:T(8,128)(2,1)S(1)}, bf16[128,1024]{1,0:T(8,128)(2,1)S(1)}, bf16[128,1024]{1,0:T(8,128)(2,1)S(1)}, bf16[128,1024]{1,0:T(8,128)(2,1)S(1)}) custom-call(bf16[512,1024]{1,0:T(8,128)(2,1)S(1)} %attention.1.att_ref, bf16[1040,256]{1,0:T(8,128)(2,1)S(1)} %get-tuple-element.62.refs_0_, ...), custom_call_target="tpu_custom_call" | custom-call | flops 1073741824 | bytes 4194304 | tf_op jit(solution)/shard_map/projection/pallas_call | solution.py:187
  42.9 6.1 %collective-permute-done.5.relayed_ref = bf16[1040,256]{1,0:T(8,128)(2,1)S(1)} collective-permute-done((bf16[1040,256]{1,0:T(8,128)(2,1)S(1)}, bf16[1040,256]{1,0:T(8,128)(2,1)S(1)}, u32[]{:S(2)}, u32[]{:S(2)}) %collective-permute-start.5) | collective-permute-done | bytes 532512 | tf_op jit(solution)/shard_map/ppermute | solution.py:350
  49.1 3.6 %collective-permute-done.10.refs_2_ = bf16[128,1024]{1,0:T(8,128)(2,1)S(1)} collective-permute-done((bf16[128,1024]{1,0:T(8,128)(2,1)S(1)}, bf16[128,1024]{1,0:T(8,128)(2,1)S(1)}, u32[]{:S(2)}, u32[]{:S(2)}) %collective-permute-start.10) | collective-permute-done | bytes 262176 | tf_op jit(solution)/shard_map/ppermute | solution.py:27
  60.6 2.3 %collective-permute-done.16.refs_7_ = bf16[128,512]{1,0:T(8,128)(2,1)S(1)} collective-permute-done((bf16[128,512]{1,0:T(8,128)(2,1)S(1)}, bf16[128,512]{1,0:T(8,128)(2,1)S(1)}, u32[]{:S(2)}, u32[]{:S(2)}) %collective-permute-start.16) | collective-permute-done | bytes 131104 | tf_op jit(solution)/shard_map/ppermute | solution.py:27
  65.7 2.4 %collective-permute-done.19.refs_11_ = bf16[128,512]{1,0:T(8,128)(2,1)S(1)} collective-permute-done((bf16[128,512]{1,0:T(8,128)(2,1)S(1)}, bf16[128,512]{1,0:T(8,128)(2,1)S(1)}, u32[]{:S(2)}, u32[]{:S(2)}) %collective-permute-start.19) | collective-permute-done | bytes 131104 | tf_op jit(solution)/shard_map/ppermute | solution.py:27
  69.3 3.7 %collective-permute-start.22 = (bf16[128,2048]{1,0:T(8,128)(2,1)S(1)}, bf16[128,2048]{1,0:T(8,128)(2,1)S(1)}, u32[]{:S(2)}, u32[]{:S(2)}) collective-permute-start(bf16[128,2048]{1,0:T(8,128)(2,1)S(1)} %get-tuple-element.101.refs_0_), channel_id=1, source_target_pairs={{0,4},{1,5},{2,6},{3,7},{4,0},{5,1},{6,2},{7,3},{8,12},{9,13},{10,... | collective-permute-start | bytes 1572872 | tf_op jit(solution)/shard_map/ppermute | solution.py:27
  73.0 8.4 %experts_first.1 = (bf16[128,2048]{1,0:T(8,128)(2,1)S(1)}, bf16[128,2048]{1,0:T(8,128)(2,1)S(1)}, s32[1]{0:T(128)}, bf16[2,2048,768]{2,1,0:T(8,128)(2,1)S(1)}, b...) custom-call(s32[1]{0:T(128)} %bitcast.mark_ref.me_ref, ...), custom_call_target="tpu_custom_call" | custom-call | flops 2415919104 | bytes 20971520 | tf_op jit(solution)/shard_map/experts_first/pallas_call | solution.py:319
  81.4 15.5 %collective-permute-done.22.refs_2_ = bf16[128,2048]{1,0:T(8,128)(2,1)S(1)} collective-permute-done((bf16[128,2048]{1,0:T(8,128)(2,1)S(1)}, bf16[128,2048]{1,0:T(8,128)(2,1)S(1)}, u32[]{:S(2)}, u32[]{:S(2)}) %collective-permute-start.22) | collective-permute-done | bytes 524320 | tf_op jit(solution)/shard_map/ppermute | solution.py:27
  99.8 7.7 %experts.2 = (bf16[128,2048]{1,0:T(8,128)(2,1)S(1)}, bf16[128,2048]{1,0:T(8,128)(2,1)S(1)}, bf16[128,2048]{1,0:T(8,128)(2,1)S(1)}, bf16[128,2048]{1,0:T(8,128)(2,1)S(1)}, s32[1]{0:T(128)}) custom-call(s32[1]{0:T(128)} %get-tuple-element.91.mark_ref, bf16[4,16,256]{2,1,0:T(8,128)(2,1)S(1)} %slice.42.share_ref, ...), custom_call_target="tpu_custom_call" | custom-call | flops 4831838208 | bytes 23068672 | tf_op jit(solution)/shard_map/experts/pallas_call | solution.py:319
  107.7 5.7 %collective-permute-done.29.relayed_ref = bf16[128,2048]{1,0:T(8,128)(2,1)S(1)} collective-permute-done((bf16[128,2048]{1,0:T(8,128)(2,1)S(1)}, bf16[128,2048]{1,0:T(8,128)(2,1)S(1)}, u32[]{:S(2)}, u32[]{:S(2)}) %collective-permute-start.29) | collective-permute-done | bytes 524320 | tf_op jit(solution)/shard_map/ppermute | solution.py:350
  114.3 3.8 %collective-permute-start.34 = (bf16[128,2048]{1,0:T(8,128)(2,1)S(1)}, bf16[128,2048]{1,0:T(8,128)(2,1)S(1)}, u32[]{:S(2)}, u32[]{:S(2)}) collective-permute-start(bf16[128,2048]{1,0:T(8,128)(2,1)S(1)} %add_convert_fusion.4), channel_id=1, source_target_pairs={{0,2},{1,3},{2,0},{3,1},{4,6},{5,7},{6,4},{7,5},{8,10},{9,11},{10,... | collective-permute-start | bytes 1572872 | tf_op jit(solution)/shard_map/ppermute | solution.py:27
  118.0 4.5 %experts.3 = (bf16[128,2048]{1,0:T(8,128)(2,1)S(1)}, bf16[128,2048]{1,0:T(8,128)(2,1)S(1)}, s32[1]{0:T(128)}) custom-call(s32[1]{0:T(128)} %get-tuple-element.100.mark_ref, bf16[2,16,256]{2,1,0:T(8,128)(2,1)S(1)} %get-tuple-element.108.share_ref, bf16[128,2048]{1,0:T(8,128)(2,1)S(1)} %pick_far.3.refs_0_, ...), custom_call_target="tpu_custom_call" | custom-call | flops 2415919104 | bytes 20971520 | tf_op jit(solution)/shard_map/experts/pallas_call | solution.py:319
  123.1 7.5 %collective-permute-done.34 = bf16[128,2048]{1,0:T(8,128)(2,1)S(1)} collective-permute-done((bf16[128,2048]{1,0:T(8,128)(2,1)S(1)}, bf16[128,2048]{1,0:T(8,128)(2,1)S(1)}, u32[]{:S(2)}, u32[]{:S(2)}) %collective-permute-start.34) | collective-permute-done | bytes 524320 | tf_op jit(solution)/shard_map/ppermute | solution.py:27
  130.9 3.7 %collective-permute-start.33 = (bf16[128,2048]{1,0:T(8,128)(2,1)S(1)}, bf16[128,2048]{1,0:T(8,128)(2,1)S(1)}, u32[]{:S(2)}, u32[]{:S(2)}) collective-permute-start(bf16[128,2048]{1,0:T(8,128)(2,1)S(1)} %get-tuple-element.107), channel_id=1, source_target_pairs={{6,4},{7,5},{0,2},{1,3},{14,12},{15,13},{8,10},{9,11},{22,20},{23,... | collective-permute-start | bytes 1572872 | tf_op jit(solution)/shard_map/ppermute | solution.py:350
  136.4 10.4 %collective-permute-done.33 = bf16[128,2048]{1,0:T(8,128)(2,1)S(1)} collective-permute-done((bf16[128,2048]{1,0:T(8,128)(2,1)S(1)}, bf16[128,2048]{1,0:T(8,128)(2,1)S(1)}, u32[]{:S(2)}, u32[]{:S(2)}) %collective-permute-start.33) | collective-permute-done | bytes 524320 | tf_op jit(solution)/shard_map/ppermute | solution.py:350
  148.3 8.5 %collective-permute-done.27 = bf16[128,2048]{1,0:T(8,128)(2,1)S(1)} collective-permute-done((bf16[128,2048]{1,0:T(8,128)(2,1)S(1)}, bf16[128,2048]{1,0:T(8,128)(2,1)S(1)}, u32[]{:S(2)}, u32[]{:S(2)}) %collective-permute-start.27) | collective-permute-done | bytes 524320 | tf_op jit(solution)/shard_map/ppermute | solution.py:27
  157.2 5.8 %collective-permute-done.36 = bf16[128,2048]{1,0:T(8,128)(2,1)S(1)} collective-permute-done((bf16[128,2048]{1,0:T(8,128)(2,1)S(1)}, bf16[128,2048]{1,0:T(8,128)(2,1)S(1)}, u32[]{:S(2)}, u32[]{:S(2)}) %collective-permute-start.36) | collective-permute-done | bytes 524320 | tf_op jit(solution)/shard_map/ppermute | solution.py:350
  (83 shorter events, 34.5 us)
Async XLA Ops:
  3.0 26.5 %collective-permute-start.1 = (bf16[1040,256]{1,0:T(8,128)(2,1)S(1)}, bf16[1040,256]{1,0:T(8,128)(2,1)S(1)}, u32[]{:S(2)}, u32[]{:S(2)}) collective-permute-start(bf16[1040,256]{1,0:T(8,128)(2,1)S(1)} %get-tuple-element.62.refs_0_), channel_id=1, source_target_pairs={{0,2},{1,3},{2,0},{3,1},{4,6},{5,7},{6,4},{7,5},{8,10},{9,11},{10,... | collective-permute-start | bytes 1597448 | tf_op jit(solution)/shard_map/ppermute | solution.py:27
  6.0 25.9 %collective-permute-start = (bf16[1040,256]{1,0:T(8,128)(2,1)S(1)}, bf16[1040,256]{1,0:T(8,128)(2,1)S(1)}, u32[]{:S(2)}, u32[]{:S(2)}) collective-permute-start(bf16[1040,256]{1,0:T(8,128)(2,1)S(1)} %get-tuple-element.62.refs_0_), channel_id=1, source_target_pairs={{0,4},{1,5},{2,6},{3,7},{4,0},{5,1},{6,2},{7,3},{8,12},{9,13},{10,... | collective-permute-start | bytes 1597448 | tf_op jit(solution)/shard_map/ppermute | solution.py:27
  8.6 10.7 %collective-permute-start.2 = (bf16[128,1280]{1,0:T(8,128)(2,1)S(1)}, bf16[128,1280]{1,0:T(8,128)(2,1)S(1)}, u32[]{:S(2)}, u32[]{:S(2)}) collective-permute-start(bf16[128,1280]{1,0:T(8,128)(2,1)S(1)} %get-tuple-element.56), channel_id=1, source_target_pairs={{0,8},{8,0},{16,24},{24,16},{1,9},{9,1},{17,25},{25,17},{2,10},{10... | collective-permute-start | bytes 983048 | tf_op jit(solution)/shard_map/ppermute | solution.py:27
  10.1 15.6 %collective-permute-start.3 = (bf16[128,1280]{1,0:T(8,128)(2,1)S(1)}, bf16[128,1280]{1,0:T(8,128)(2,1)S(1)}, u32[]{:S(2)}, u32[]{:S(2)}) collective-permute-start(bf16[128,1280]{1,0:T(8,128)(2,1)S(1)} %get-tuple-element.57), channel_id=1, source_target_pairs={{0,16},{8,24},{16,0},{24,8},{1,17},{9,25},{17,1},{25,9},{2,18},{10... | collective-permute-start | bytes 983048 | tf_op jit(solution)/shard_map/ppermute | solution.py:27
  11.6 14.1 %collective-permute-start.4 = (bf16[128,1280]{1,0:T(8,128)(2,1)S(1)}, bf16[128,1280]{1,0:T(8,128)(2,1)S(1)}, u32[]{:S(2)}, u32[]{:S(2)}) collective-permute-start(bf16[128,1280]{1,0:T(8,128)(2,1)S(1)} %get-tuple-element.58), channel_id=1, source_target_pairs={{0,24},{8,16},{16,8},{24,0},{1,25},{9,17},{17,9},{25,1},{2,26},{10... | collective-permute-start | bytes 983048 | tf_op jit(solution)/shard_map/ppermute | solution.py:27
  32.5 16.6 %collective-permute-start.6 = (bf16[1040,256]{1,0:T(8,128)(2,1)S(1)}, bf16[1040,256]{1,0:T(8,128)(2,1)S(1)}, u32[]{:S(2)}, u32[]{:S(2)}) collective-permute-start(bf16[1040,256]{1,0:T(8,128)(2,1)S(1)} %get-tuple-element.62.refs_0_), channel_id=1, source_target_pairs={{2,4},{3,5},{4,2},{5,3},{10,12},{11,13},{12,10},{13,11},{18,20},{1... | collective-permute-start | bytes 1597448 | tf_op jit(solution)/shard_map/ppermute | solution.py:350
  33.2 15.9 %collective-permute-start.5 = (bf16[1040,256]{1,0:T(8,128)(2,1)S(1)}, bf16[1040,256]{1,0:T(8,128)(2,1)S(1)}, u32[]{:S(2)}, u32[]{:S(2)}) collective-permute-start(bf16[1040,256]{1,0:T(8,128)(2,1)S(1)} %collective-permute-done.refs_0_), channel_id=1, source_target_pairs={{4,6},{5,7},{2,0},{3,1},{12,14},{13,15},{10,8},{11,9},{20,22},{21,... | collective-permute-start | bytes 1597448 | tf_op jit(solution)/shard_map/ppermute | solution.py:350
  37.3 11.8 %collective-permute-start.9 = (bf16[128,1024]{1,0:T(8,128)(2,1)S(1)}, bf16[128,1024]{1,0:T(8,128)(2,1)S(1)}, u32[]{:S(2)}, u32[]{:S(2)}) collective-permute-start(bf16[128,1024]{1,0:T(8,128)(2,1)S(1)} %get-tuple-element.66), channel_id=1, source_target_pairs={{0,8},{8,0},{16,24},{24,16},{1,9},{9,1},{17,25},{25,17},{2,10},{10... | collective-permute-start | bytes 786440 | tf_op jit(solution)/shard_map/ppermute | solution.py:27
  38.8 13.8 %collective-permute-start.10 = (bf16[128,1024]{1,0:T(8,128)(2,1)S(1)}, bf16[128,1024]{1,0:T(8,128)(2,1)S(1)}, u32[]{:S(2)}, u32[]{:S(2)}) collective-permute-start(bf16[128,1024]{1,0:T(8,128)(2,1)S(1)} %get-tuple-element.67), channel_id=1, source_target_pairs={{0,16},{8,24},{16,0},{24,8},{1,17},{9,25},{17,1},{25,9},{2,18},{10... | collective-permute-start | bytes 786440 | tf_op jit(solution)/shard_map/ppermute | solution.py:27
  41.0 11.6 %collective-permute-start.11 = (bf16[128,1024]{1,0:T(8,128)(2,1)S(1)}, bf16[128,1024]{1,0:T(8,128)(2,1)S(1)}, u32[]{:S(2)}, u32[]{:S(2)}) collective-permute-start(bf16[128,1024]{1,0:T(8,128)(2,1)S(1)} %get-tuple-element.68), channel_id=1, source_target_pairs={{0,24},{8,16},{16,8},{24,0},{1,25},{9,17},{17,9},{25,1},{2,26},{10... | collective-permute-start | bytes 786440 | tf_op jit(solution)/shard_map/ppermute | solution.py:27
  54.9 8.0 %collective-permute-start.16 = (bf16[128,512]{1,0:T(8,128)(2,1)S(1)}, bf16[128,512]{1,0:T(8,128)(2,1)S(1)}, u32[]{:S(2)}, u32[]{:S(2)}) collective-permute-start(bf16[128,512]{1,0:T(8,128)(2,1)S(1)} %get-tuple-element.80), channel_id=1, source_target_pairs={{0,24},{8,16},{16,8},{24,0},{1,25},{9,17},{17,9},{25,1},{2,26},{10... | collective-permute-start | bytes 393224 | tf_op jit(solution)/shard_map/ppermute | solution.py:27
  59.2 8.9 %collective-permute-start.19 = (bf16[128,512]{1,0:T(8,128)(2,1)S(1)}, bf16[128,512]{1,0:T(8,128)(2,1)S(1)}, u32[]{:S(2)}, u32[]{:S(2)}) collective-permute-start(bf16[128,512]{1,0:T(8,128)(2,1)S(1)} %get-tuple-element.84), channel_id=1, source_target_pairs={{0,24},{8,16},{16,8},{24,0},{1,25},{9,17},{17,9},{25,1},{2,26},{10... | collective-permute-start | bytes 393224 | tf_op jit(solution)/shard_map/ppermute | solution.py:27
  69.3 27.6 %collective-permute-start.22 = (bf16[128,2048]{1,0:T(8,128)(2,1)S(1)}, bf16[128,2048]{1,0:T(8,128)(2,1)S(1)}, u32[]{:S(2)}, u32[]{:S(2)}) collective-permute-start(bf16[128,2048]{1,0:T(8,128)(2,1)S(1)} %get-tuple-element.101.refs_0_), channel_id=1, source_target_pairs={{0,4},{1,5},{2,6},{3,7},{4,0},{5,1},{6,2},{7,3},{8,12},{9,13},{10,... | collective-permute-start | bytes 1572872 | tf_op jit(solution)/shard_map/ppermute | solution.py:27
  73.0 24.1 %collective-permute-start.23 = (bf16[128,2048]{1,0:T(8,128)(2,1)S(1)}, bf16[128,2048]{1,0:T(8,128)(2,1)S(1)}, u32[]{:S(2)}, u32[]{:S(2)}) collective-permute-start(bf16[128,2048]{1,0:T(8,128)(2,1)S(1)} %get-tuple-element.101.refs_0_), channel_id=1, source_target_pairs={{0,2},{1,3},{2,0},{3,1},{4,6},{5,7},{6,4},{7,5},{8,10},{9,11},{10,... | collective-permute-start | bytes 1572872 | tf_op jit(solution)/shard_map/ppermute | solution.py:27
  97.7 15.7 %collective-permute-start.29 = (bf16[128,2048]{1,0:T(8,128)(2,1)S(1)}, bf16[128,2048]{1,0:T(8,128)(2,1)S(1)}, u32[]{:S(2)}, u32[]{:S(2)}) collective-permute-start(bf16[128,2048]{1,0:T(8,128)(2,1)S(1)} %collective-permute-done.22.refs_2_), channel_id=1, source_target_pairs={{4,6},{5,7},{2,0},{3,1},{12,14},{13,15},{10,8},{11,9},{20,22},{21,... | collective-permute-start | bytes 1572872 | tf_op jit(solution)/shard_map/ppermute | solution.py:350
  98.9 14.4 %collective-permute-start.30 = (bf16[128,2048]{1,0:T(8,128)(2,1)S(1)}, bf16[128,2048]{1,0:T(8,128)(2,1)S(1)}, u32[]{:S(2)}, u32[]{:S(2)}) collective-permute-start(bf16[128,2048]{1,0:T(8,128)(2,1)S(1)} %get-tuple-element.101.refs_0_), channel_id=1, source_target_pairs={{2,4},{3,5},{4,2},{5,3},{10,12},{11,13},{12,10},{13,11},{18,20},{1... | collective-permute-start | bytes 1572872 | tf_op jit(solution)/shard_map/ppermute | solution.py:350
  114.3 16.3 %collective-permute-start.34 = (bf16[128,2048]{1,0:T(8,128)(2,1)S(1)}, bf16[128,2048]{1,0:T(8,128)(2,1)S(1)}, u32[]{:S(2)}, u32[]{:S(2)}) collective-permute-start(bf16[128,2048]{1,0:T(8,128)(2,1)S(1)} %add_convert_fusion.4), channel_id=1, source_target_pairs={{0,2},{1,3},{2,0},{3,1},{4,6},{5,7},{6,4},{7,5},{8,10},{9,11},{10,... | collective-permute-start | bytes 1572872 | tf_op jit(solution)/shard_map/ppermute | solution.py:27
  122.5 8.1 %collective-permute-start.32 = (bf16[128,2048]{1,0:T(8,128)(2,1)S(1)}, bf16[128,2048]{1,0:T(8,128)(2,1)S(1)}, u32[]{:S(2)}, u32[]{:S(2)}) collective-permute-start(bf16[128,2048]{1,0:T(8,128)(2,1)S(1)} %get-tuple-element.103), channel_id=1, source_target_pairs={{0,1},{1,0},{2,3},{3,2},{4,5},{5,4},{6,7},{7,6},{8,9},{9,8},{10,11... | collective-permute-start | bytes 1572872 | tf_op jit(solution)/shard_map/ppermute | solution.py:27
  122.8 12.6 %collective-permute-start.26 = (bf16[128,2048]{1,0:T(8,128)(2,1)S(1)}, bf16[128,2048]{1,0:T(8,128)(2,1)S(1)}, u32[]{:S(2)}, u32[]{:S(2)}) collective-permute-start(bf16[128,2048]{1,0:T(8,128)(2,1)S(1)} %get-tuple-element.97), channel_id=1, source_target_pairs={{0,1},{1,0},{2,3},{3,2},{4,5},{5,4},{6,7},{7,6},{8,9},{9,8},{10,11... | collective-permute-start | bytes 1572872 | tf_op jit(solution)/shard_map/ppermute | solution.py:27
  130.9 16.0 %collective-permute-start.33 = (bf16[128,2048]{1,0:T(8,128)(2,1)S(1)}, bf16[128,2048]{1,0:T(8,128)(2,1)S(1)}, u32[]{:S(2)}, u32[]{:S(2)}) collective-permute-start(bf16[128,2048]{1,0:T(8,128)(2,1)S(1)} %get-tuple-element.107), channel_id=1, source_target_pairs={{6,4},{7,5},{0,2},{1,3},{14,12},{15,13},{8,10},{9,11},{22,20},{23,... | collective-permute-start | bytes 1572872 | tf_op jit(solution)/shard_map/ppermute | solution.py:350
  134.6 13.7 %collective-permute-start.21 = (bf16[128,2048]{1,0:T(8,128)(2,1)S(1)}, bf16[128,2048]{1,0:T(8,128)(2,1)S(1)}, u32[]{:S(2)}, u32[]{:S(2)}) collective-permute-start(bf16[128,2048]{1,0:T(8,128)(2,1)S(1)} %get-tuple-element.89), channel_id=1, source_target_pairs={{0,1},{1,0},{2,3},{3,2},{4,5},{5,4},{6,7},{7,6},{8,9},{9,8},{10,11... | collective-permute-start | bytes 1572872 | tf_op jit(solution)/shard_map/ppermute | solution.py:27
  134.7 12.4 %collective-permute-start.35 = (bf16[128,2048]{1,0:T(8,128)(2,1)S(1)}, bf16[128,2048]{1,0:T(8,128)(2,1)S(1)}, u32[]{:S(2)}, u32[]{:S(2)}) collective-permute-start(bf16[128,2048]{1,0:T(8,128)(2,1)S(1)} %get-tuple-element.106), channel_id=1, source_target_pairs={{2,4},{3,5},{4,2},{5,3},{10,12},{11,13},{12,10},{13,11},{18,20},{1... | collective-permute-start | bytes 1572872 | tf_op jit(solution)/shard_map/ppermute | solution.py:350
  135.5 21.3 %collective-permute-start.27 = (bf16[128,2048]{1,0:T(8,128)(2,1)S(1)}, bf16[128,2048]{1,0:T(8,128)(2,1)S(1)}, u32[]{:S(2)}, u32[]{:S(2)}) collective-permute-start(bf16[128,2048]{1,0:T(8,128)(2,1)S(1)} %add_convert_fusion.5), channel_id=1, source_target_pairs={{0,2},{1,3},{2,0},{3,1},{4,6},{5,7},{6,4},{7,5},{8,10},{9,11},{10,... | collective-permute-start | bytes 1572872 | tf_op jit(solution)/shard_map/ppermute | solution.py:27
  147.0 16.0 %collective-permute-start.36 = (bf16[128,2048]{1,0:T(8,128)(2,1)S(1)}, bf16[128,2048]{1,0:T(8,128)(2,1)S(1)}, u32[]{:S(2)}, u32[]{:S(2)}) collective-permute-start(bf16[128,2048]{1,0:T(8,128)(2,1)S(1)} %add_convert_fusion.2), channel_id=1, source_target_pairs={{4,0},{5,1},{2,6},{3,7},{12,8},{13,9},{10,14},{11,15},{20,16},{21,... | collective-permute-start | bytes 1572872 | tf_op jit(solution)/shard_map/ppermute | solution.py:350
  (16 other events, 186.8 us)
